TPU v7x, 256 devices: a whole 4x4x8 slice. The times are simulated.
256 devices in a mesh: row: 16 (over z, core), col: 16 (over y, x).
Axes of the slice: x: 4, y: 4, z: 8, core: 2. Of those that a mesh axis runs over, the one named last changes fastest.
Arguments:
- teacher_image: bfloat16 [16384, 1024], P(('row', 'col')), may hold values from -1 to 1
- teacher_text: bfloat16 [16384, 1024], P(('row', 'col')), may hold values from -1 to 1
- student_image: bfloat16 [16384, 1024], P(('row', 'col')), may hold values from -1 to 1
- student_text: bfloat16 [16384, 1024], P(('row', 'col')), may hold values from -1 to 1
Outputs:
- image_grad: bfloat16 [16384, 1024], P(('row', 'col'))
- text_grad: bfloat16 [16384, 1024], P(('row', 'col'))
- loss: float32 [], replicated
All inputs are finite; a program needn't handle non-finite values.
Results may differ from a plain program's by a relative error of at most 0.0048.
Values may be sent and summed in bfloat16 or wider, within the bound.
No kernel may reach another device: no remote copies, remote signals or barrier semaphores. Data moves between devices by JAX's collectives and lax.ppermute only.
A program may use at most 64 MiB of HBM per device.

v0:
```python
import jax
import jax.numpy as jnp
from jax import lax
from jax.sharding import PartitionSpec as P


def merged(value, axis, combine):
    everything = jax.tree.map(lambda part: lax.all_gather(part, axis), value)
    leading = jax.tree.map(lambda part: part[0], everything)

    def step(k, so_far):
        return combine(so_far, jax.tree.map(lambda part: part[k], everything))

    return lax.fori_loop(1, lax.axis_size(axis), step, leading)


def similarity(left, right):
    return 100.0 * lax.dot_general(
        left, right, (((1,), (1,)), ((), ())), preferred_element_type=jnp.float32
    )


def softmax_parts(values, axis):
    top = jnp.max(values, axis=axis)
    total = jnp.sum(jnp.exp(values - jnp.expand_dims(top, axis)), axis=axis)
    return (top, total)


def join_parts(first, second):
    t_top = jnp.maximum(first[0], second[0])
    scale_a = jnp.exp(first[0] - t_top)
    scale_b = jnp.exp(second[0] - t_top)
    s_top = jnp.maximum(first[2], second[2])
    s_total = first[3] * jnp.exp(first[2] - s_top) + second[3] * jnp.exp(second[2] - s_top)
    joined = (t_top, first[1] * scale_a + second[1] * scale_b, s_top, s_total)
    if len(first) == 5:
        joined = joined + (first[4] * scale_a + second[4] * scale_b,)
    return joined


def per_device(teacher_image, teacher_text, student_image, student_text):
    rows_dev = teacher_image.shape[0]
    total_pairs = rows_dev * lax.axis_size("row") * lax.axis_size("col")
    t_rows, s_rows = (
        lax.all_gather(teacher_image, "col", axis=0, tiled=True),
        lax.all_gather(student_image, "col", axis=0, tiled=True),
    )
    t_cols, s_cols = (
        lax.all_gather(teacher_text, "row", axis=0, tiled=True),
        lax.all_gather(student_text, "row", axis=0, tiled=True),
    )
    teach = similarity(t_rows, t_cols)
    learn = similarity(s_rows, s_cols)
    gap = teach - learn
    rt_top, rt_total = softmax_parts(teach, 1)
    rs_top, rs_total = softmax_parts(learn, 1)
    ct_top, ct_total = softmax_parts(teach, 0)
    cs_top, cs_total = softmax_parts(learn, 0)
    row_local = (rt_top, rt_total, rs_top, rs_total)
    col_local = (ct_top, ct_total, cs_top, cs_total)
    row_stats = merged(row_local, "col", join_parts)
    col_stats = merged(col_local, "row", join_parts)
    row_t = row_stats[0] + jnp.log(row_stats[1])
    row_s = row_stats[2] + jnp.log(row_stats[3])
    col_t = col_stats[0] + jnp.log(col_stats[1])
    col_s = col_stats[2] + jnp.log(col_stats[3])
    row_start = lax.axis_index("col") * rows_dev
    col_start = lax.axis_index("row") * rows_dev
    p_row = jnp.exp(teach - row_t[:, None])
    p_col = jnp.exp(teach - col_t[None, :])
    own_rows = lax.dynamic_slice_in_dim(row_s - row_t, row_start, rows_dev)
    own_cols = lax.dynamic_slice_in_dim(col_s - col_t, col_start, rows_dev)
    local_part = jnp.sum((p_row + p_col) * gap) + jnp.sum(own_rows) + jnp.sum(own_cols)
    loss = lax.psum(local_part, ("row", "col")) * (0.5 / total_pairs)
    q_row = jnp.exp(learn - row_s[:, None])
    q_col = jnp.exp(learn - col_s[None, :])
    coupling = (0.5 * (q_row - p_row + q_col - p_col)).astype(jnp.bfloat16)
    image_term_all = 100.0 * jnp.dot(coupling, s_cols, preferred_element_type=jnp.float32)
    image_grad = lax.psum_scatter(image_term_all, "col", scatter_dimension=0, tiled=True)
    text_grad = lax.psum_scatter(
        100.0
        * lax.dot_general(
            coupling, s_rows, (((0,), (0,)), ((), ())), preferred_element_type=jnp.float32
        ),
        "row",
        scatter_dimension=0,
        tiled=True,
    )
    return (image_grad.astype(jnp.bfloat16), text_grad.astype(jnp.bfloat16), loss)


def solution(mesh):
    placed = (
        P(("row", "col"), None),
        P(("row", "col"), None),
        P(("row", "col"), None),
        P(("row", "col"), None),
    )
    return jax.shard_map(
        per_device,
        mesh=mesh,
        in_specs=placed,
        out_specs=(P(("row", "col"), None), P(("row", "col"), None), P()),
        check_vma=False,
    )
```

profile of v0, /device:TPU:39, one launch (start us, length us, event | category | flops | bytes accessed | tf_op | source)
XLA Modules:
  0.0 446.0 jit_solution(11719640046574814192)
XLA Ops:
  7.2 0.0 all-gather.17.cloned.1.call-start
  7.2 0.7 all-gather.17.cloned.1.call-update
  7.9 0.0 all-gather.19.cloned.1.call-start
  7.9 0.7 all-gather.19.cloned.1.call-update
  8.6 0.0 all-gather.13.cloned.1.call-start
  8.7 0.7 all-gather.13.cloned.1.call-update
  9.4 0.0 all-gather.15.cloned.1.call-start
  9.4 0.5 all-gather.15.cloned.1.call-update
  10.0 0.0 reduce-scatter.3.cloned.1.call-start
  10.0 51.8 %all-gather.17.cloned.1.call-done = bf16[1024,1024]{1,0:T(8,128)(2,1)} async-done(((bf16[64,1024]{1,0:T(8,128)(2,1)}), bf16[1024,1024]{1,0:T(8,128)(2,1)}) %all-gather.17.cloned.1.call-update) | async-done | bytes 2097168 | tf_op jit(solution)/shard_map/all_gather | solution.py:45
  61.8 41.8 %all-gather.19.cloned.1.call-done = bf16[1024,1024]{1,0:T(8,128)(2,1)} async-done(((bf16[64,1024]{1,0:T(8,128)(2,1)}), bf16[1024,1024]{1,0:T(8,128)(2,1)}) %all-gather.19.cloned.1.call-update) | async-done | bytes 2097168 | tf_op jit(solution)/shard_map/all_gather | solution.py:49
  103.6 4.7 %multiply_reduce_fusion.2 = (f32[1024]{0:T(1024)S(1)}, f32[1024,1024]{1,0:T(8,128)S(1)}) fusion(bf16[1024,1024]{1,0:T(8,128)(2,1)} %all-gather.17.cloned.1.call-done, bf16[1024,1024]{1,0:T(8,128)(2,1)} %all-gather.19.cloned.1.call-done), kind=kOutput, calls=%fused_computation.21 | convolution fusion | flops 2149579776 | bytes 8392704 | tf_op jit(solution)/shard_map/dot_general | solution.py:18
  108.3 0.0 copy-start
  108.3 1.9 copy-done
  110.2 1.2 exponential_reduce_fusion.3
  111.4 15.6 %all-gather.4 = f32[16384]{0:T(1024)S(1)} all-gather(f32[1024]{0:T(1024)S(1)} %get-tuple-element.460), channel_id=6, replica_groups=mesh['row'=16,'col'=16] {'row'}, dimensions={0}, use_global_device_ids=true | all-gather | bytes 69632 | tf_op jit(solution)/shard_map/all_gather | solution.py:8
  127.0 2.9 exponential_reduce_fusion.1
  130.0 15.9 %all-gather.5 = f32[16384]{0:T(1024)S(1)} all-gather(f32[1024]{0:T(1024)S(1)} %exponential_reduce_fusion.1), channel_id=7, replica_groups=mesh['row'=16,'col'=16] {'row'}, dimensions={0}, use_global_device_ids=true | all-gather | bytes 69632 | tf_op jit(solution)/shard_map/all_gather | solution.py:8
  145.9 18.3 %all-gather.1 = f32[16384]{0:T(1024)S(1)} all-gather(f32[1024]{0:T(1024)S(1)} %get-tuple-element.459), channel_id=3, replica_groups=mesh['row'=16,'col'=16] {'col'}, dimensions={0}, use_global_device_ids=true | all-gather | bytes 69632 | tf_op jit(solution)/shard_map/all_gather | solution.py:8
  164.2 16.3 %all-gather = f32[16384]{0:T(1024)S(1)} all-gather(f32[1024]{0:T(1024)S(1)} %get-tuple-element.517), channel_id=2, replica_groups=mesh['row'=16,'col'=16] {'col'}, dimensions={0}, use_global_device_ids=true | all-gather | bytes 69632 | tf_op jit(solution)/shard_map/all_gather | solution.py:8
  180.5 0.0 all-gather.13.cloned.1.call-done
  180.6 14.7 %all-gather.15.cloned.1.call-done = bf16[1024,1024]{1,0:T(8,128)(2,1)} async-done(((bf16[64,1024]{1,0:T(8,128)(2,1)}), bf16[1024,1024]{1,0:T(8,128)(2,1)}) %all-gather.15.cloned.1.call-update) | async-done | bytes 2097168 | tf_op jit(solution)/shard_map/all_gather | solution.py:50
  195.2 4.7 %multiply_reduce_fusion.4 = (f32[1024]{0:T(1024)S(1)}, f32[1024,1024]{1,0:T(8,128)S(1)}) fusion(bf16[1024,1024]{1,0:T(8,128)(2,1)} %all-gather.13.cloned.1.call-done, bf16[1024,1024]{1,0:T(8,128)(2,1)} %all-gather.15.cloned.1.call-done), kind=kOutput, calls=%fused_computation.23 | convolution fusion | flops 2149579776 | bytes 8392704 | tf_op jit(solution)/shard_map/dot_general | solution.py:18
  200.0 0.0 slice-start
  200.0 0.0 slice-start.3
  200.0 0.0 slice-start.1
  200.0 0.0 slice-start.2
  200.0 1.2 exponential_reduce_fusion.2
  201.2 0.7 exponential_reduce_fusion
  201.9 15.5 %all-gather.6 = f32[16384]{0:T(1024)S(1)} all-gather(f32[1024]{0:T(1024)S(1)} %get-tuple-element.458), channel_id=8, replica_groups=mesh['row'=16,'col'=16] {'row'}, dimensions={0}, use_global_device_ids=true | all-gather | bytes 69632 | tf_op jit(solution)/shard_map/all_gather | solution.py:8
  217.4 16.0 %all-gather.7 = f32[16384]{0:T(1024)S(1)} all-gather(f32[1024]{0:T(1024)S(1)} %exponential_reduce_fusion), channel_id=9, replica_groups=mesh['row'=16,'col'=16] {'row'}, dimensions={0}, use_global_device_ids=true | all-gather | bytes 69632 | tf_op jit(solution)/shard_map/all_gather | solution.py:8
  233.5 17.8 %all-gather.3 = f32[16384]{0:T(1024)S(1)} all-gather(f32[1024]{0:T(1024)S(1)} %get-tuple-element.457), channel_id=5, replica_groups=mesh['row'=16,'col'=16] {'col'}, dimensions={0}, use_global_device_ids=true | all-gather | bytes 69632 | tf_op jit(solution)/shard_map/all_gather | solution.py:8
  251.3 16.4 %all-gather.2 = f32[16384]{0:T(1024)S(1)} all-gather(f32[1024]{0:T(1024)S(1)} %get-tuple-element.519), channel_id=4, replica_groups=mesh['row'=16,'col'=16] {'col'}, dimensions={0}, use_global_device_ids=true | all-gather | bytes 69632 | tf_op jit(solution)/shard_map/all_gather | solution.py:8
  267.7 1.9 while.43
  269.7 1.9 while.42
  271.6 8.0 %multiply_reduce_fusion = (f32[]{:T(128)}, bf16[1024,1024]{1,0:T(8,128)(2,1)S(1)}) fusion(f32[1024,1024]{1,0:T(8,128)} %copy-done, f32[1024,1024]{1,0:T(8,128)} %copy-done.1, f32[1024]{0:T(1024)S(1)} %get-tuple-element.507, f32[1024]{0:T(1024)S(1)} %get-tuple-element.522, f32[1024]{0:T(1024)S(1)} %get-tuple-element.506, f32[1024]{0:T(1024)S(1)} %get-tuple-element.523), kind=kLoop, calls=%fused_computation.12 | loop fusion | flops 15728639 | bytes 10502148 | tf_op jit(solution)/shard_map/reduce_sum | solution.py:73
  279.6 4.3 convolution_multiply_fusion.1
  283.9 0.0 reduce-scatter.3.cloned.1.call-update
  283.9 0.0 reduce-scatter.5.cloned.1.call-start
  284.0 5.9 %convolution_multiply_fusion = f32[1024,1024]{1,0:T(8,128)} fusion(bf16[1024,1024]{1,0:T(8,128)(2,1)S(1)} %get-tuple-element.516, bf16[1024,1024]{1,0:T(8,128)(2,1)} %all-gather.13.cloned.1.call-done), kind=kOutput, calls=%fused_computation.24 | convolution fusion | flops 2148532224 | bytes 8388608 | tf_op jit(solution)/shard_map/dot_general | solution.py:82
  289.9 0.0 reduce-scatter.5.cloned.1.call-update
  289.9 0.7 dynamic-slice_reduce_fusion.1
  291.9 0.7 dynamic-slice_reduce_fusion
  293.2 84.3 %psum.7 = f32[]{:T(128)} all-reduce(f32[]{:T(128)S(6)} %add.157), channel_id=1, replica_groups=mesh['row'=16,'col'=16] {'row','col'}, use_global_device_ids=true, to_apply=%region_17.0 | all-reduce | flops 1 | bytes 8 | tf_op jit(solution)/shard_map/psum | solution.py:74
  378.2 0.0 reduce-scatter.3.cloned.1.call-done
  378.3 1.6 convert_element_type.10
  379.9 56.5 %reduce-scatter.5.cloned.1.call-done = f32[64,1024]{1,0:T(8,128)} async-done(((f32[1024,1024]{1,0:T(8,128)}), f32[64,1024]{1,0:T(8,128)}) %reduce-scatter.5.cloned.1.call-update) | async-done | bytes 262160 | tf_op jit(solution)/shard_map/reduce_scatter | solution.py:80
  436.4 1.6 convert_element_type.11
  (179 shorter events, 2.2 us)
Async XLA Ops:
  7.2 54.6 %all-gather.17.cloned.1.call-start = ((), (), s32[]{:S(2)}) async-start(), calls=%async_computation.4 | async-start | bytes 2228224 | tf_op jit(solution)/shard_map/all_gather | solution.py:45
  7.9 95.7 %all-gather.19.cloned.1.call-start = ((), (), s32[]{:S(2)}) async-start(), calls=%async_computation.5 | async-start | bytes 2228224 | tf_op jit(solution)/shard_map/all_gather | solution.py:49
  8.6 171.9 %all-gather.13.cloned.1.call-start = ((), (), s32[]{:S(2)}) async-start(), calls=%async_computation.2 | async-start | bytes 2228224 | tf_op jit(solution)/shard_map/all_gather | solution.py:46
  9.4 185.9 %all-gather.15.cloned.1.call-start = ((), (), s32[]{:S(2)}) async-start(), calls=%async_computation.3 | async-start | bytes 2228224 | tf_op jit(solution)/shard_map/all_gather | solution.py:50
  10.0 368.3 %reduce-scatter.3.cloned.1.call-start = ((), (), s32[]{:S(2)}) async-start(), calls=%async_computation.6 | async-start | bytes 4456448 | tf_op jit(solution)/shard_map/reduce_scatter | solution.py:79
  108.3 1.9 copy-start
  127.0 72.9 %copy-start.5 = (f32[16384]{0:T(1024)}, f32[16384]{0:T(1024)S(1)}, u32[]{:S(2)}) copy-start(f32[16384]{0:T(1024)S(1)} %all-gather.4) | copy-start | bytes 196612
  145.9 54.1 %copy-start.2 = (f32[16384]{0:T(1024)}, f32[16384]{0:T(1024)S(1)}, u32[]{:S(2)}) copy-start(f32[16384]{0:T(1024)S(1)} %all-gather.5) | copy-start | bytes 196612
  164.2 35.7 %copy-start.3 = (f32[16384]{0:T(1024)}, f32[16384]{0:T(1024)S(1)}, u32[]{:S(2)}) copy-start(f32[16384]{0:T(1024)S(1)} %all-gather.1) | copy-start | bytes 196612
  180.5 19.4 %copy-start.4 = (f32[16384]{0:T(1024)}, f32[16384]{0:T(1024)S(1)}, u32[]{:S(2)}) copy-start(f32[16384]{0:T(1024)S(1)} %all-gather) | copy-start | bytes 196612
  199.9 2.0 copy-start.1
  200.0 67.8 %slice-start = ((f32[16384]{0:T(1024)}), f32[1024]{0:T(1024)S(1)}, s32[]{:S(2)}) async-start(f32[16384]{0:T(1024)} %copy-done.2), calls=%async_computation.8 | async-start | bytes 8192 | tf_op jit(solution)/shard_map/slice | solution.py:9
  200.0 67.8 %slice-start.3 = ((f32[16384]{0:T(1024)}), f32[1024]{0:T(1024)S(1)}, s32[]{:S(2)}) async-start(f32[16384]{0:T(1024)} %copy-done.5), calls=%async_computation.11 | async-start | bytes 8192 | tf_op jit(solution)/shard_map/slice | solution.py:9
  200.0 69.7 %slice-start.1 = ((f32[16384]{0:T(1024)}), f32[1024]{0:T(1024)S(1)}, s32[]{:S(2)}) async-start(f32[16384]{0:T(1024)} %copy-done.3), calls=%async_computation.9 | async-start | bytes 8192 | tf_op jit(solution)/shard_map/slice | solution.py:9
  200.0 69.7 %slice-start.2 = ((f32[16384]{0:T(1024)}), f32[1024]{0:T(1024)S(1)}, s32[]{:S(2)}) async-start(f32[16384]{0:T(1024)} %copy-done.4), calls=%async_computation.10 | async-start | bytes 8192 | tf_op jit(solution)/shard_map/slice | solution.py:9
  271.6 8.0 %copy-start.6 = (bf16[1024,1024]{1,0:T(8,128)(2,1)S(1)}, bf16[1024,1024]{1,0:T(8,128)(2,1)}, u32[]{:S(2)}) copy-start(bf16[1024,1024]{1,0:T(8,128)(2,1)} %all-gather.15.cloned.1.call-done) | copy-start | bytes 6291460
  283.9 152.4 %reduce-scatter.5.cloned.1.call-start = ((), (), s32[]{:S(2)}) async-start(), calls=%async_computation.7 | async-start | bytes 4456448 | tf_op jit(solution)/shard_map/reduce_scatter | solution.py:80
Sparse Core Ops, SparseCore 0:
  10.4 51.3 all-gather.16
  63.6 39.9 all-gather.18
  106.1 47.4 all-gather.12
  155.2 39.9 all-gather.14
  284.0 89.5 reduce-scatter.2
  376.2 60.1 reduce-scatter.4
where the time goes:
time: 451 us; the launch traced here: 446 us
  blocking collectives  216 us (48%)
  waiting for transfers between devices  167 us (37%)
  matrix products  19.6 us (4%)
  other arithmetic  19.1 us (4%)
  between operations  18.1 us (4%)
    all_gather x8, blocking collectives, merged(): everything = jax.tree.map(lambda part: lax.all_gather(part, axis), value)  132 us
    psum x1, blocking collectives, per_device(): loss = lax.psum(local_part, ('row', 'col')) * (0.5 / total_pairs)  84.3 us
    reduce_scatter x1, waiting for transfers between devices, per_device(): lax.psum_scatter(100.0 * lax.dot_general(coupling, s_rows, (((0,), (0,)),...  56.5 us
    all_gather x1, waiting for transfers between devices, per_device(): lax.all_gather(teacher_image, 'col', axis=0, tiled=True)  51.8 us
    all_gather x1, waiting for transfers between devices, per_device(): lax.all_gather(teacher_text, 'row', axis=0, tiled=True)  41.8 us
    all_gather x1, waiting for transfers between devices, per_device(): lax.all_gather(student_text, 'row', axis=0, tiled=True)  14.7 us
    dot_general x2, matrix products, similarity(): lax.dot_general(left, right, (((1,), (1,)), ((), ())), preferred_element_...  9.34 us
  transfers between devices with their start and end apart: 6, of which 4 were waited for; matrix products, arithmetic and copies ran while one was open for 4% of the time, Pallas kernels for 0%

commit v1 on v0

v1 whole, which is shorter than its diff:
```python
import jax
import jax.numpy as jnp
from jax import lax
from jax.experimental import pallas as pl
from jax.experimental.pallas import tpu as pltpu
from jax.sharding import PartitionSpec as P

NX, NY, NZ, NC = 4, 4, 8, 2
BF = jnp.bfloat16
F32 = jnp.float32
GROUP = 8
LANES = 128
VMEM_BYTES = 16 << 20
PASS_1_BYTES = 40 << 20
PASS_2_BYTES = 52 << 20


def place(z, c, y, x):
    return ((z % NZ * NC + c) * NY + y % NY) * NX + x % NX


def send(v, target):
    pairs = [
        (place(z, c, y, x), place(*target(z, c, y, x)))
        for z in range(NZ)
        for c in range(NC)
        for y in range(NY)
        for x in range(NX)
    ]
    return lax.ppermute(v, ("row", "col"), pairs)


def swap(v, z_bits=0, c_bits=0, y_bits=0, x_bits=0):
    return send(v, lambda z, c, y, x: (z ^ z_bits, c ^ c_bits, y ^ y_bits, x ^ x_bits))


def move_first(v, d):
    return send(v, lambda z, c, y, x: (z, c, y + d * c, x + d * (1 - c)))


def move_second(v, d):
    return send(v, lambda z, c, y, x: (z, c, y + d * (1 - c), x + d * c))


def move_z(v, d):
    return send(v, lambda z, c, y, x: (z + d * (1 - 2 * c), c, y, x))


def position():
    row, col = lax.axis_index("row"), lax.axis_index("col")
    return lax.div(row, NC), lax.rem(row, NC), lax.div(col, NX), lax.rem(col, NX)


def gather_rows(v):
    from_m = move_first(v, 1)
    from_p = move_first(v, -1)
    from_2 = move_first(v, 2)
    line = jnp.stack([v, from_p, from_2, from_m], axis=1)
    up = move_second(line, 1)
    down = move_second(line, -1)
    far_a = move_second(up[:, :2], 1)
    far_b = move_second(down[:, 2:], -1)
    got_0 = swap(line[1], c_bits=1)
    got_1 = swap(jnp.stack([down[1], up[1]]), c_bits=1)
    got_2 = swap(jnp.concatenate([far_a[1], far_b[1]]), c_bits=1)
    return line, up, down, far_a, far_b, got_0, got_1, got_2


def gather_cols(v):
    out = [v]
    for _ in range(3):
        out.append(move_z(out[-1], 1))
    far = move_z(out[3][0], 1)
    back = [swap(b, c_bits=1) for b in out[1:]]
    return out + [far] + back + [swap(far, c_bits=1)]


def pass_1_kernel(
    line, up, down, far_a, far_b, got_0, got_1, got_2,
    t0, t1, t2, t3, far, b1, b2, b3, far_sib,
    both_out, student, row_st, col_st,
    teach, learn, rows, cols, tops, wide, sums, sem,
):
    z, c, y, x = position()
    n, d = rows.shape[2:]
    size = teach.shape[0]
    tiles = size // LANES

    def row_place(second, first):
        dy = second * (1 - c) + first * c
        dx = first * (1 - c) + second * c
        return lax.rem(y + dy, NY) * NX + lax.rem(x + dx, NX)

    def col_place(steps, core):
        return lax.rem(z + NZ + steps, NZ) * NC + core

    pieces = []
    for k in range(4):
        for f in range(4):
            if k == 2:
                src = (far_a, (0, f)) if f < 2 else (far_b, (0, f - 2))
            else:
                src = ({0: line, 1: down, 3: up}[k], (0, f))
            pieces.append((src, (rows, c, row_place(k, f))))
            src = {0: (got_0, k), 1: (got_1, (0, k)), 2: (got_2, k), 3: (got_1, (1, k))}[f]
            pieces.append((src, (rows, 1 - c, row_place(k, f))))
    way = 2 * c - 1
    for kind in range(2):
        for j, ref in enumerate((t0, t1, t2, t3)):
            for dc in range(2):
                core = c if dc == 0 else 1 - c
                pieces.append(((ref, (dc, kind)), (cols, kind, col_place(way * j, core))))
        for j, ref in enumerate((b1, b2, b3)):
            for dc in range(2):
                core = 1 - c if dc == 0 else c
                pieces.append(((ref, (dc, kind)), (cols, kind, col_place(-way * (j + 1), core))))
        pieces.append(((far, kind), (cols, kind, col_place(4, c))))
        pieces.append(((far_sib, kind), (cols, kind, col_place(4, 1 - c))))
    for (src, i), (dst, j, k) in pieces:
        dst[j, k] = src[i]
    leave = [
        pltpu.make_async_copy(rows.at[1], student.at[0], sem.at[0]),
        pltpu.make_async_copy(cols.at[1], student.at[1], sem.at[1]),
    ]
    for copy in leave:
        copy.start()

    for kind, buf in ((0, teach), (1, learn)):
        buf[...] = 100.0 * lax.dot_general(
            rows[kind].reshape(size, d),
            cols[kind].reshape(size, d),
            (((1,), (1,)), ((), ())),
            preferred_element_type=F32,
        )
        copy = pltpu.make_async_copy(buf, both_out.at[kind], sem.at[2 + kind])
        copy.start()
        leave.append(copy)

    def tile(ref, part, q):
        return ref[part, q * LANES : (q + 1) * LANES]

    def top_step(i, carry):
        part = pl.ds(pl.multiple_of(i * GROUP, GROUP), GROUP)
        out = []
        for k, ref in ((0, teach), (1, learn)):
            v = [tile(ref, part, q) for q in range(tiles)]
            out.append([jnp.maximum(a, b) for a, b in zip(carry[k], v)])
            while len(v) > 1:
                v = [jnp.maximum(a, b) for a, b in zip(v[::2], v[1::2])]
            tops[k, part, :] = v[0]
        return out

    low = jnp.full((GROUP, LANES), -jnp.inf, F32)
    col_tops = lax.fori_loop(0, size // GROUP, top_step, [[low] * tiles] * 2, unroll=2)
    col_tops = [[jnp.max(v, axis=0, keepdims=True) for v in tops_k] for tops_k in col_tops]
    row_tops = []
    for k in range(2):
        top = jnp.max(tops[k].T, axis=0, keepdims=True)
        row_tops.append(top)
        wide[k] = jnp.broadcast_to(top, (LANES, size)).T

    for h in range(2):
        span = range(h * tiles // 2, (h + 1) * tiles // 2)
        t_tops = [jnp.broadcast_to(col_tops[0][q], (GROUP, LANES)) for q in span]
        s_tops = [jnp.broadcast_to(col_tops[1][q], (GROUP, LANES)) for q in span]

        def sum_step(i, carry):
            part = pl.ds(pl.multiple_of(i * GROUP, GROUP), GROUP)
            rt, rs = wide[0, part, :], wide[1, part, :]
            acc = [0.0, 0.0, 0.0] if h == 0 else [sums[k, part, :] for k in range(3)]
            out = []
            for j, q in enumerate(span):
                t, s = tile(teach, part, q), tile(learn, part, q)
                gap = t - s
                e = jnp.exp(t - rt)
                acc = [acc[0] + e, acc[1] + jnp.exp(s - rs), acc[2] + e * gap]
                e = jnp.exp(t - t_tops[j])
                a, b, w = carry[j]
                out.append((a + e, b + jnp.exp(s - s_tops[j]), w + e * gap))
            for k in range(3):
                sums[k, part, :] = acc[k]
            return out

        none = jnp.zeros((GROUP, LANES), F32)
        out = lax.fori_loop(0, size // GROUP, sum_step, [(none,) * 3] * len(span), unroll=2)
        for j, q in enumerate(span):
            a, b, w = [jnp.sum(v, axis=0, keepdims=True) for v in out[j]]
            zero = jnp.zeros_like(w)
            col_st[:, q * LANES : (q + 1) * LANES] = jnp.concatenate(
                [col_tops[0][q], a, col_tops[1][q], b, w, zero, zero, zero], axis=0
            )
    a, b, w = [jnp.sum(sums[k].T, axis=0, keepdims=True) for k in range(3)]
    zero = jnp.zeros_like(w)
    row_st[...] = jnp.concatenate([row_tops[0], a, row_tops[1], b, w, zero, zero, zero], axis=0)
    for copy in leave:
        copy.wait()


def pass_1(pieces, n, d):
    size = NY * NX * n
    vmem = pl.BlockSpec(memory_space=pltpu.VMEM)
    hbm = pl.BlockSpec(memory_space=pltpu.HBM)
    both = jax.ShapeDtypeStruct((2, size, size), F32)
    blocks = jax.ShapeDtypeStruct((2, 16, n, d), BF)
    small = jax.ShapeDtypeStruct((8, size), F32)
    return pl.pallas_call(
        pass_1_kernel,
        out_shape=(both, blocks, small, small),
        in_specs=[vmem] * len(pieces),
        out_specs=(hbm, hbm, vmem, vmem),
        scratch_shapes=[
            pltpu.VMEM((size, size), F32),
            pltpu.VMEM((size, size), F32),
            pltpu.VMEM((2, 16, n, d), BF),
            pltpu.VMEM((2, 16, n, d), BF),
            pltpu.VMEM((2, size, LANES), F32),
            pltpu.VMEM((2, size, LANES), F32),
            pltpu.VMEM((3, size, LANES), F32),
            pltpu.SemaphoreType.DMA((4,)),
        ],
        compiler_params=pltpu.CompilerParams(vmem_limit_bytes=PASS_1_BYTES),
        cost_estimate=pl.CostEstimate(
            flops=4 * size * size * d, bytes_accessed=20 << 20, transcendentals=4 * size * size
        ),
    )(*pieces)


def merge(parts):
    parts = [[p[k : k + 1] for k in range(5)] for p in parts]
    t_top = parts[0][0]
    s_top = parts[0][2]
    for p in parts[1:]:
        t_top = jnp.maximum(t_top, p[0])
        s_top = jnp.maximum(s_top, p[2])
    terms = []
    for p in parts:
        a = jnp.exp(p[0] - t_top)
        terms.append((p[1] * a, p[3] * jnp.exp(p[2] - s_top), p[4] * a))
    while len(terms) > 1:
        terms = [
            tuple(u + v for u, v in zip(terms[i], terms[i + 1])) for i in range(0, len(terms), 2)
        ]
    t_sum, s_sum, w = terms[0]
    return [t_top, t_sum, s_top, s_sum, w]


def merged(parts):
    return jnp.concatenate(merge(parts), axis=0)


def pass_2_kernel(
    both_in, student_in, ra, rb, rc, rd, ca, cb,
    give, keep_image, keep_text, loss_part,
    teach, learn, rows, cols, coupling, wide, product, sem,
):
    z, c, y, x = position()
    n, d = rows.shape[1:]
    size = teach.shape[0]
    half = d // 2
    chunk = size // 4
    enter = []
    for r in range(4):
        part = pl.ds(r * chunk, chunk)
        for k, dst in ((0, teach), (1, learn)):
            enter.append(pltpu.make_async_copy(both_in.at[k, part], dst.at[part], sem.at[len(enter)]))
    enter.append(pltpu.make_async_copy(student_in.at[0], rows, sem.at[8]))
    enter.append(pltpu.make_async_copy(student_in.at[1], cols, sem.at[9]))
    for copy in enter:
        copy.start()
    row_st = merge([r[...] for r in (ra, rb, rc, rd)])
    col_st = merge([r[...] for r in (ca, cb)])
    row_t, row_s = row_st[0] + jnp.log(row_st[1]), row_st[2] + jnp.log(row_st[3])
    col_t, col_s = col_st[0] + jnp.log(col_st[1]), col_st[2] + jnp.log(col_st[3])
    part_r = jnp.sum(row_st[4] / row_st[1] + (row_s - row_t), axis=1, keepdims=True)
    part_c = jnp.sum(col_st[4] / col_st[1] + (col_s - col_t), axis=1, keepdims=True)
    loss_part[0] = jnp.broadcast_to(part_r, (8, LANES))
    loss_part[1] = jnp.broadcast_to(part_c, (8, LANES))
    whole = jnp.broadcast_to(part_r, (16, half))
    for k in range(3):
        piece = whole.astype(BF)
        give[32, 16 * k : 16 * k + 16] = piece
        whole = whole - piece.astype(F32)
    give[32, 48:] = jnp.zeros((n - 48, half), BF)
    for k, v in ((0, row_t), (1, row_s)):
        wide[k] = jnp.broadcast_to(v, (LANES, size)).T

    span = 4

    def chunk_step(r, carry):
        part = pl.ds(pl.multiple_of(r * chunk, chunk), chunk)
        pltpu.make_async_copy(both_in.at[0, part], teach.at[part], sem.at[2 * r]).wait()
        pltpu.make_async_copy(both_in.at[1, part], learn.at[part], sem.at[2 * r + 1]).wait()
        for h in range(size // (span * LANES)):
            lanes = [slice((h * span + j) * LANES, (h * span + j + 1) * LANES) for j in range(span)]
            ct = [jnp.broadcast_to(col_t[:, s], (16, LANES)) for s in lanes]
            cs = [jnp.broadcast_to(col_s[:, s], (16, LANES)) for s in lanes]

            def step(i, inner):
                part = pl.ds(pl.multiple_of(i * 16, 16), 16)
                rt, rs = wide[0, part, :], wide[1, part, :]
                for j in range(span):
                    t, s = teach[part, lanes[j]], learn[part, lanes[j]]
                    v = jnp.exp(s - rs) - jnp.exp(t - rt) + jnp.exp(s - cs[j]) - jnp.exp(t - ct[j])
                    coupling[part, lanes[j]] = (0.5 * v).astype(BF)
                return inner

            lax.fori_loop(r * (chunk // 16), (r + 1) * (chunk // 16), step, 0)
        return carry

    lax.fori_loop(0, 4, chunk_step, 0)
    enter[8].wait()
    enter[9].wait()

    def text_step(i, carry):
        part = pl.ds(pl.multiple_of(i * chunk, chunk), chunk)
        product[part, :] = 100.0 * lax.dot_general(
            coupling[:, part],
            rows[...].reshape(size, d),
            (((0,), (0,)), ((), ())),
            preferred_element_type=F32,
        )
        return carry

    lax.fori_loop(0, 4, text_step, 0)
    out = 1 - 2 * c

    def text_block(k, core):
        at = lax.rem(z + NZ + k, NZ) * NC + core
        return product[pl.ds(pl.multiple_of(at * n, n), n), :]

    def put(i, v):
        v = v.astype(BF)
        give[16 + i] = v[:, :half]
        give[24 + i] = v[:, half:]

    put(0, text_block(0, 1 - c))
    put(1, text_block(4, 1 - c))
    keep_text[0] = text_block(0, c)
    keep_text[1] = text_block(4, c)
    for k in (1, 2, 3):
        for core in range(2):
            put(2 * k + core, text_block(-out * k, core))
            keep_text[2 * k + core] = text_block(out * k, core)

    def image_step(i, carry):
        lanes = pl.ds(pl.multiple_of(i * (d // 4), d // 4), d // 4)
        product[:, lanes] = 100.0 * jnp.dot(
            coupling[...], cols[:, :, lanes].reshape(size, d // 4), preferred_element_type=F32
        )
        return carry

    lax.fori_loop(0, 4, image_step, 0)
    mine = pl.ds(pl.multiple_of(c * half, half), half)
    other = pl.ds(pl.multiple_of((1 - c) * half, half), half)
    for k in range(4):
        for f in range(4):
            dy = k * (1 - c) + f * c
            dx = f * (1 - c) + k * c
            at = lax.rem(y + dy, NY) * NX + lax.rem(x + dx, NX)
            part = pl.ds(pl.multiple_of(at * n, n), n)
            keep_image[f * 4 + k] = product[part, mine].astype(BF)
            give[k * 4 + f] = product[part, other].astype(BF)


def pass_2(args, n, d):
    size = NY * NX * n
    vmem = pl.BlockSpec(memory_space=pltpu.VMEM)
    return pl.pallas_call(
        pass_2_kernel,
        out_shape=(
            jax.ShapeDtypeStruct((33, n, d // 2), BF),
            jax.ShapeDtypeStruct((16, n, d // 2), BF),
            jax.ShapeDtypeStruct((8, n, d), F32),
            jax.ShapeDtypeStruct((2, 8, LANES), F32),
        ),
        in_specs=[pl.BlockSpec(memory_space=pltpu.HBM)] * 2 + [vmem] * (len(args) - 2),
        out_specs=(vmem,) * 4,
        scratch_shapes=[
            pltpu.VMEM((size, size), F32),
            pltpu.VMEM((size, size), F32),
            pltpu.VMEM((16, n, d), BF),
            pltpu.VMEM((16, n, d), BF),
            pltpu.VMEM((size, size), BF),
            pltpu.VMEM((2, size, LANES), F32),
            pltpu.VMEM((size, d), F32),
            pltpu.SemaphoreType.DMA((10,)),
        ],
        compiler_params=pltpu.CompilerParams(vmem_limit_bytes=PASS_2_BYTES),
        cost_estimate=pl.CostEstimate(
            flops=4 * size * size * d, bytes_accessed=20 << 20, transcendentals=4 * size * size
        ),
    )(*args)


def vmem_call(kernel, outs, args):
    vmem = pl.BlockSpec(memory_space=pltpu.VMEM)
    return pl.pallas_call(
        kernel,
        out_shape=tuple(jax.ShapeDtypeStruct(s, t) for s, t in outs),
        in_specs=[vmem] * len(args),
        out_specs=(vmem,) * len(outs),
        compiler_params=pltpu.CompilerParams(vmem_limit_bytes=VMEM_BYTES),
        cost_estimate=pl.CostEstimate(flops=1 << 20, bytes_accessed=4 << 20, transcendentals=0),
    )(*args)


def pack(ref, row, lane, v):
    v = jnp.broadcast_to(v, (16, LANES))
    for k in range(3):
        piece = v.astype(BF)
        ref[row : row + 16, lane + k * LANES : lane + (k + 1) * LANES] = piece
        v = v - piece.astype(F32)


def unpack(ref, row, lane):
    v = ref[row : row + 16, lane : lane + 3 * LANES].astype(F32)
    return (v[:1, :LANES] + v[:1, LANES : 2 * LANES]) + v[:1, 2 * LANES :]


def choose(flag, a, b):
    return jnp.where(flag + jnp.zeros(a.shape, jnp.int32) == 0, a, b)


def load_kernel(
    keep_text, keep_image, got, loss_part,
    text_own, k1, k2, k34, image_own, p1, m1, far, rows_loss,
):
    z, _, _, _ = position()
    n, h = got.shape[1:]
    for i in range(8):
        for q in range(2):
            lanes = slice(q * h, (q + 1) * h)
            v = keep_text[i, :, lanes] + got[16 + 8 * q + i].astype(F32)
            if i == 0:
                text_own[:, lanes] = v
            elif i == 1:
                k34[2 * n : 3 * n, lanes] = v.astype(BF)
            elif i >= 6:
                k34[(i - 6) * n : (i - 5) * n, lanes] = v.astype(BF)
            else:
                (k1, k2)[i // 2 - 1][i % 2, :, lanes] = v
    image_own[0] = keep_image[0:4]
    image_own[1] = got[0:4]
    cols_loss = loss_part[1, :1]
    for f, out in ((1, p1), (2, far), (3, m1)):
        out[: 4 * n] = keep_image[f * 4 : f * 4 + 4].reshape(4 * n, h)
        out[4 * n : 8 * n] = got[f * 4 : f * 4 + 4].reshape(4 * n, h)
        out[8 * n :] = jnp.zeros((16, h), BF)
        pack(out, 8 * n, 0, cols_loss)
    sib = got[32].astype(F32)
    chip = loss_part[0, :1] + ((sib[0:1, :LANES] + sib[16:17, :LANES]) + sib[32:33, :LANES])
    lane = lax.broadcasted_iota(jnp.int32, (1, LANES), 1)
    mine = jnp.where(lane == z, chip, 0.0)
    rows_loss[...] = jnp.broadcast_to(mine, (8, LANES))
    k34[3 * n :] = jnp.zeros((16, 2 * h), BF)
    pack(k34, 3 * n, 0, mine)


def pass_on_kernel(k1, k2, k34, rows_loss, b1, b2):
    _, c, _, _ = position()
    n, d = k1.shape[1:]
    for core in range(2):
        part = slice(core * n, (core + 1) * n)
        b1[part] = (k1[core] + k34[part].astype(F32)).astype(BF)
        v = k34[2 * n : 3 * n].astype(F32)
        b2[part] = (k2[core] + choose(c - core, v, jnp.zeros_like(v))).astype(BF)
    came = unpack(k34, 3 * n, 0)
    for ref in (b1, b2):
        ref[2 * n :] = jnp.zeros((16, d), BF)
    pack(b1, 2 * n, 0, rows_loss[:1] + came)
    pack(b2, 2 * n, 0, came)


def ring_sum(odd, own, back, ahead, far):
    return (own + choose(odd, ahead, back)) + (far + choose(odd, back, ahead))


def line_kernel(own, p1, m1, far, loss_part, out, w1, w2, w3, cols_loss):
    _, c, y, x = position()
    n, h = own.shape[2:]
    for k, ref in enumerate((out, w1, w2, w3)):
        for core in range(2):
            part = slice((core * 4 + k) * n, (core * 4 + k + 1) * n)
            v = own[core, k].astype(F32) + far[part].astype(F32)
            v = v + p1[part].astype(F32) + m1[part].astype(F32)
            ref[core * n : (core + 1) * n] = v.astype(ref.dtype)
    odd = lax.rem(x * (1 - c) + y * c, 2)
    v = ring_sum(odd, loss_part[1, :1], *[unpack(r, 8 * n, 0) for r in (p1, m1, far)])
    cols_loss[...] = jnp.broadcast_to(v, (8, LANES))
    for ref in (w1, w2, w3):
        ref[2 * n :] = jnp.zeros((16, h), BF)
        pack(ref, 2 * n, 0, v)


def last_kernel(
    text_own, b1, b2, k34, rows_loss, line, w1, w2, w3, cols_loss,
    text, image, share, loss,
):
    _, c, y, x = position()
    n, d = text.shape
    ways = []
    for core in range(2):
        part = slice(core * n, (core + 1) * n)
        ways.append(b1[part].astype(F32) + b2[part].astype(F32))
    text[...] = text_own[...] + choose(c, ways[0], ways[1])
    share[:n, :d] = choose(c, ways[1], ways[0]).astype(BF)
    v = line[...]
    for r in (w1, w2, w3):
        v = v + r[: 2 * n].astype(F32)
    image[...] = v[:n].astype(BF)
    share[:n, d:] = v[n:].astype(BF)
    odd = lax.rem(y * (1 - c) + x * c, 2)
    cols = ring_sum(odd, cols_loss[:1], *[unpack(r, 2 * n, 0) for r in (w1, w3, w2)])
    near = unpack(k34, 3 * n, 0) + unpack(b1, 2 * n, 0)
    rows = choose(c, near + (rows_loss[:1] + unpack(b2, 2 * n, 0)), near)
    share[n:] = jnp.zeros((16, share.shape[1]), BF)
    pack(share, n, 0, rows)
    pack(share, n, 3 * LANES, cols)
    loss[0] = jnp.broadcast_to(rows, (8, LANES))
    loss[1] = jnp.broadcast_to(cols, (8, LANES))


def end_kernel(text, image, share, loss, text_grad, image_grad, total):
    _, c, _, _ = position()
    n, d = text.shape
    h = d // 2
    text_grad[...] = (text[...] + share[:n, :d].astype(F32)).astype(BF)
    mine, other = image[...].astype(F32), share[:n, d:].astype(F32)
    image_grad[:, :h] = choose(c, mine, other).astype(BF)
    image_grad[:, h:] = choose(c, other, mine).astype(BF)
    rows = loss[0, :1] + unpack(share, n, 0)
    cols = choose(c, loss[1, :1], unpack(share, n, 3 * LANES))
    total[...] = jnp.broadcast_to(jnp.sum(rows, axis=1, keepdims=True) + cols, (8, LANES))


def reduce_all(give, keep_image, keep_text, loss_part):
    n, d = keep_text.shape[1:]
    h = d // 2
    got = swap(give, c_bits=1)
    small = ((8, LANES), F32)
    pair, line_out = ((2, n, d), F32), ((8 * n + 16, h), BF)
    text_own, k1, k2, k34, image_own, p1, m1, far, rows_loss = vmem_call(
        load_kernel,
        [((n, d), F32), pair, pair, ((3 * n + 16, d), BF), ((2, 4, n, h), BF)]
        + [line_out] * 3
        + [small],
        (keep_text, keep_image, got, loss_part),
    )
    far = move_first(far, 2)
    k34 = move_z(k34, 2)
    p1 = move_first(p1, 1)
    m1 = move_first(m1, -1)
    b1, b2 = vmem_call(
        pass_on_kernel, [((2 * n + 16, d), BF)] * 2, (k1, k2, k34, rows_loss)
    )
    b1 = move_z(b1, 1)
    b2 = move_z(b2, 2)
    line, w1, w2, w3, cols_loss = vmem_call(
        line_kernel,
        [((2 * n, h), F32)] + [((2 * n + 16, h), BF)] * 3 + [small],
        (image_own, p1, m1, far, loss_part),
    )
    w1 = move_second(w1, 1)
    w2 = move_second(w2, 2)
    w3 = move_second(w3, -1)
    text, image, share, loss = vmem_call(
        last_kernel,
        [((n, d), F32), ((n, h), BF), ((n + 16, d + h), BF), ((2, 8, LANES), F32)],
        (text_own, b1, b2, k34, rows_loss, line, w1, w2, w3, cols_loss),
    )
    return vmem_call(
        end_kernel,
        [((n, d), BF), ((n, d), BF), small],
        (text, image, swap(share, c_bits=1), loss),
    )


def merge_steps(row_st, col_st):
    row_st = merged([row_st] + [swap(row_st, x_bits=b) for b in (1, 2, 3)])
    col_st = merged([col_st, swap(col_st, c_bits=1)])
    col_st = merged([col_st] + [swap(col_st, z_bits=b) for b in (1, 2, 3)])
    return [row_st] + [swap(row_st, y_bits=b) for b in (1, 2, 3)] + [
        col_st,
        swap(col_st, z_bits=4),
    ]


def per_device(teacher_image, teacher_text, student_image, student_text):
    n, d = teacher_image.shape
    total_pairs = n * NX * NY * NZ * NC
    core = lax.rem(lax.axis_index("row"), NC)
    keep = jnp.where(core == 0, teacher_image, student_image)
    give = jnp.where(core == 0, student_image, teacher_image)
    shared = swap(jnp.stack([give, teacher_text, student_text]), c_bits=1)
    text_blocks = gather_cols(
        jnp.stack([jnp.stack([teacher_text, student_text]), shared[1:]])
    )
    image_blocks = gather_rows(jnp.stack([keep, shared[0]]))
    both, student, row_st, col_st = pass_1(
        list(image_blocks) + list(text_blocks), n, d
    )
    give, keep_image, keep_text, loss_part = pass_2(
        [both, student] + merge_steps(row_st, col_st), n, d
    )
    text_grad, image_grad, loss = reduce_all(give, keep_image, keep_text, loss_part)
    return (image_grad, text_grad, loss[0, 0] * (0.5 / total_pairs))


def solution(mesh):
    placed = P(("row", "col"), None)
    return jax.shard_map(
        per_device,
        mesh=mesh,
        in_specs=(placed,) * 4,
        out_specs=(placed, placed, P()),
        check_vma=False,
    )
```

time: 451 us -> 148 us (0.33)
  blocking collectives: 216 us -> 0 us
  waiting for transfers between devices: 167 us -> 39.9 us
  starting transfers between devices: 0.23 us -> 68.6 us
  Pallas kernels: 0 us -> 27.1 us
  matrix products: 19.6 us -> 0 us
  other arithmetic: 19.1 us -> 3.67 us
  between operations: 18.1 us -> 2.68 us
    all_gather x8 -> x0, blocking collectives: 132 us -> none  [merged(): everything = jax.tree.map(lambda part: lax.all_gather(part, axis), value)]
    all_gather x4 -> x0, waiting for transfers between devices: 108 us -> none  [the longest x1 51.8 us: per_device(): lax.all_gather(teacher_image, 'col', axis=0, tiled=True)]
    psum x1 -> x0, blocking collectives: 84.3 us -> none  [per_device(): loss = lax.psum(local_part, ('row', 'col')) * (0.5 / total_pairs)]
    ppermute x0 -> x41, starting transfers between devices: none -> 68.6 us  [send(): return lax.ppermute(v, ('row', 'col'), pairs)]
    reduce_scatter x2 -> x0, waiting for transfers between devices: 56.5 us -> none  [the longest x1 56.5 us: per_device(): lax.psum_scatter(100.0 * lax.dot_general(coupling, s_rows, (((0,), (0,)),...]
    ppermute x0 -> x41, waiting for transfers between devices: none -> 39.9 us  [send(): return lax.ppermute(v, ('row', 'col'), pairs)]
    pallas_call x0 -> x7, Pallas kernels: none -> 27.1 us  [the longest x1 14.1 us: pass_2(): pl.pallas_call(pass_2_kernel, out_shape=(jax.ShapeDtypeStruct((33, n, d /...]
    dot_general x4 -> x0, matrix products: 19.6 us -> none  [the longest x2 9.34 us: similarity(): lax.dot_general(left, right, (((1,), (1,)), ((), ())), preferred_element_...]
  transfers between devices with their start and end apart: 6 -> 41, of which waited for: 4 -> 17; matrix products, arithmetic and copies ran while one was open for 4% -> 2% of each run, Pallas kernels for 0% -> 0%
where the time goes in v1:
time: 148 us; the launch traced here: 145 us
  starting transfers between devices  68.6 us (46%)
  waiting for transfers between devices  39.9 us (27%)
  Pallas kernels  27.1 us (18%)
  other arithmetic  3.67 us (2%)
  local copies, waits for them, and re-layouts  2.84 us (2%)
  between operations  2.68 us (2%)
    ppermute x41, starting transfers between devices, send(): return lax.ppermute(v, ('row', 'col'), pairs)  68.6 us
    ppermute x41, waiting for transfers between devices, send(): return lax.ppermute(v, ('row', 'col'), pairs)  39.9 us
    pallas_call x1, Pallas kernels, pass_2(): pl.pallas_call(pass_2_kernel, out_shape=(jax.ShapeDtypeStruct((33, n, d /...  14.1 us
    pallas_call x1, Pallas kernels, pass_1(): pl.pallas_call(pass_1_kernel, out_shape=(both, blocks, small, small), in_...  11.3 us
  transfers between devices with their start and end apart: 41, of which 17 were waited for; matrix products, arithmetic and copies ran while one was open for 2% of the time, Pallas kernels for 0%

profile of v1, /device:TPU:39, one launch (start us, length us, event | category | flops | bytes accessed | tf_op | source)
XLA Modules:
  0.0 144.8 jit_solution(15026935135140827435)
XLA Ops:
  0.6 1.0 select_bitcast_fusion.1
  1.6 1.0 pad_maximum_fusion.4
  2.6 0.8 collective-permute-start
  3.4 1.0 maximum_bitcast_fusion
  4.8 3.0 %collective-permute-start.2 = (bf16[2,64,1024]{2,1,0:T(8,128)(2,1)S(1)}, bf16[2,64,1024]{2,1,0:T(8,128)(2,1)S(1)}, u32[]{:S(2)}, u32[]{:S(2)}) collective-permute-start(bf16[2,64,1024]{2,1,0:T(8,128)(2,1)S(1)} %get-tuple-element.78), channel_id=1, source_target_pairs={{0,2},{1,3},{2,0},{3,1},{4,6},{5,7},{6,4},{7,5},{8,10},{9,11},{10,... | collective-permute-start | bytes 786440 | tf_op jit(solution)/shard_map/ppermute | solution.py:30
  7.8 0.8 collective-permute-start.1
  9.5 2.5 %collective-permute-done.2 = bf16[2,64,1024]{2,1,0:T(8,128)(2,1)S(1)} collective-permute-done((bf16[2,64,1024]{2,1,0:T(8,128)(2,1)S(1)}, bf16[2,64,1024]{2,1,0:T(8,128)(2,1)S(1)}, u32[]{:S(2)}, u32[]{:S(2)}) %collective-permute-start.2) | collective-permute-done | bytes 262176 | tf_op jit(solution)/shard_map/ppermute | solution.py:30
  11.9 3.2 %collective-permute-done.1 = bf16[2,64,1024]{2,1,0:T(8,128)(2,1)S(1)} collective-permute-done((bf16[2,64,1024]{2,1,0:T(8,128)(2,1)S(1)}, bf16[2,64,1024]{2,1,0:T(8,128)(2,1)S(1)}, u32[]{:S(2)}, u32[]{:S(2)}) %collective-permute-start.1) | collective-permute-done | bytes 262176 | tf_op jit(solution)/shard_map/ppermute | solution.py:30
  15.9 2.3 %collective-permute-start.4 = (bf16[2,4,64,1024]{3,2,0,1:T(8,128)(2,1)S(1)}, bf16[2,4,64,1024]{3,2,0,1:T(8,128)(2,1)S(1)}, u32[]{:S(2)}, u32[]{:S(2)}) collective-permute-start(bf16[2,4,64,1024]{3,2,0,1:T(8,128)(2,1)S(1)} %pad_maximum_fusion), channel_id=1, source_target_pairs={{0,4},{1,5},{2,6},{3,7},{4,8},{5,9},{6,10},{7,11},{8,12},{9,13},{1... | collective-permute-start | bytes 3145736 | tf_op jit(solution)/shard_map/ppermute | solution.py:30
  18.2 2.8 %collective-permute-start.12 = (bf16[2,2,64,1024]{3,2,1,0:T(8,128)(2,1)S(1)}, bf16[2,2,64,1024]{3,2,1,0:T(8,128)(2,1)S(1)}, u32[]{:S(2)}, u32[]{:S(2)}) collective-permute-start(bf16[2,2,64,1024]{3,2,1,0:T(8,128)(2,1)S(1)} %collective-permute-done.11.t1), channel_id=1, source_target_pairs={{0,32},{1,33},{2,34},{3,35},{4,36},{5,37},{6,38},{7,39},{8,40},{9,... | collective-permute-start | bytes 1572872 | tf_op jit(solution)/shard_map/ppermute | solution.py:30
  21.0 6.1 %collective-permute-done.12.t2 = bf16[2,2,64,1024]{3,2,1,0:T(8,128)(2,1)S(1)} collective-permute-done((bf16[2,2,64,1024]{3,2,1,0:T(8,128)(2,1)S(1)}, bf16[2,2,64,1024]{3,2,1,0:T(8,128)(2,1)S(1)}, u32[]{:S(2)}, u32[]{:S(2)}) %collective-permute-start.12) | collective-permute-done | bytes 524320 | tf_op jit(solution)/shard_map/ppermute | solution.py:30
  27.1 3.1 %collective-permute-start.13 = (bf16[2,2,64,1024]{3,2,1,0:T(8,128)(2,1)S(1)}, bf16[2,2,64,1024]{3,2,1,0:T(8,128)(2,1)S(1)}, u32[]{:S(2)}, u32[]{:S(2)}) collective-permute-start(bf16[2,2,64,1024]{3,2,1,0:T(8,128)(2,1)S(1)} %collective-permute-done.12.t2), channel_id=1, source_target_pairs={{0,32},{1,33},{2,34},{3,35},{4,36},{5,37},{6,38},{7,39},{8,40},{9,... | collective-permute-start | bytes 1572872 | tf_op jit(solution)/shard_map/ppermute | solution.py:30
  31.0 4.5 %collective-permute-start.8 = (bf16[4,64,1024]{2,1,0:T(8,128)(2,1)S(1)}, bf16[4,64,1024]{2,1,0:T(8,128)(2,1)S(1)}, u32[]{:S(2)}, u32[]{:S(2)}) collective-permute-start(bf16[4,64,1024]{2,1,0:T(8,128)(2,1)S(1)} %slice_bitcast_fusion), channel_id=1, source_target_pairs={{0,16},{1,17},{2,18},{3,19},{4,20},{5,21},{6,22},{7,23},{8,24},{9,... | collective-permute-start | bytes 1572872 | tf_op jit(solution)/shard_map/ppermute | solution.py:30
  35.7 1.3 collective-permute-start.6
  37.2 3.6 %collective-permute-start.9 = (bf16[2,4,64,1024]{3,2,0,1:T(8,128)(2,1)S(1)}, bf16[2,4,64,1024]{3,2,0,1:T(8,128)(2,1)S(1)}, u32[]{:S(2)}, u32[]{:S(2)}) collective-permute-start(bf16[2,4,64,1024]{3,2,0,1:T(8,128)(2,1)S(1)} %pad_maximum_fusion.1), channel_id=1, source_target_pairs={{0,16},{1,17},{2,18},{3,19},{4,20},{5,21},{6,22},{7,23},{8,24},{9,... | collective-permute-start | bytes 3145736 | tf_op jit(solution)/shard_map/ppermute | solution.py:30
  40.8 1.3 collective-permute-start.16
  42.1 1.9 %collective-permute-done.6 = bf16[2,2,64,1024]{3,2,0,1:T(8,128)(2,1)S(1)} collective-permute-done((bf16[2,2,64,1024]{3,2,0,1:T(8,128)(2,1)S(1)}, bf16[2,2,64,1024]{3,2,0,1:T(8,128)(2,1)S(1)}, u32[]{:S(2)}, u32[]{:S(2)}) %collective-permute-start.6) | collective-permute-done | bytes 524320 | tf_op jit(solution)/shard_map/ppermute | solution.py:30
  44.1 1.1 collective-permute-start.14
  45.3 3.6 %collective-permute-start.17 = (bf16[2,2,64,1024]{3,2,1,0:T(8,128)(2,1)S(1)}, bf16[2,2,64,1024]{3,2,1,0:T(8,128)(2,1)S(1)}, u32[]{:S(2)}, u32[]{:S(2)}) collective-permute-start(bf16[2,2,64,1024]{3,2,1,0:T(8,128)(2,1)S(1)} %collective-permute-done.13.t3), channel_id=1, source_target_pairs={{0,16},{1,17},{2,18},{3,19},{4,20},{5,21},{6,22},{7,23},{8,24},{9,... | collective-permute-start | bytes 1572872 | tf_op jit(solution)/shard_map/ppermute | solution.py:30
  48.9 0.9 collective-permute-done.14.far
  49.8 3.1 %collective-permute-start.10 = (bf16[4,64,1024]{2,1,0:T(8,128)(2,1)S(1)}, bf16[4,64,1024]{2,1,0:T(8,128)(2,1)S(1)}, u32[]{:S(2)}, u32[]{:S(2)}) collective-permute-start(bf16[4,64,1024]{2,1,0:T(8,128)(2,1)S(1)} %pad_maximum_fusion.2), channel_id=1, source_target_pairs={{0,16},{1,17},{2,18},{3,19},{4,20},{5,21},{6,22},{7,23},{8,24},{9,... | collective-permute-start | bytes 1572872 | tf_op jit(solution)/shard_map/ppermute | solution.py:30
  53.3 1.6 %collective-permute-done.18.far_sib = bf16[2,64,1024]{2,1,0:T(8,128)(2,1)S(1)} collective-permute-done((bf16[2,64,1024]{2,1,0:T(8,128)(2,1)S(1)}, bf16[2,64,1024]{2,1,0:T(8,128)(2,1)S(1)}, u32[]{:S(2)}, u32[]{:S(2)}) %collective-permute-start.18) | collective-permute-done | bytes 262176 | tf_op jit(solution)/shard_map/ppermute | solution.py:30
  54.8 11.3 %shard_map.67 = (f32[2,1024,1024]{2,1,0:T(8,128)}, bf16[2,16,64,1024]{3,2,1,0:T(8,128)(2,1)}, f32[8,1024]{1,0:T(8,128)S(1)}, f32[8,1024]{1,0:T(8,128)S(1)}) custom-call(bf16[2,4,64,1024]{3,2,1,0:T(8,128)(2,1)S(1)} %copy.8.line, bf16[2,4,64,1024]{3,2,1,0:T(8,128)(2,1)S(1)} %copy.9.up, bf16[2,4,64,1024]{3,2,1,0:T(8,128)(2,1)S(1)} %copy.10.down, ...), custom_call_target="tpu_custom_call" | custom-call | flops 4294967296 | bytes 20971520 | tf_op jit(solution)/shard_map/pallas_call | solution.py:206
  66.6 1.3 collective-permute-start.21
  67.8 1.1 collective-permute-start.20
  68.9 0.9 collective-permute-start.19
  70.0 3.0 %collective-permute-start.28 = (f32[5,1024]{1,0:T(8,128)S(1)}, f32[5,1024]{1,0:T(8,128)S(1)}, u32[]{:S(2)}, u32[]{:S(2)}) collective-permute-start(f32[5,1024]{1,0:T(8,128)S(1)} %concatenate.14), channel_id=1, source_target_pairs={{0,96},{1,97},{2,98},{3,99},{4,100},{5,101},{6,102},{7,103},{8,104... | collective-permute-start | bytes 61448 | tf_op jit(solution)/shard_map/ppermute | solution.py:30
  72.9 2.9 %collective-permute-start.27 = (f32[5,1024]{1,0:T(8,128)S(1)}, f32[5,1024]{1,0:T(8,128)S(1)}, u32[]{:S(2)}, u32[]{:S(2)}) collective-permute-start(f32[5,1024]{1,0:T(8,128)S(1)} %concatenate.14), channel_id=1, source_target_pairs={{0,64},{1,65},{2,66},{3,67},{4,68},{5,69},{6,70},{7,71},{8,72},{9,... | collective-permute-start | bytes 61448 | tf_op jit(solution)/shard_map/ppermute | solution.py:30
  76.6 3.0 %collective-permute-start.22 = (f32[5,1024]{1,0:T(8,128)S(1)}, f32[5,1024]{1,0:T(8,128)S(1)}, u32[]{:S(2)}, u32[]{:S(2)}) collective-permute-start(f32[5,1024]{1,0:T(8,128)S(1)} %concatenate.13.ra), channel_id=1, source_target_pairs={{0,4},{1,5},{2,6},{3,7},{4,0},{5,1},{6,2},{7,3},{8,12},{9,13},{10,... | collective-permute-start | bytes 61448 | tf_op jit(solution)/shard_map/ppermute | solution.py:30
  79.7 4.4 %collective-permute-start.29 = (f32[5,1024]{1,0:T(8,128)S(1)}, f32[5,1024]{1,0:T(8,128)S(1)}, u32[]{:S(2)}, u32[]{:S(2)}) collective-permute-start(f32[5,1024]{1,0:T(8,128)S(1)} %concatenate.15.ca), channel_id=1, source_target_pairs={{0,128},{1,129},{2,130},{3,131},{4,132},{5,133},{6,134},{7,135},{8... | collective-permute-start | bytes 61448 | tf_op jit(solution)/shard_map/ppermute | solution.py:30
  84.1 2.6 %collective-permute-done.29.cb = f32[5,1024]{1,0:T(8,128)S(1)} collective-permute-done((f32[5,1024]{1,0:T(8,128)S(1)}, f32[5,1024]{1,0:T(8,128)S(1)}, u32[]{:S(2)}, u32[]{:S(2)}) %collective-permute-start.29) | collective-permute-done | bytes 20512 | tf_op jit(solution)/shard_map/ppermute | solution.py:30
  86.7 14.1 %shard_map.68 = (bf16[33,64,512]{2,1,0:T(8,128)(2,1)}, bf16[16,64,512]{2,1,0:T(8,128)(2,1)S(1)}, f32[8,64,1024]{2,1,0:T(8,128)}, f32[2,8,128]{2,1,0:T(8,128)S(1)}) custom-call(f32[2,1024,1024]{2,1,0:T(8,128)} %get-tuple-element.34.both_in, bf16[2,16,64,1024]{3,2,1,0:T(8,128)(2,1)} %get-tuple-element.35.student_in, f32[5,1024]{1,0:T(8,128)S(1)} %concatenate.13.ra, ...), custom_call_target="tpu_custom_call" | custom-call | flops 4294967296 | bytes 20971520 | tf_op jit(solution)/shard_map/pallas_call | solution.py:368
  100.8 3.7 %collective-permute-start.30 = (bf16[33,64,512]{2,1,0:T(8,128)(2,1)}, bf16[33,64,512]{2,1,0:T(8,128)(2,1)S(1)}, u32[]{:S(2)}, u32[]{:S(2)}) collective-permute-start(bf16[33,64,512]{2,1,0:T(8,128)(2,1)} %get-tuple-element.40), channel_id=1, source_target_pairs={{0,16},{1,17},{2,18},{3,19},{4,20},{5,21},{6,22},{7,23},{8,24},{9,... | collective-permute-start | bytes 6488072 | tf_op jit(solution)/shard_map/ppermute | solution.py:30
  104.5 4.1 %collective-permute-done.30.got = bf16[33,64,512]{2,1,0:T(8,128)(2,1)S(1)} collective-permute-done((bf16[33,64,512]{2,1,0:T(8,128)(2,1)}, bf16[33,64,512]{2,1,0:T(8,128)(2,1)S(1)}, u32[]{:S(2)}, u32[]{:S(2)}) %collective-permute-start.30) | collective-permute-done | bytes 2162720 | tf_op jit(solution)/shard_map/ppermute | solution.py:30
  108.6 1.6 %copy-done = f32[8,64,1024]{2,1,0:T(8,128)S(1)} copy-done((f32[8,64,1024]{2,1,0:T(8,128)S(1)}, f32[8,64,1024]{2,1,0:T(8,128)}, u32[]{:S(2)}) %copy-start) | copy-done | bytes 2097176
  110.6 3.0 %collective-permute-start.31 = (bf16[208,1024]{1,0:T(8,128)(2,1)S(1)}, bf16[208,1024]{1,0:T(8,128)(2,1)S(1)}, u32[]{:S(2)}, u32[]{:S(2)}) collective-permute-start(bf16[208,1024]{1,0:T(8,128)(2,1)S(1)} %get-tuple-element.45), channel_id=1, source_target_pairs={{0,64},{1,65},{2,66},{3,67},{4,68},{5,69},{6,70},{7,71},{8,72},{9,... | collective-permute-start | bytes 1277960 | tf_op jit(solution)/shard_map/ppermute | solution.py:30
  113.6 2.7 %collective-permute-start.35 = (bf16[528,512]{1,0:T(8,128)(2,1)S(1)}, bf16[528,512]{1,0:T(8,128)(2,1)S(1)}, u32[]{:S(2)}, u32[]{:S(2)}) collective-permute-start(bf16[528,512]{1,0:T(8,128)(2,1)S(1)} %get-tuple-element.51), channel_id=1, source_target_pairs={{0,3},{1,0},{2,1},{3,2},{4,7},{5,4},{6,5},{7,6},{8,11},{9,8},{10,9... | collective-permute-start | bytes 1622024 | tf_op jit(solution)/shard_map/ppermute | solution.py:30
  116.2 7.0 %collective-permute-done.31.k34 = bf16[208,1024]{1,0:T(8,128)(2,1)S(1)} collective-permute-done((bf16[208,1024]{1,0:T(8,128)(2,1)S(1)}, bf16[208,1024]{1,0:T(8,128)(2,1)S(1)}, u32[]{:S(2)}, u32[]{:S(2)}) %collective-permute-start.31) | collective-permute-done | bytes 426016 | tf_op jit(solution)/shard_map/ppermute | solution.py:30
  123.3 1.8 %collective-permute-start.32 = (bf16[144,1024]{1,0:T(8,128)(2,1)S(1)}, bf16[144,1024]{1,0:T(8,128)(2,1)S(1)}, u32[]{:S(2)}, u32[]{:S(2)}) collective-permute-start(bf16[144,1024]{1,0:T(8,128)(2,1)S(1)} %get-tuple-element.47), channel_id=1, source_target_pairs={{0,32},{1,33},{2,34},{3,35},{4,36},{5,37},{6,38},{7,39},{8,40},{9,... | collective-permute-start | bytes 884744 | tf_op jit(solution)/shard_map/ppermute | solution.py:30
  125.1 2.7 %collective-permute-start.33 = (bf16[144,1024]{1,0:T(8,128)(2,1)S(1)}, bf16[144,1024]{1,0:T(8,128)(2,1)S(1)}, u32[]{:S(2)}, u32[]{:S(2)}) collective-permute-start(bf16[144,1024]{1,0:T(8,128)(2,1)S(1)} %get-tuple-element.48), channel_id=1, source_target_pairs={{0,64},{1,65},{2,66},{3,67},{4,68},{5,69},{6,70},{7,71},{8,72},{9,... | collective-permute-start | bytes 884744 | tf_op jit(solution)/shard_map/ppermute | solution.py:30
  127.8 1.2 collective-permute-done.34.p1
  129.3 1.7 %collective-permute-start.37 = (bf16[144,512]{1,0:T(8,128)(2,1)S(1)}, bf16[144,512]{1,0:T(8,128)(2,1)S(1)}, u32[]{:S(2)}, u32[]{:S(2)}) collective-permute-start(bf16[144,512]{1,0:T(8,128)(2,1)S(1)} %get-tuple-element.54), channel_id=1, source_target_pairs={{0,4},{1,5},{2,6},{3,7},{4,8},{5,9},{6,10},{7,11},{8,12},{9,13},{1... | collective-permute-start | bytes 442376 | tf_op jit(solution)/shard_map/ppermute | solution.py:30
  131.0 0.8 collective-permute-start.38
  131.8 2.9 %collective-permute-done.37.w1 = bf16[144,512]{1,0:T(8,128)(2,1)S(1)} collective-permute-done((bf16[144,512]{1,0:T(8,128)(2,1)S(1)}, bf16[144,512]{1,0:T(8,128)(2,1)S(1)}, u32[]{:S(2)}, u32[]{:S(2)}) %collective-permute-start.37) | collective-permute-done | bytes 147488 | tf_op jit(solution)/shard_map/ppermute | solution.py:30
  134.7 2.1 %collective-permute-done.38.w2 = bf16[144,512]{1,0:T(8,128)(2,1)S(1)} collective-permute-done((bf16[144,512]{1,0:T(8,128)(2,1)S(1)}, bf16[144,512]{1,0:T(8,128)(2,1)S(1)}, u32[]{:S(2)}, u32[]{:S(2)}) %collective-permute-start.38) | collective-permute-done | bytes 147488 | tf_op jit(solution)/shard_map/ppermute | solution.py:30
  136.8 1.6 %collective-permute-done.39.w3 = bf16[144,512]{1,0:T(8,128)(2,1)S(1)} collective-permute-done((bf16[144,512]{1,0:T(8,128)(2,1)S(1)}, bf16[144,512]{1,0:T(8,128)(2,1)S(1)}, u32[]{:S(2)}, u32[]{:S(2)}) %collective-permute-start.39) | collective-permute-done | bytes 147488 | tf_op jit(solution)/shard_map/ppermute | solution.py:30
  138.6 2.1 %collective-permute-start.40 = (bf16[80,1536]{1,0:T(8,128)(2,1)S(1)}, bf16[80,1536]{1,0:T(8,128)(2,1)S(1)}, u32[]{:S(2)}, u32[]{:S(2)}) collective-permute-start(bf16[80,1536]{1,0:T(8,128)(2,1)S(1)} %get-tuple-element.60), channel_id=1, source_target_pairs={{0,16},{1,17},{2,18},{3,19},{4,20},{5,21},{6,22},{7,23},{8,24},{9,... | collective-permute-start | bytes 737288 | tf_op jit(solution)/shard_map/ppermute | solution.py:30
  140.6 1.1 collective-permute-done.40.share
  (76 shorter events, 7.3 us)
Async XLA Ops:
  2.6 2.1 %collective-permute-start = (bf16[3,64,1024]{2,1,0:T(8,128)(2,1)S(1)}, bf16[3,64,1024]{2,1,0:T(8,128)(2,1)S(1)}, u32[]{:S(2)}, u32[]{:S(2)}) collective-permute-start(bf16[3,64,1024]{2,1,0:T(8,128)(2,1)S(1)} %pad_maximum_fusion.4), channel_id=1, source_target_pairs={{0,16},{1,17},{2,18},{3,19},{4,20},{5,21},{6,22},{7,23},{8,24},{9,... | collective-permute-start | bytes 1179656 | tf_op jit(solution)/shard_map/ppermute | solution.py:30
  4.8 7.1 %collective-permute-start.2 = (bf16[2,64,1024]{2,1,0:T(8,128)(2,1)S(1)}, bf16[2,64,1024]{2,1,0:T(8,128)(2,1)S(1)}, u32[]{:S(2)}, u32[]{:S(2)}) collective-permute-start(bf16[2,64,1024]{2,1,0:T(8,128)(2,1)S(1)} %get-tuple-element.78), channel_id=1, source_target_pairs={{0,2},{1,3},{2,0},{3,1},{4,6},{5,7},{6,4},{7,5},{8,10},{9,11},{10,... | collective-permute-start | bytes 786440 | tf_op jit(solution)/shard_map/ppermute | solution.py:30
  7.8 7.3 %collective-permute-start.1 = (bf16[2,64,1024]{2,1,0:T(8,128)(2,1)S(1)}, bf16[2,64,1024]{2,1,0:T(8,128)(2,1)S(1)}, u32[]{:S(2)}, u32[]{:S(2)}) collective-permute-start(bf16[2,64,1024]{2,1,0:T(8,128)(2,1)S(1)} %get-tuple-element.78), channel_id=1, source_target_pairs={{0,3},{1,0},{2,1},{3,2},{4,7},{5,4},{6,5},{7,6},{8,11},{9,8},{10,9... | collective-permute-start | bytes 786440 | tf_op jit(solution)/shard_map/ppermute | solution.py:30
  8.6 6.7 %collective-permute-start.3 = (bf16[2,64,1024]{2,1,0:T(8,128)(2,1)S(1)}, bf16[2,64,1024]{2,1,0:T(8,128)(2,1)S(1)}, u32[]{:S(2)}, u32[]{:S(2)}) collective-permute-start(bf16[2,64,1024]{2,1,0:T(8,128)(2,1)S(1)} %get-tuple-element.78), channel_id=1, source_target_pairs={{0,1},{1,2},{2,3},{3,0},{4,5},{5,6},{6,7},{7,4},{8,9},{9,10},{10,1... | collective-permute-start | bytes 786440 | tf_op jit(solution)/shard_map/ppermute | solution.py:30
  9.4 8.8 %collective-permute-start.11 = (bf16[2,2,64,1024]{3,2,1,0:T(8,128)(2,1)S(1)}, bf16[2,2,64,1024]{3,2,1,0:T(8,128)(2,1)S(1)}, u32[]{:S(2)}, u32[]{:S(2)}) collective-permute-start(bf16[2,2,64,1024]{3,2,1,0:T(8,128)(2,1)S(1)} %pad_maximum_fusion.3.t0), channel_id=1, source_target_pairs={{0,32},{1,33},{2,34},{3,35},{4,36},{5,37},{6,38},{7,39},{8,40},{9,... | collective-permute-start | bytes 1572872 | tf_op jit(solution)/shard_map/ppermute | solution.py:30
  15.5 15.2 %collective-permute-start.5 = (bf16[2,4,64,1024]{3,2,0,1:T(8,128)(2,1)S(1)}, bf16[2,4,64,1024]{3,2,0,1:T(8,128)(2,1)S(1)}, u32[]{:S(2)}, u32[]{:S(2)}) collective-permute-start(bf16[2,4,64,1024]{3,2,0,1:T(8,128)(2,1)S(1)} %pad_maximum_fusion), channel_id=1, source_target_pairs={{0,12},{1,13},{2,14},{3,15},{4,0},{5,1},{6,2},{7,3},{8,4},{9,5},{1... | collective-permute-start | bytes 3145736 | tf_op jit(solution)/shard_map/ppermute | solution.py:30
  15.9 19.7 %collective-permute-start.4 = (bf16[2,4,64,1024]{3,2,0,1:T(8,128)(2,1)S(1)}, bf16[2,4,64,1024]{3,2,0,1:T(8,128)(2,1)S(1)}, u32[]{:S(2)}, u32[]{:S(2)}) collective-permute-start(bf16[2,4,64,1024]{3,2,0,1:T(8,128)(2,1)S(1)} %pad_maximum_fusion), channel_id=1, source_target_pairs={{0,4},{1,5},{2,6},{3,7},{4,8},{5,9},{6,10},{7,11},{8,12},{9,13},{1... | collective-permute-start | bytes 3145736 | tf_op jit(solution)/shard_map/ppermute | solution.py:30
  18.2 8.9 %collective-permute-start.12 = (bf16[2,2,64,1024]{3,2,1,0:T(8,128)(2,1)S(1)}, bf16[2,2,64,1024]{3,2,1,0:T(8,128)(2,1)S(1)}, u32[]{:S(2)}, u32[]{:S(2)}) collective-permute-start(bf16[2,2,64,1024]{3,2,1,0:T(8,128)(2,1)S(1)} %collective-permute-done.11.t1), channel_id=1, source_target_pairs={{0,32},{1,33},{2,34},{3,35},{4,36},{5,37},{6,38},{7,39},{8,40},{9,... | collective-permute-start | bytes 1572872 | tf_op jit(solution)/shard_map/ppermute | solution.py:30
  27.1 10.1 %collective-permute-start.13 = (bf16[2,2,64,1024]{3,2,1,0:T(8,128)(2,1)S(1)}, bf16[2,2,64,1024]{3,2,1,0:T(8,128)(2,1)S(1)}, u32[]{:S(2)}, u32[]{:S(2)}) collective-permute-start(bf16[2,2,64,1024]{3,2,1,0:T(8,128)(2,1)S(1)} %collective-permute-done.12.t2), channel_id=1, source_target_pairs={{0,32},{1,33},{2,34},{3,35},{4,36},{5,37},{6,38},{7,39},{8,40},{9,... | collective-permute-start | bytes 1572872 | tf_op jit(solution)/shard_map/ppermute | solution.py:30
  30.8 10.0 %collective-permute-start.7 = (bf16[2,2,64,1024]{3,2,1,0:T(8,128)(2,1)S(1)}, bf16[2,2,64,1024]{3,2,1,0:T(8,128)(2,1)S(1)}, u32[]{:S(2)}, u32[]{:S(2)}) collective-permute-start(bf16[2,2,64,1024]{3,2,1,0:T(8,128)(2,1)S(1)} %slice.226), channel_id=1, source_target_pairs={{0,12},{1,13},{2,14},{3,15},{4,0},{5,1},{6,2},{7,3},{8,4},{9,5},{1... | collective-permute-start | bytes 1572872 | tf_op jit(solution)/shard_map/ppermute | solution.py:30
  31.0 14.3 %collective-permute-start.8 = (bf16[4,64,1024]{2,1,0:T(8,128)(2,1)S(1)}, bf16[4,64,1024]{2,1,0:T(8,128)(2,1)S(1)}, u32[]{:S(2)}, u32[]{:S(2)}) collective-permute-start(bf16[4,64,1024]{2,1,0:T(8,128)(2,1)S(1)} %slice_bitcast_fusion), channel_id=1, source_target_pairs={{0,16},{1,17},{2,18},{3,19},{4,20},{5,21},{6,22},{7,23},{8,24},{9,... | collective-permute-start | bytes 1572872 | tf_op jit(solution)/shard_map/ppermute | solution.py:30
  35.5 17.7 %collective-permute-start.15 = (bf16[2,2,64,1024]{3,2,1,0:T(8,128)(2,1)S(1)}, bf16[2,2,64,1024]{3,2,1,0:T(8,128)(2,1)S(1)}, u32[]{:S(2)}, u32[]{:S(2)}) collective-permute-start(bf16[2,2,64,1024]{3,2,1,0:T(8,128)(2,1)S(1)} %collective-permute-done.11.t1), channel_id=1, source_target_pairs={{0,16},{1,17},{2,18},{3,19},{4,20},{5,21},{6,22},{7,23},{8,24},{9,... | collective-permute-start | bytes 1572872 | tf_op jit(solution)/shard_map/ppermute | solution.py:30
  35.7 8.4 %collective-permute-start.6 = (bf16[2,2,64,1024]{3,2,0,1:T(8,128)(2,1)S(1)}, bf16[2,2,64,1024]{3,2,0,1:T(8,128)(2,1)S(1)}, u32[]{:S(2)}, u32[]{:S(2)}) collective-permute-start(bf16[2,2,64,1024]{3,2,0,1:T(8,128)(2,1)S(1)} %slice.225), channel_id=1, source_target_pairs={{0,4},{1,5},{2,6},{3,7},{4,8},{5,9},{6,10},{7,11},{8,12},{9,13},{1... | collective-permute-start | bytes 1572872 | tf_op jit(solution)/shard_map/ppermute | solution.py:30
  37.2 15.7 %collective-permute-start.9 = (bf16[2,4,64,1024]{3,2,0,1:T(8,128)(2,1)S(1)}, bf16[2,4,64,1024]{3,2,0,1:T(8,128)(2,1)S(1)}, u32[]{:S(2)}, u32[]{:S(2)}) collective-permute-start(bf16[2,4,64,1024]{3,2,0,1:T(8,128)(2,1)S(1)} %pad_maximum_fusion.1), channel_id=1, source_target_pairs={{0,16},{1,17},{2,18},{3,19},{4,20},{5,21},{6,22},{7,23},{8,24},{9,... | collective-permute-start | bytes 3145736 | tf_op jit(solution)/shard_map/ppermute | solution.py:30
  40.8 12.5 %collective-permute-start.16 = (bf16[2,2,64,1024]{3,2,1,0:T(8,128)(2,1)S(1)}, bf16[2,2,64,1024]{3,2,1,0:T(8,128)(2,1)S(1)}, u32[]{:S(2)}, u32[]{:S(2)}) collective-permute-start(bf16[2,2,64,1024]{3,2,1,0:T(8,128)(2,1)S(1)} %collective-permute-done.12.t2), channel_id=1, source_target_pairs={{0,16},{1,17},{2,18},{3,19},{4,20},{5,21},{6,22},{7,23},{8,24},{9,... | collective-permute-start | bytes 1572872 | tf_op jit(solution)/shard_map/ppermute | solution.py:30
  44.1 5.7 %collective-permute-start.14 = (bf16[2,64,1024]{2,1,0:T(8,128)(2,1)S(1)}, bf16[2,64,1024]{2,1,0:T(8,128)(2,1)S(1)}, u32[]{:S(2)}, u32[]{:S(2)}) collective-permute-start(bf16[2,64,1024]{2,1,0:T(8,128)(2,1)S(1)} %slice_bitcast_fusion.1), channel_id=1, source_target_pairs={{0,32},{1,33},{2,34},{3,35},{4,36},{5,37},{6,38},{7,39},{8,40},{9,... | collective-permute-start | bytes 786440 | tf_op jit(solution)/shard_map/ppermute | solution.py:30
  45.3 9.5 %collective-permute-start.17 = (bf16[2,2,64,1024]{3,2,1,0:T(8,128)(2,1)S(1)}, bf16[2,2,64,1024]{3,2,1,0:T(8,128)(2,1)S(1)}, u32[]{:S(2)}, u32[]{:S(2)}) collective-permute-start(bf16[2,2,64,1024]{3,2,1,0:T(8,128)(2,1)S(1)} %collective-permute-done.13.t3), channel_id=1, source_target_pairs={{0,16},{1,17},{2,18},{3,19},{4,20},{5,21},{6,22},{7,23},{8,24},{9,... | collective-permute-start | bytes 1572872 | tf_op jit(solution)/shard_map/ppermute | solution.py:30
  49.8 5.0 %collective-permute-start.10 = (bf16[4,64,1024]{2,1,0:T(8,128)(2,1)S(1)}, bf16[4,64,1024]{2,1,0:T(8,128)(2,1)S(1)}, u32[]{:S(2)}, u32[]{:S(2)}) collective-permute-start(bf16[4,64,1024]{2,1,0:T(8,128)(2,1)S(1)} %pad_maximum_fusion.2), channel_id=1, source_target_pairs={{0,16},{1,17},{2,18},{3,19},{4,20},{5,21},{6,22},{7,23},{8,24},{9,... | collective-permute-start | bytes 1572872 | tf_op jit(solution)/shard_map/ppermute | solution.py:30
  52.9 1.9 %collective-permute-start.18 = (bf16[2,64,1024]{2,1,0:T(8,128)(2,1)S(1)}, bf16[2,64,1024]{2,1,0:T(8,128)(2,1)S(1)}, u32[]{:S(2)}, u32[]{:S(2)}) collective-permute-start(bf16[2,64,1024]{2,1,0:T(8,128)(2,1)S(1)} %collective-permute-done.14.far), channel_id=1, source_target_pairs={{0,16},{1,17},{2,18},{3,19},{4,20},{5,21},{6,22},{7,23},{8,24},{9,... | collective-permute-start | bytes 786440 | tf_op jit(solution)/shard_map/ppermute | solution.py:30
  66.1 3.7 %collective-permute-start.25 = (f32[8,1024]{1,0:T(8,128)S(1)}, f32[8,1024]{1,0:T(8,128)S(1)}, u32[]{:S(2)}, u32[]{:S(2)}) collective-permute-start(f32[8,1024]{1,0:T(8,128)S(1)} %get-tuple-element.37), channel_id=1, source_target_pairs={{0,16},{1,17},{2,18},{3,19},{4,20},{5,21},{6,22},{7,23},{8,24},{9,... | collective-permute-start | bytes 98312 | tf_op jit(solution)/shard_map/ppermute | solution.py:30
  66.6 9.2 %collective-permute-start.21 = (f32[8,1024]{1,0:T(8,128)S(1)}, f32[8,1024]{1,0:T(8,128)S(1)}, u32[]{:S(2)}, u32[]{:S(2)}) collective-permute-start(f32[8,1024]{1,0:T(8,128)S(1)} %get-tuple-element.36), channel_id=1, source_target_pairs={{0,3},{1,2},{2,1},{3,0},{4,7},{5,6},{6,5},{7,4},{8,11},{9,10},{10,... | collective-permute-start | bytes 98312 | tf_op jit(solution)/shard_map/ppermute | solution.py:30
  67.8 8.2 %collective-permute-start.20 = (f32[8,1024]{1,0:T(8,128)S(1)}, f32[8,1024]{1,0:T(8,128)S(1)}, u32[]{:S(2)}, u32[]{:S(2)}) collective-permute-start(f32[8,1024]{1,0:T(8,128)S(1)} %get-tuple-element.36), channel_id=1, source_target_pairs={{0,2},{1,3},{2,0},{3,1},{4,6},{5,7},{6,4},{7,5},{8,10},{9,11},{10,... | collective-permute-start | bytes 98312 | tf_op jit(solution)/shard_map/ppermute | solution.py:30
  68.9 7.1 %collective-permute-start.19 = (f32[8,1024]{1,0:T(8,128)S(1)}, f32[8,1024]{1,0:T(8,128)S(1)}, u32[]{:S(2)}, u32[]{:S(2)}) collective-permute-start(f32[8,1024]{1,0:T(8,128)S(1)} %get-tuple-element.36), channel_id=1, source_target_pairs={{0,1},{1,0},{2,3},{3,2},{4,5},{5,4},{6,7},{7,6},{8,9},{9,8},{10,11... | collective-permute-start | bytes 98312 | tf_op jit(solution)/shard_map/ppermute | solution.py:30
  70.0 6.6 %collective-permute-start.28 = (f32[5,1024]{1,0:T(8,128)S(1)}, f32[5,1024]{1,0:T(8,128)S(1)}, u32[]{:S(2)}, u32[]{:S(2)}) collective-permute-start(f32[5,1024]{1,0:T(8,128)S(1)} %concatenate.14), channel_id=1, source_target_pairs={{0,96},{1,97},{2,98},{3,99},{4,100},{5,101},{6,102},{7,103},{8,104... | collective-permute-start | bytes 61448 | tf_op jit(solution)/shard_map/ppermute | solution.py:30
  72.9 6.6 %collective-permute-start.27 = (f32[5,1024]{1,0:T(8,128)S(1)}, f32[5,1024]{1,0:T(8,128)S(1)}, u32[]{:S(2)}, u32[]{:S(2)}) collective-permute-start(f32[5,1024]{1,0:T(8,128)S(1)} %concatenate.14), channel_id=1, source_target_pairs={{0,64},{1,65},{2,66},{3,67},{4,68},{5,69},{6,70},{7,71},{8,72},{9,... | collective-permute-start | bytes 61448 | tf_op jit(solution)/shard_map/ppermute | solution.py:30
  75.8 3.8 %collective-permute-start.26 = (f32[5,1024]{1,0:T(8,128)S(1)}, f32[5,1024]{1,0:T(8,128)S(1)}, u32[]{:S(2)}, u32[]{:S(2)}) collective-permute-start(f32[5,1024]{1,0:T(8,128)S(1)} %concatenate.14), channel_id=1, source_target_pairs={{0,32},{1,33},{2,34},{3,35},{4,36},{5,37},{6,38},{7,39},{8,40},{9,... | collective-permute-start | bytes 61448 | tf_op jit(solution)/shard_map/ppermute | solution.py:30
  76.2 7.9 %collective-permute-start.24 = (f32[5,1024]{1,0:T(8,128)S(1)}, f32[5,1024]{1,0:T(8,128)S(1)}, u32[]{:S(2)}, u32[]{:S(2)}) collective-permute-start(f32[5,1024]{1,0:T(8,128)S(1)} %concatenate.13.ra), channel_id=1, source_target_pairs={{0,12},{1,13},{2,14},{3,15},{4,8},{5,9},{6,10},{7,11},{8,4},{9,5},... | collective-permute-start | bytes 61448 | tf_op jit(solution)/shard_map/ppermute | solution.py:30
  76.3 7.8 %collective-permute-start.23 = (f32[5,1024]{1,0:T(8,128)S(1)}, f32[5,1024]{1,0:T(8,128)S(1)}, u32[]{:S(2)}, u32[]{:S(2)}) collective-permute-start(f32[5,1024]{1,0:T(8,128)S(1)} %concatenate.13.ra), channel_id=1, source_target_pairs={{0,8},{1,9},{2,10},{3,11},{4,12},{5,13},{6,14},{7,15},{8,0},{9,1},... | collective-permute-start | bytes 61448 | tf_op jit(solution)/shard_map/ppermute | solution.py:30
  76.6 7.5 %collective-permute-start.22 = (f32[5,1024]{1,0:T(8,128)S(1)}, f32[5,1024]{1,0:T(8,128)S(1)}, u32[]{:S(2)}, u32[]{:S(2)}) collective-permute-start(f32[5,1024]{1,0:T(8,128)S(1)} %concatenate.13.ra), channel_id=1, source_target_pairs={{0,4},{1,5},{2,6},{3,7},{4,0},{5,1},{6,2},{7,3},{8,12},{9,13},{10,... | collective-permute-start | bytes 61448 | tf_op jit(solution)/shard_map/ppermute | solution.py:30
  79.7 7.0 %collective-permute-start.29 = (f32[5,1024]{1,0:T(8,128)S(1)}, f32[5,1024]{1,0:T(8,128)S(1)}, u32[]{:S(2)}, u32[]{:S(2)}) collective-permute-start(f32[5,1024]{1,0:T(8,128)S(1)} %concatenate.15.ca), channel_id=1, source_target_pairs={{0,128},{1,129},{2,130},{3,131},{4,132},{5,133},{6,134},{7,135},{8... | collective-permute-start | bytes 61448 | tf_op jit(solution)/shard_map/ppermute | solution.py:30
  100.8 7.8 %collective-permute-start.30 = (bf16[33,64,512]{2,1,0:T(8,128)(2,1)}, bf16[33,64,512]{2,1,0:T(8,128)(2,1)S(1)}, u32[]{:S(2)}, u32[]{:S(2)}) collective-permute-start(bf16[33,64,512]{2,1,0:T(8,128)(2,1)} %get-tuple-element.40), channel_id=1, source_target_pairs={{0,16},{1,17},{2,18},{3,19},{4,20},{5,21},{6,22},{7,23},{8,24},{9,... | collective-permute-start | bytes 6488072 | tf_op jit(solution)/shard_map/ppermute | solution.py:30
  108.6 1.6 %copy-start = (f32[8,64,1024]{2,1,0:T(8,128)S(1)}, f32[8,64,1024]{2,1,0:T(8,128)}, u32[]{:S(2)}) copy-start(f32[8,64,1024]{2,1,0:T(8,128)} %get-tuple-element.38.keep_text) | copy-start | bytes 6291460
  110.6 12.6 %collective-permute-start.31 = (bf16[208,1024]{1,0:T(8,128)(2,1)S(1)}, bf16[208,1024]{1,0:T(8,128)(2,1)S(1)}, u32[]{:S(2)}, u32[]{:S(2)}) collective-permute-start(bf16[208,1024]{1,0:T(8,128)(2,1)S(1)} %get-tuple-element.45), channel_id=1, source_target_pairs={{0,64},{1,65},{2,66},{3,67},{4,68},{5,69},{6,70},{7,71},{8,72},{9,... | collective-permute-start | bytes 1277960 | tf_op jit(solution)/shard_map/ppermute | solution.py:30
  113.5 15.5 %collective-permute-start.34 = (bf16[528,512]{1,0:T(8,128)(2,1)S(1)}, bf16[528,512]{1,0:T(8,128)(2,1)S(1)}, u32[]{:S(2)}, u32[]{:S(2)}) collective-permute-start(bf16[528,512]{1,0:T(8,128)(2,1)S(1)} %get-tuple-element.50), channel_id=1, source_target_pairs={{0,1},{1,2},{2,3},{3,0},{4,5},{5,6},{6,7},{7,4},{8,9},{9,10},{10,1... | collective-permute-start | bytes 1622024 | tf_op jit(solution)/shard_map/ppermute | solution.py:30
  113.6 15.5 %collective-permute-start.35 = (bf16[528,512]{1,0:T(8,128)(2,1)S(1)}, bf16[528,512]{1,0:T(8,128)(2,1)S(1)}, u32[]{:S(2)}, u32[]{:S(2)}) collective-permute-start(bf16[528,512]{1,0:T(8,128)(2,1)S(1)} %get-tuple-element.51), channel_id=1, source_target_pairs={{0,3},{1,0},{2,1},{3,2},{4,7},{5,4},{6,5},{7,6},{8,11},{9,8},{10,9... | collective-permute-start | bytes 1622024 | tf_op jit(solution)/shard_map/ppermute | solution.py:30
  116.2 12.8 %collective-permute-start.36 = (bf16[528,512]{1,0:T(8,128)(2,1)S(1)}, bf16[528,512]{1,0:T(8,128)(2,1)S(1)}, u32[]{:S(2)}, u32[]{:S(2)}) collective-permute-start(bf16[528,512]{1,0:T(8,128)(2,1)S(1)} %get-tuple-element.52), channel_id=1, source_target_pairs={{0,2},{1,3},{2,0},{3,1},{4,6},{5,7},{6,4},{7,5},{8,10},{9,11},{10,... | collective-permute-start | bytes 1622024 | tf_op jit(solution)/shard_map/ppermute | solution.py:30
  123.3 15.1 %collective-permute-start.32 = (bf16[144,1024]{1,0:T(8,128)(2,1)S(1)}, bf16[144,1024]{1,0:T(8,128)(2,1)S(1)}, u32[]{:S(2)}, u32[]{:S(2)}) collective-permute-start(bf16[144,1024]{1,0:T(8,128)(2,1)S(1)} %get-tuple-element.47), channel_id=1, source_target_pairs={{0,32},{1,33},{2,34},{3,35},{4,36},{5,37},{6,38},{7,39},{8,40},{9,... | collective-permute-start | bytes 884744 | tf_op jit(solution)/shard_map/ppermute | solution.py:30
  125.1 13.3 %collective-permute-start.33 = (bf16[144,1024]{1,0:T(8,128)(2,1)S(1)}, bf16[144,1024]{1,0:T(8,128)(2,1)S(1)}, u32[]{:S(2)}, u32[]{:S(2)}) collective-permute-start(bf16[144,1024]{1,0:T(8,128)(2,1)S(1)} %get-tuple-element.48), channel_id=1, source_target_pairs={{0,64},{1,65},{2,66},{3,67},{4,68},{5,69},{6,70},{7,71},{8,72},{9,... | collective-permute-start | bytes 884744 | tf_op jit(solution)/shard_map/ppermute | solution.py:30
  129.3 5.4 %collective-permute-start.37 = (bf16[144,512]{1,0:T(8,128)(2,1)S(1)}, bf16[144,512]{1,0:T(8,128)(2,1)S(1)}, u32[]{:S(2)}, u32[]{:S(2)}) collective-permute-start(bf16[144,512]{1,0:T(8,128)(2,1)S(1)} %get-tuple-element.54), channel_id=1, source_target_pairs={{0,4},{1,5},{2,6},{3,7},{4,8},{5,9},{6,10},{7,11},{8,12},{9,13},{1... | collective-permute-start | bytes 442376 | tf_op jit(solution)/shard_map/ppermute | solution.py:30
  131.0 5.8 %collective-permute-start.38 = (bf16[144,512]{1,0:T(8,128)(2,1)S(1)}, bf16[144,512]{1,0:T(8,128)(2,1)S(1)}, u32[]{:S(2)}, u32[]{:S(2)}) collective-permute-start(bf16[144,512]{1,0:T(8,128)(2,1)S(1)} %get-tuple-element.55), channel_id=1, source_target_pairs={{0,8},{1,9},{2,10},{3,11},{4,12},{5,13},{6,14},{7,15},{8,0},{9,1},... | collective-permute-start | bytes 442376 | tf_op jit(solution)/shard_map/ppermute | solution.py:30
  131.8 6.6 %collective-permute-start.39 = (bf16[144,512]{1,0:T(8,128)(2,1)S(1)}, bf16[144,512]{1,0:T(8,128)(2,1)S(1)}, u32[]{:S(2)}, u32[]{:S(2)}) collective-permute-start(bf16[144,512]{1,0:T(8,128)(2,1)S(1)} %get-tuple-element.56), channel_id=1, source_target_pairs={{0,12},{1,13},{2,14},{3,15},{4,0},{5,1},{6,2},{7,3},{8,4},{9,5},{1... | collective-permute-start | bytes 442376 | tf_op jit(solution)/shard_map/ppermute | solution.py:30
  138.6 3.2 %collective-permute-start.40 = (bf16[80,1536]{1,0:T(8,128)(2,1)S(1)}, bf16[80,1536]{1,0:T(8,128)(2,1)S(1)}, u32[]{:S(2)}, u32[]{:S(2)}) collective-permute-start(bf16[80,1536]{1,0:T(8,128)(2,1)S(1)} %get-tuple-element.60), channel_id=1, source_target_pairs={{0,16},{1,17},{2,18},{3,19},{4,20},{5,21},{6,22},{7,23},{8,24},{9,... | collective-permute-start | bytes 737288 | tf_op jit(solution)/shard_map/ppermute | solution.py:30

commit v2 on v1

--- a/solution.py
+++ b/solution.py
@@ -1,3 +1,5 @@
+import functools
+
 import jax
 import jax.numpy as jnp
 from jax import lax
@@ -12,7 +14,7 @@
 LANES = 128
 VMEM_BYTES = 16 << 20
 PASS_1_BYTES = 40 << 20
-PASS_2_BYTES = 52 << 20
+PASS_2_BYTES = 48 << 20
 
 
 def place(z, c, y, x):
@@ -60,10 +62,9 @@
     down = move_second(line, -1)
     far_a = move_second(up[:, :2], 1)
     far_b = move_second(down[:, 2:], -1)
-    got_0 = swap(line[1], c_bits=1)
-    got_1 = swap(jnp.stack([down[1], up[1]]), c_bits=1)
+    got_1 = swap(jnp.stack([line[1], down[1], up[1]]), c_bits=1)
     got_2 = swap(jnp.concatenate([far_a[1], far_b[1]]), c_bits=1)
-    return line, up, down, far_a, far_b, got_0, got_1, got_2
+    return line, up, down, far_a, far_b, got_1, got_2
 
 
 def gather_cols(v):
@@ -71,13 +72,13 @@
     for _ in range(3):
         out.append(move_z(out[-1], 1))
     far = move_z(out[3][0], 1)
-    back = [swap(b, c_bits=1) for b in out[1:]]
-    return out + [far] + back + [swap(far, c_bits=1)]
+    back = swap(jnp.stack(out[1:3]), c_bits=1)
+    return out + [far, back, swap(out[3], c_bits=1), swap(far, c_bits=1)]
 
 
 def pass_1_kernel(
-    line, up, down, far_a, far_b, got_0, got_1, got_2,
-    t0, t1, t2, t3, far, b1, b2, b3, far_sib,
+    line, up, down, far_a, far_b, got_1, got_2,
+    t0, t1, t2, t3, far, back, b3, far_sib,
     both_out, student, row_st, col_st,
     teach, learn, rows, cols, tops, wide, sums, sem,
 ):
@@ -102,7 +103,7 @@
             else:
                 src = ({0: line, 1: down, 3: up}[k], (0, f))
             pieces.append((src, (rows, c, row_place(k, f))))
-            src = {0: (got_0, k), 1: (got_1, (0, k)), 2: (got_2, k), 3: (got_1, (1, k))}[f]
+            src = {0: (got_1, (0, k)), 1: (got_1, (1, k)), 2: (got_2, k), 3: (got_1, (2, k))}[f]
             pieces.append((src, (rows, 1 - c, row_place(k, f))))
     way = 2 * c - 1
     for kind in range(2):
@@ -110,10 +111,11 @@
             for dc in range(2):
                 core = c if dc == 0 else 1 - c
                 pieces.append(((ref, (dc, kind)), (cols, kind, col_place(way * j, core))))
-        for j, ref in enumerate((b1, b2, b3)):
+        for j in range(3):
             for dc in range(2):
                 core = 1 - c if dc == 0 else c
-                pieces.append(((ref, (dc, kind)), (cols, kind, col_place(-way * (j + 1), core))))
+                src = (back, (j, dc, kind)) if j < 2 else (b3, (dc, kind))
+                pieces.append((src, (cols, kind, col_place(-way * (j + 1), core))))
         pieces.append(((far, kind), (cols, kind, col_place(4, c))))
         pieces.append(((far_sib, kind), (cols, kind, col_place(4, 1 - c))))
     for (src, i), (dst, j, k) in pieces:
@@ -265,8 +267,8 @@
             enter.append(pltpu.make_async_copy(both_in.at[k, part], dst.at[part], sem.at[len(enter)]))
     enter.append(pltpu.make_async_copy(student_in.at[0], rows, sem.at[8]))
     enter.append(pltpu.make_async_copy(student_in.at[1], cols, sem.at[9]))
-    for copy in enter:
-        copy.start()
+    for i in (0, 1, 9, 2, 3, 4, 5, 6, 7, 8):
+        enter[i].start()
     row_st = merge([r[...] for r in (ra, rb, rc, rd)])
     col_st = merge([r[...] for r in (ca, cb)])
     row_t, row_s = row_st[0] + jnp.log(row_st[1]), row_st[2] + jnp.log(row_st[3])
@@ -285,6 +287,8 @@
         wide[k] = jnp.broadcast_to(v, (LANES, size)).T
 
     span = 4
+    mine = pl.ds(pl.multiple_of(c * half, half), half)
+    other = pl.ds(pl.multiple_of((1 - c) * half, half), half)
 
     def chunk_step(r, carry):
         part = pl.ds(pl.multiple_of(r * chunk, chunk), chunk)
@@ -305,11 +309,27 @@
                 return inner
 
             lax.fori_loop(r * (chunk // 16), (r + 1) * (chunk // 16), step, 0)
+
+        @pl.when(r == 0)
+        def _():
+            enter[9].wait()
+
+        product[:chunk, :] = 100.0 * jnp.dot(
+            coupling[part, :], cols[...].reshape(size, d), preferred_element_type=F32
+        )
+        for i in range(chunk // n):
+            at = r * (chunk // n) + i
+            dy = lax.rem(lax.div(at, NX) + NY - y, NY)
+            dx = lax.rem(lax.rem(at, NX) + NX - x, NX)
+            k = dy * (1 - c) + dx * c
+            f = dx * (1 - c) + dy * c
+            block = slice(i * n, (i + 1) * n)
+            keep_image[f * 4 + k] = product[block, mine].astype(BF)
+            give[k * 4 + f] = product[block, other].astype(BF)
         return carry
 
     lax.fori_loop(0, 4, chunk_step, 0)
     enter[8].wait()
-    enter[9].wait()
 
     def text_step(i, carry):
         part = pl.ds(pl.multiple_of(i * chunk, chunk), chunk)
@@ -341,25 +361,6 @@
         for core in range(2):
             put(2 * k + core, text_block(-out * k, core))
             keep_text[2 * k + core] = text_block(out * k, core)
-
-    def image_step(i, carry):
-        lanes = pl.ds(pl.multiple_of(i * (d // 4), d // 4), d // 4)
-        product[:, lanes] = 100.0 * jnp.dot(
-            coupling[...], cols[:, :, lanes].reshape(size, d // 4), preferred_element_type=F32
-        )
-        return carry
-
-    lax.fori_loop(0, 4, image_step, 0)
-    mine = pl.ds(pl.multiple_of(c * half, half), half)
-    other = pl.ds(pl.multiple_of((1 - c) * half, half), half)
-    for k in range(4):
-        for f in range(4):
-            dy = k * (1 - c) + f * c
-            dx = f * (1 - c) + k * c
-            at = lax.rem(y + dy, NY) * NX + lax.rem(x + dx, NX)
-            part = pl.ds(pl.multiple_of(at * n, n), n)
-            keep_image[f * 4 + k] = product[part, mine].astype(BF)
-            give[k * 4 + f] = product[part, other].astype(BF)
 
 
 def pass_2(args, n, d):
@@ -520,7 +521,7 @@
     loss[1] = jnp.broadcast_to(cols, (8, LANES))
 
 
-def end_kernel(text, image, share, loss, text_grad, image_grad, total):
+def end_kernel(scale, text, image, share, loss, text_grad, image_grad, total):
     _, c, _, _ = position()
     n, d = text.shape
     h = d // 2
@@ -530,7 +531,7 @@
     image_grad[:, h:] = choose(c, other, mine).astype(BF)
     rows = loss[0, :1] + unpack(share, n, 0)
     cols = choose(c, loss[1, :1], unpack(share, n, 3 * LANES))
-    total[...] = jnp.broadcast_to(jnp.sum(rows, axis=1, keepdims=True) + cols, (8, LANES))
+    total[0] = (jnp.sum(rows) + jnp.max(cols)) * scale
 
 
 def reduce_all(give, keep_image, keep_text, loss_part):
@@ -568,34 +569,37 @@
         [((n, d), F32), ((n, h), BF), ((n + 16, d + h), BF), ((2, 8, LANES), F32)],
         (text_own, b1, b2, k34, rows_loss, line, w1, w2, w3, cols_loss),
     )
-    return vmem_call(
-        end_kernel,
-        [((n, d), BF), ((n, d), BF), small],
-        (text, image, swap(share, c_bits=1), loss),
-    )
+    vmem = pl.BlockSpec(memory_space=pltpu.VMEM)
+    scale = 0.5 / (n * NX * NY * NZ * NC)
+    return pl.pallas_call(
+        functools.partial(end_kernel, scale),
+        out_shape=(
+            jax.ShapeDtypeStruct((n, d), BF),
+            jax.ShapeDtypeStruct((n, d), BF),
+            jax.ShapeDtypeStruct((1,), F32),
+        ),
+        in_specs=[vmem] * 4,
+        out_specs=(vmem, vmem, pl.BlockSpec(memory_space=pltpu.SMEM)),
+        compiler_params=pltpu.CompilerParams(vmem_limit_bytes=VMEM_BYTES),
+    )(text, image, swap(share, c_bits=1), loss)
 
 
 def merge_steps(row_st, col_st):
     row_st = merged([row_st] + [swap(row_st, x_bits=b) for b in (1, 2, 3)])
-    col_st = merged([col_st, swap(col_st, c_bits=1)])
     col_st = merged([col_st] + [swap(col_st, z_bits=b) for b in (1, 2, 3)])
-    return [row_st] + [swap(row_st, y_bits=b) for b in (1, 2, 3)] + [
-        col_st,
-        swap(col_st, z_bits=4),
-    ]
+    row_parts = [row_st] + [swap(row_st, y_bits=b) for b in (1, 2, 3)]
+    col_st = merged([col_st, swap(col_st, z_bits=4)])
+    return row_parts + [col_st, swap(col_st, c_bits=1)]
 
 
 def per_device(teacher_image, teacher_text, student_image, student_text):
     n, d = teacher_image.shape
-    total_pairs = n * NX * NY * NZ * NC
     core = lax.rem(lax.axis_index("row"), NC)
     keep = jnp.where(core == 0, teacher_image, student_image)
     give = jnp.where(core == 0, student_image, teacher_image)
-    shared = swap(jnp.stack([give, teacher_text, student_text]), c_bits=1)
-    text_blocks = gather_cols(
-        jnp.stack([jnp.stack([teacher_text, student_text]), shared[1:]])
-    )
-    image_blocks = gather_rows(jnp.stack([keep, shared[0]]))
+    got = swap(jnp.stack([give, teacher_text, student_text]), c_bits=1)
+    text_blocks = gather_cols(jnp.stack([jnp.stack([teacher_text, student_text]), got[1:]]))
+    image_blocks = gather_rows(jnp.stack([keep, got[0]]))
     both, student, row_st, col_st = pass_1(
         list(image_blocks) + list(text_blocks), n, d
     )
@@ -603,7 +607,7 @@
         [both, student] + merge_steps(row_st, col_st), n, d
     )
     text_grad, image_grad, loss = reduce_all(give, keep_image, keep_text, loss_part)
-    return (image_grad, text_grad, loss[0, 0] * (0.5 / total_pairs))
+    return (image_grad, text_grad, loss.reshape(()))
 
 
 def solution(mesh):

time: 148 us -> 135 us (0.912); the launches traced: 145 us -> 135 us
  waiting for transfers between devices: 39.9 us -> 35.2 us
  local copies, waits for them, and re-layouts: 2.84 us -> 0.69 us
  Pallas kernels: 27.1 us -> 25.4 us
  between operations: 2.68 us -> 1.08 us
    ppermute x41 -> x39, waiting for transfers between devices: 39.9 us -> 35.2 us  [send(): return lax.ppermute(v, ('row', 'col'), pairs)]
    pallas_call x1, Pallas kernels: 14.1 us -> 12.3 us  [pass_2(): pl.pallas_call(pass_2_kernel, out_shape=(jax.ShapeDtypeStruct((33, n, d /...]
    unnamed x2 -> x0, local copies, waits for them, and re-layouts: 1.59 us -> none
    another operation x5 -> x6, other arithmetic: 3.15 us -> 3.32 us  [the longest x2 1.04 us: per_device(): jnp.stack([jnp.stack([teacher_text, student_text]), got[1:]])]
    ppermute x41 -> x39, starting transfers between devices: 68.6 us -> 68.6 us  [send(): return lax.ppermute(v, ('row', 'col'), pairs)]
  transfers between devices with their start and end apart: 41 -> 39, of which waited for: 17 -> 19; matrix products, arithmetic and copies ran while one was open for 2% -> 2% of each run, Pallas kernels for 0% -> 0%
where the time goes in v2:
time: 135 us
  starting transfers between devices  68.6 us (51%)
  waiting for transfers between devices  35.2 us (26%)
  Pallas kernels  25.4 us (19%)
  other arithmetic  3.83 us (3%)
    ppermute x39, starting transfers between devices, send(): return lax.ppermute(v, ('row', 'col'), pairs)  68.6 us
    ppermute x39, waiting for transfers between devices, send(): return lax.ppermute(v, ('row', 'col'), pairs)  35.2 us
    pallas_call x1, Pallas kernels, pass_2(): pl.pallas_call(pass_2_kernel, out_shape=(jax.ShapeDtypeStruct((33, n, d /...  12.3 us
    pallas_call x1, Pallas kernels, pass_1(): pl.pallas_call(pass_1_kernel, out_shape=(both, blocks, small, small), in_...  11.3 us
  transfers between devices with their start and end apart: 39, of which 19 were waited for; matrix products, arithmetic and copies ran while one was open for 2% of the time, Pallas kernels for 0%

profile of v2, /device:TPU:39, one launch (start us, length us, event | category | flops | bytes accessed | tf_op | source)
XLA Modules:
  0.0 134.8 jit_solution(13979818172967517029)
XLA Ops:
  0.6 1.0 select_bitcast_fusion.1
  1.6 1.0 pad_maximum_fusion.5
  2.6 0.8 collective-permute-start
  3.4 1.0 maximum_bitcast_fusion
  4.8 3.0 %collective-permute-start.2 = (bf16[2,64,1024]{2,1,0:T(8,128)(2,1)S(1)}, bf16[2,64,1024]{2,1,0:T(8,128)(2,1)S(1)}, u32[]{:S(2)}, u32[]{:S(2)}) collective-permute-start(bf16[2,64,1024]{2,1,0:T(8,128)(2,1)S(1)} %get-tuple-element.74), channel_id=1, source_target_pairs={{0,2},{1,3},{2,0},{3,1},{4,6},{5,7},{6,4},{7,5},{8,10},{9,11},{10,... | collective-permute-start | bytes 786440 | tf_op jit(solution)/shard_map/ppermute | solution.py:32
  7.8 0.8 collective-permute-start.1
  8.6 0.7 collective-permute-start.3
  9.5 2.5 %collective-permute-done.2 = bf16[2,64,1024]{2,1,0:T(8,128)(2,1)S(1)} collective-permute-done((bf16[2,64,1024]{2,1,0:T(8,128)(2,1)S(1)}, bf16[2,64,1024]{2,1,0:T(8,128)(2,1)S(1)}, u32[]{:S(2)}, u32[]{:S(2)}) %collective-permute-start.2) | collective-permute-done | bytes 262176 | tf_op jit(solution)/shard_map/ppermute | solution.py:32
  11.9 3.2 %collective-permute-done.1 = bf16[2,64,1024]{2,1,0:T(8,128)(2,1)S(1)} collective-permute-done((bf16[2,64,1024]{2,1,0:T(8,128)(2,1)S(1)}, bf16[2,64,1024]{2,1,0:T(8,128)(2,1)S(1)}, u32[]{:S(2)}, u32[]{:S(2)}) %collective-permute-start.1) | collective-permute-done | bytes 262176 | tf_op jit(solution)/shard_map/ppermute | solution.py:32
  16.0 2.3 %collective-permute-start.4 = (bf16[2,4,64,1024]{3,2,0,1:T(8,128)(2,1)S(1)}, bf16[2,4,64,1024]{3,2,0,1:T(8,128)(2,1)S(1)}, u32[]{:S(2)}, u32[]{:S(2)}) collective-permute-start(bf16[2,4,64,1024]{3,2,0,1:T(8,128)(2,1)S(1)} %pad_maximum_fusion.1), channel_id=1, source_target_pairs={{0,4},{1,5},{2,6},{3,7},{4,8},{5,9},{6,10},{7,11},{8,12},{9,13},{1... | collective-permute-start | bytes 3145736 | tf_op jit(solution)/shard_map/ppermute | solution.py:32
  18.3 2.7 %collective-permute-start.11 = (bf16[2,2,64,1024]{3,2,1,0:T(8,128)(2,1)S(1)}, bf16[2,2,64,1024]{3,2,1,0:T(8,128)(2,1)S(1)}, u32[]{:S(2)}, u32[]{:S(2)}) collective-permute-start(bf16[2,2,64,1024]{3,2,1,0:T(8,128)(2,1)S(1)} %collective-permute-done.10.t1), channel_id=1, source_target_pairs={{0,32},{1,33},{2,34},{3,35},{4,36},{5,37},{6,38},{7,39},{8,40},{9,... | collective-permute-start | bytes 1572872 | tf_op jit(solution)/shard_map/ppermute | solution.py:32
  21.0 6.1 %collective-permute-done.11.t2 = bf16[2,2,64,1024]{3,2,1,0:T(8,128)(2,1)S(1)} collective-permute-done((bf16[2,2,64,1024]{3,2,1,0:T(8,128)(2,1)S(1)}, bf16[2,2,64,1024]{3,2,1,0:T(8,128)(2,1)S(1)}, u32[]{:S(2)}, u32[]{:S(2)}) %collective-permute-start.11) | collective-permute-done | bytes 524320 | tf_op jit(solution)/shard_map/ppermute | solution.py:32
  27.1 3.1 %collective-permute-start.12 = (bf16[2,2,64,1024]{3,2,1,0:T(8,128)(2,1)S(1)}, bf16[2,2,64,1024]{3,2,1,0:T(8,128)(2,1)S(1)}, u32[]{:S(2)}, u32[]{:S(2)}) collective-permute-start(bf16[2,2,64,1024]{3,2,1,0:T(8,128)(2,1)S(1)} %collective-permute-done.11.t2), channel_id=1, source_target_pairs={{0,32},{1,33},{2,34},{3,35},{4,36},{5,37},{6,38},{7,39},{8,40},{9,... | collective-permute-start | bytes 1572872 | tf_op jit(solution)/shard_map/ppermute | solution.py:32
  30.2 0.6 collective-permute-done.5.down
  31.2 4.6 %collective-permute-start.8 = (bf16[3,4,64,1024]{3,2,0,1:T(8,128)(2,1)S(1)}, bf16[3,4,64,1024]{3,2,0,1:T(8,128)(2,1)S(1)}, u32[]{:S(2)}, u32[]{:S(2)}) collective-permute-start(bf16[3,4,64,1024]{3,2,0,1:T(8,128)(2,1)S(1)} %pad_maximum_fusion), channel_id=1, source_target_pairs={{0,16},{1,17},{2,18},{3,19},{4,20},{5,21},{6,22},{7,23},{8,24},{9,... | collective-permute-start | bytes 4718600 | tf_op jit(solution)/shard_map/ppermute | solution.py:32
  35.8 1.3 collective-permute-start.6
  37.4 2.5 %collective-permute-start.13 = (bf16[2,64,1024]{2,1,0:T(8,128)(2,1)S(1)}, bf16[2,64,1024]{2,1,0:T(8,128)(2,1)S(1)}, u32[]{:S(2)}, u32[]{:S(2)}) collective-permute-start(bf16[2,64,1024]{2,1,0:T(8,128)(2,1)S(1)} %slice_bitcast_fusion.1), channel_id=1, source_target_pairs={{0,32},{1,33},{2,34},{3,35},{4,36},{5,37},{6,38},{7,39},{8,40},{9,... | collective-permute-start | bytes 786440 | tf_op jit(solution)/shard_map/ppermute | solution.py:32
  39.9 0.6 collective-permute-done.7.far_b
  40.4 1.7 %collective-permute-start.15 = (bf16[2,2,64,1024]{3,2,1,0:T(8,128)(2,1)S(1)}, bf16[2,2,64,1024]{3,2,1,0:T(8,128)(2,1)S(1)}, u32[]{:S(2)}, u32[]{:S(2)}) collective-permute-start(bf16[2,2,64,1024]{3,2,1,0:T(8,128)(2,1)S(1)} %collective-permute-done.12.t3), channel_id=1, source_target_pairs={{0,16},{1,17},{2,18},{3,19},{4,20},{5,21},{6,22},{7,23},{8,24},{9,... | collective-permute-start | bytes 1572872 | tf_op jit(solution)/shard_map/ppermute | solution.py:32
  42.1 2.1 %collective-permute-done.6 = bf16[2,2,64,1024]{3,2,0,1:T(8,128)(2,1)S(1)} collective-permute-done((bf16[2,2,64,1024]{3,2,0,1:T(8,128)(2,1)S(1)}, bf16[2,2,64,1024]{3,2,0,1:T(8,128)(2,1)S(1)}, u32[]{:S(2)}, u32[]{:S(2)}) %collective-permute-start.6) | collective-permute-done | bytes 524320 | tf_op jit(solution)/shard_map/ppermute | solution.py:32
  44.3 2.2 %collective-permute-start.9 = (bf16[4,64,1024]{2,1,0:T(8,128)(2,1)S(1)}, bf16[4,64,1024]{2,1,0:T(8,128)(2,1)S(1)}, u32[]{:S(2)}, u32[]{:S(2)}) collective-permute-start(bf16[4,64,1024]{2,1,0:T(8,128)(2,1)S(1)} %pad_maximum_fusion.3), channel_id=1, source_target_pairs={{0,16},{1,17},{2,18},{3,19},{4,20},{5,21},{6,22},{7,23},{8,24},{9,... | collective-permute-start | bytes 1572872 | tf_op jit(solution)/shard_map/ppermute | solution.py:32
  46.4 2.0 %collective-permute-start.16 = (bf16[2,64,1024]{2,1,0:T(8,128)(2,1)S(1)}, bf16[2,64,1024]{2,1,0:T(8,128)(2,1)S(1)}, u32[]{:S(2)}, u32[]{:S(2)}) collective-permute-start(bf16[2,64,1024]{2,1,0:T(8,128)(2,1)S(1)} %collective-permute-done.13.far), channel_id=1, source_target_pairs={{0,16},{1,17},{2,18},{3,19},{4,20},{5,21},{6,22},{7,23},{8,24},{9,... | collective-permute-start | bytes 786440 | tf_op jit(solution)/shard_map/ppermute | solution.py:32
  48.7 0.9 collective-permute-done.16.far_sib
  49.6 11.3 %shard_map.67 = (f32[2,1024,1024]{2,1,0:T(8,128)}, bf16[2,16,64,1024]{3,2,1,0:T(8,128)(2,1)}, f32[8,1024]{1,0:T(8,128)S(1)}, f32[8,1024]{1,0:T(8,128)S(1)}) custom-call(bf16[2,4,64,1024]{3,2,1,0:T(8,128)(2,1)S(1)} %copy.9.line, bf16[2,4,64,1024]{3,2,1,0:T(8,128)(2,1)S(1)} %copy.10.up, bf16[2,4,64,1024]{3,2,1,0:T(8,128)(2,1)S(1)} %collective-permute-done.5.down, ...), custom_call_target="tpu_custom_call" | custom-call | flops 4294967296 | bytes 20971520 | tf_op jit(solution)/shard_map/pallas_call | solution.py:208
  61.4 4.6 %collective-permute-start.24 = (f32[8,1024]{1,0:T(8,128)S(1)}, f32[8,1024]{1,0:T(8,128)S(1)}, u32[]{:S(2)}, u32[]{:S(2)}) collective-permute-start(f32[8,1024]{1,0:T(8,128)S(1)} %get-tuple-element.37), channel_id=1, source_target_pairs={{0,64},{1,65},{2,66},{3,67},{4,68},{5,69},{6,70},{7,71},{8,72},{9,... | collective-permute-start | bytes 98312 | tf_op jit(solution)/shard_map/ppermute | solution.py:32
  66.1 0.6 collective-permute-start.19
  67.2 2.1 %collective-permute-start.17 = (f32[8,1024]{1,0:T(8,128)S(1)}, f32[8,1024]{1,0:T(8,128)S(1)}, u32[]{:S(2)}, u32[]{:S(2)}) collective-permute-start(f32[8,1024]{1,0:T(8,128)S(1)} %get-tuple-element.36), channel_id=1, source_target_pairs={{0,1},{1,0},{2,3},{3,2},{4,5},{5,4},{6,7},{7,6},{8,9},{9,8},{10,11... | collective-permute-start | bytes 98312 | tf_op jit(solution)/shard_map/ppermute | solution.py:32
  69.5 4.4 %collective-permute-start.26 = (f32[5,1024]{1,0:T(8,128)S(1)}, f32[5,1024]{1,0:T(8,128)S(1)}, u32[]{:S(2)}, u32[]{:S(2)}) collective-permute-start(f32[5,1024]{1,0:T(8,128)S(1)} %concatenate.14), channel_id=1, source_target_pairs={{0,128},{1,129},{2,130},{3,131},{4,132},{5,133},{6,134},{7,135},{8... | collective-permute-start | bytes 61448 | tf_op jit(solution)/shard_map/ppermute | solution.py:32
  74.1 2.8 %collective-permute-start.22 = (f32[5,1024]{1,0:T(8,128)S(1)}, f32[5,1024]{1,0:T(8,128)S(1)}, u32[]{:S(2)}, u32[]{:S(2)}) collective-permute-start(f32[5,1024]{1,0:T(8,128)S(1)} %concatenate.13.ra), channel_id=1, source_target_pairs={{0,12},{1,13},{2,14},{3,15},{4,8},{5,9},{6,10},{7,11},{8,4},{9,5},... | collective-permute-start | bytes 61448 | tf_op jit(solution)/shard_map/ppermute | solution.py:32
  77.7 3.0 %collective-permute-start.27 = (f32[5,1024]{1,0:T(8,128)S(1)}, f32[5,1024]{1,0:T(8,128)S(1)}, u32[]{:S(2)}, u32[]{:S(2)}) collective-permute-start(f32[5,1024]{1,0:T(8,128)S(1)} %concatenate.15.ca), channel_id=1, source_target_pairs={{0,16},{1,17},{2,18},{3,19},{4,20},{5,21},{6,22},{7,23},{8,24},{9,... | collective-permute-start | bytes 61448 | tf_op jit(solution)/shard_map/ppermute | solution.py:32
  81.6 12.3 %shard_map.68 = (bf16[33,64,512]{2,1,0:T(8,128)(2,1)S(1)}, bf16[16,64,512]{2,1,0:T(8,128)(2,1)S(1)}, f32[8,64,1024]{2,1,0:T(8,128)S(1)}, f32[2,8,128]{2,1,0:T(8,128)S(1)}) custom-call(f32[2,1024,1024]{2,1,0:T(8,128)} %get-tuple-element.34.both_in, bf16[2,16,64,1024]{3,2,1,0:T(8,128)(2,1)} %get-tuple-element.35.student_in, f32[5,1024]{1,0:T(8,128)S(1)} %concatenate.13.ra, ...), custom_call_target="tpu_custom_call" | custom-call | flops 4294967296 | bytes 20971520 | tf_op jit(solution)/shard_map/pallas_call | solution.py:369
  93.9 3.2 %collective-permute-start.28 = (bf16[33,64,512]{2,1,0:T(8,128)(2,1)S(1)}, bf16[33,64,512]{2,1,0:T(8,128)(2,1)S(1)}, u32[]{:S(2)}, u32[]{:S(2)}) collective-permute-start(bf16[33,64,512]{2,1,0:T(8,128)(2,1)S(1)} %get-tuple-element.40), channel_id=1, source_target_pairs={{0,16},{1,17},{2,18},{3,19},{4,20},{5,21},{6,22},{7,23},{8,24},{9,... | collective-permute-start | bytes 6488072 | tf_op jit(solution)/shard_map/ppermute | solution.py:32
  97.1 3.9 %collective-permute-done.28.got = bf16[33,64,512]{2,1,0:T(8,128)(2,1)S(1)} collective-permute-done((bf16[33,64,512]{2,1,0:T(8,128)(2,1)S(1)}, bf16[33,64,512]{2,1,0:T(8,128)(2,1)S(1)}, u32[]{:S(2)}, u32[]{:S(2)}) %collective-permute-start.28) | collective-permute-done | bytes 2162720 | tf_op jit(solution)/shard_map/ppermute | solution.py:32
  101.4 0.8 collective-permute-start.29
  102.2 2.7 %collective-permute-start.33 = (bf16[528,512]{1,0:T(8,128)(2,1)S(1)}, bf16[528,512]{1,0:T(8,128)(2,1)S(1)}, u32[]{:S(2)}, u32[]{:S(2)}) collective-permute-start(bf16[528,512]{1,0:T(8,128)(2,1)S(1)} %get-tuple-element.51), channel_id=1, source_target_pairs={{0,3},{1,0},{2,1},{3,2},{4,7},{5,4},{6,5},{7,6},{8,11},{9,8},{10,9... | collective-permute-start | bytes 1622024 | tf_op jit(solution)/shard_map/ppermute | solution.py:32
  105.3 4.7 %collective-permute-done.29.k34 = bf16[208,1024]{1,0:T(8,128)(2,1)S(1)} collective-permute-done((bf16[208,1024]{1,0:T(8,128)(2,1)S(1)}, bf16[208,1024]{1,0:T(8,128)(2,1)S(1)}, u32[]{:S(2)}, u32[]{:S(2)}) %collective-permute-start.29) | collective-permute-done | bytes 426016 | tf_op jit(solution)/shard_map/ppermute | solution.py:32
  110.2 5.4 %collective-permute-start.30 = (bf16[144,1024]{1,0:T(8,128)(2,1)S(1)}, bf16[144,1024]{1,0:T(8,128)(2,1)S(1)}, u32[]{:S(2)}, u32[]{:S(2)}) collective-permute-start(bf16[144,1024]{1,0:T(8,128)(2,1)S(1)} %get-tuple-element.47), channel_id=1, source_target_pairs={{0,32},{1,33},{2,34},{3,35},{4,36},{5,37},{6,38},{7,39},{8,40},{9,... | collective-permute-start | bytes 884744 | tf_op jit(solution)/shard_map/ppermute | solution.py:32
  115.6 1.5 %collective-permute-start.31 = (bf16[144,1024]{1,0:T(8,128)(2,1)S(1)}, bf16[144,1024]{1,0:T(8,128)(2,1)S(1)}, u32[]{:S(2)}, u32[]{:S(2)}) collective-permute-start(bf16[144,1024]{1,0:T(8,128)(2,1)S(1)} %get-tuple-element.48), channel_id=1, source_target_pairs={{0,64},{1,65},{2,66},{3,67},{4,68},{5,69},{6,70},{7,71},{8,72},{9,... | collective-permute-start | bytes 884744 | tf_op jit(solution)/shard_map/ppermute | solution.py:32
  117.1 0.6 collective-permute-done.32.p1
  118.0 1.4 %collective-permute-start.35 = (bf16[144,512]{1,0:T(8,128)(2,1)S(1)}, bf16[144,512]{1,0:T(8,128)(2,1)S(1)}, u32[]{:S(2)}, u32[]{:S(2)}) collective-permute-start(bf16[144,512]{1,0:T(8,128)(2,1)S(1)} %get-tuple-element.54), channel_id=1, source_target_pairs={{0,4},{1,5},{2,6},{3,7},{4,8},{5,9},{6,10},{7,11},{8,12},{9,13},{1... | collective-permute-start | bytes 442376 | tf_op jit(solution)/shard_map/ppermute | solution.py:32
  119.3 0.8 collective-permute-start.36
  120.2 2.1 %collective-permute-done.35.w1 = bf16[144,512]{1,0:T(8,128)(2,1)S(1)} collective-permute-done((bf16[144,512]{1,0:T(8,128)(2,1)S(1)}, bf16[144,512]{1,0:T(8,128)(2,1)S(1)}, u32[]{:S(2)}, u32[]{:S(2)}) %collective-permute-start.35) | collective-permute-done | bytes 147488 | tf_op jit(solution)/shard_map/ppermute | solution.py:32
  122.3 2.6 %collective-permute-done.36.w2 = bf16[144,512]{1,0:T(8,128)(2,1)S(1)} collective-permute-done((bf16[144,512]{1,0:T(8,128)(2,1)S(1)}, bf16[144,512]{1,0:T(8,128)(2,1)S(1)}, u32[]{:S(2)}, u32[]{:S(2)}) %collective-permute-start.36) | collective-permute-done | bytes 147488 | tf_op jit(solution)/shard_map/ppermute | solution.py:32
  124.9 1.8 %collective-permute-done.37.w3 = bf16[144,512]{1,0:T(8,128)(2,1)S(1)} collective-permute-done((bf16[144,512]{1,0:T(8,128)(2,1)S(1)}, bf16[144,512]{1,0:T(8,128)(2,1)S(1)}, u32[]{:S(2)}, u32[]{:S(2)}) %collective-permute-start.37) | collective-permute-done | bytes 147488 | tf_op jit(solution)/shard_map/ppermute | solution.py:32
  126.7 1.0 collective-permute-done.31.b2
  127.9 4.8 %collective-permute-start.38 = (bf16[80,1536]{1,0:T(8,128)(2,1)S(1)}, bf16[80,1536]{1,0:T(8,128)(2,1)S(1)}, u32[]{:S(2)}, u32[]{:S(2)}) collective-permute-start(bf16[80,1536]{1,0:T(8,128)(2,1)S(1)} %get-tuple-element.60), channel_id=1, source_target_pairs={{0,16},{1,17},{2,18},{3,19},{4,20},{5,21},{6,22},{7,23},{8,24},{9,... | collective-permute-start | bytes 737288 | tf_op jit(solution)/shard_map/ppermute | solution.py:32
  132.7 1.1 collective-permute-done.38.share
  133.8 0.8 shard_map.73
  (68 shorter events, 6.9 us)
Async XLA Ops:
  2.6 2.1 %collective-permute-start = (bf16[3,64,1024]{2,1,0:T(8,128)(2,1)S(1)}, bf16[3,64,1024]{2,1,0:T(8,128)(2,1)S(1)}, u32[]{:S(2)}, u32[]{:S(2)}) collective-permute-start(bf16[3,64,1024]{2,1,0:T(8,128)(2,1)S(1)} %pad_maximum_fusion.5), channel_id=1, source_target_pairs={{0,16},{1,17},{2,18},{3,19},{4,20},{5,21},{6,22},{7,23},{8,24},{9,... | collective-permute-start | bytes 1179656 | tf_op jit(solution)/shard_map/ppermute | solution.py:32
  4.8 7.1 %collective-permute-start.2 = (bf16[2,64,1024]{2,1,0:T(8,128)(2,1)S(1)}, bf16[2,64,1024]{2,1,0:T(8,128)(2,1)S(1)}, u32[]{:S(2)}, u32[]{:S(2)}) collective-permute-start(bf16[2,64,1024]{2,1,0:T(8,128)(2,1)S(1)} %get-tuple-element.74), channel_id=1, source_target_pairs={{0,2},{1,3},{2,0},{3,1},{4,6},{5,7},{6,4},{7,5},{8,10},{9,11},{10,... | collective-permute-start | bytes 786440 | tf_op jit(solution)/shard_map/ppermute | solution.py:32
  7.8 7.3 %collective-permute-start.1 = (bf16[2,64,1024]{2,1,0:T(8,128)(2,1)S(1)}, bf16[2,64,1024]{2,1,0:T(8,128)(2,1)S(1)}, u32[]{:S(2)}, u32[]{:S(2)}) collective-permute-start(bf16[2,64,1024]{2,1,0:T(8,128)(2,1)S(1)} %get-tuple-element.74), channel_id=1, source_target_pairs={{0,3},{1,0},{2,1},{3,2},{4,7},{5,4},{6,5},{7,6},{8,11},{9,8},{10,9... | collective-permute-start | bytes 786440 | tf_op jit(solution)/shard_map/ppermute | solution.py:32
  8.6 6.7 %collective-permute-start.3 = (bf16[2,64,1024]{2,1,0:T(8,128)(2,1)S(1)}, bf16[2,64,1024]{2,1,0:T(8,128)(2,1)S(1)}, u32[]{:S(2)}, u32[]{:S(2)}) collective-permute-start(bf16[2,64,1024]{2,1,0:T(8,128)(2,1)S(1)} %get-tuple-element.74), channel_id=1, source_target_pairs={{0,1},{1,2},{2,3},{3,0},{4,5},{5,6},{6,7},{7,4},{8,9},{9,10},{10,1... | collective-permute-start | bytes 786440 | tf_op jit(solution)/shard_map/ppermute | solution.py:32
  9.4 8.9 %collective-permute-start.10 = (bf16[2,2,64,1024]{3,2,1,0:T(8,128)(2,1)S(1)}, bf16[2,2,64,1024]{3,2,1,0:T(8,128)(2,1)S(1)}, u32[]{:S(2)}, u32[]{:S(2)}) collective-permute-start(bf16[2,2,64,1024]{3,2,1,0:T(8,128)(2,1)S(1)} %pad_maximum_fusion.4.t0), channel_id=1, source_target_pairs={{0,32},{1,33},{2,34},{3,35},{4,36},{5,37},{6,38},{7,39},{8,40},{9,... | collective-permute-start | bytes 1572872 | tf_op jit(solution)/shard_map/ppermute | solution.py:32
  15.5 15.2 %collective-permute-start.5 = (bf16[2,4,64,1024]{3,2,1,0:T(8,128)(2,1)S(1)}, bf16[2,4,64,1024]{3,2,1,0:T(8,128)(2,1)S(1)}, u32[]{:S(2)}, u32[]{:S(2)}) collective-permute-start(bf16[2,4,64,1024]{3,2,1,0:T(8,128)(2,1)S(1)} %copy.9.line), channel_id=1, source_target_pairs={{0,12},{1,13},{2,14},{3,15},{4,0},{5,1},{6,2},{7,3},{8,4},{9,5},{1... | collective-permute-start | bytes 3145736 | tf_op jit(solution)/shard_map/ppermute | solution.py:32
  16.0 14.9 %collective-permute-start.4 = (bf16[2,4,64,1024]{3,2,0,1:T(8,128)(2,1)S(1)}, bf16[2,4,64,1024]{3,2,0,1:T(8,128)(2,1)S(1)}, u32[]{:S(2)}, u32[]{:S(2)}) collective-permute-start(bf16[2,4,64,1024]{3,2,0,1:T(8,128)(2,1)S(1)} %pad_maximum_fusion.1), channel_id=1, source_target_pairs={{0,4},{1,5},{2,6},{3,7},{4,8},{5,9},{6,10},{7,11},{8,12},{9,13},{1... | collective-permute-start | bytes 3145736 | tf_op jit(solution)/shard_map/ppermute | solution.py:32
  18.3 8.8 %collective-permute-start.11 = (bf16[2,2,64,1024]{3,2,1,0:T(8,128)(2,1)S(1)}, bf16[2,2,64,1024]{3,2,1,0:T(8,128)(2,1)S(1)}, u32[]{:S(2)}, u32[]{:S(2)}) collective-permute-start(bf16[2,2,64,1024]{3,2,1,0:T(8,128)(2,1)S(1)} %collective-permute-done.10.t1), channel_id=1, source_target_pairs={{0,32},{1,33},{2,34},{3,35},{4,36},{5,37},{6,38},{7,39},{8,40},{9,... | collective-permute-start | bytes 1572872 | tf_op jit(solution)/shard_map/ppermute | solution.py:32
  27.1 10.2 %collective-permute-start.12 = (bf16[2,2,64,1024]{3,2,1,0:T(8,128)(2,1)S(1)}, bf16[2,2,64,1024]{3,2,1,0:T(8,128)(2,1)S(1)}, u32[]{:S(2)}, u32[]{:S(2)}) collective-permute-start(bf16[2,2,64,1024]{3,2,1,0:T(8,128)(2,1)S(1)} %collective-permute-done.11.t2), channel_id=1, source_target_pairs={{0,32},{1,33},{2,34},{3,35},{4,36},{5,37},{6,38},{7,39},{8,40},{9,... | collective-permute-start | bytes 1572872 | tf_op jit(solution)/shard_map/ppermute | solution.py:32
  30.8 9.6 %collective-permute-start.7 = (bf16[2,2,64,1024]{3,2,1,0:T(8,128)(2,1)S(1)}, bf16[2,2,64,1024]{3,2,1,0:T(8,128)(2,1)S(1)}, u32[]{:S(2)}, u32[]{:S(2)}) collective-permute-start(bf16[2,2,64,1024]{3,2,1,0:T(8,128)(2,1)S(1)} %slice.222), channel_id=1, source_target_pairs={{0,12},{1,13},{2,14},{3,15},{4,0},{5,1},{6,2},{7,3},{8,4},{9,5},{1... | collective-permute-start | bytes 1572872 | tf_op jit(solution)/shard_map/ppermute | solution.py:32
  31.2 17.4 %collective-permute-start.8 = (bf16[3,4,64,1024]{3,2,0,1:T(8,128)(2,1)S(1)}, bf16[3,4,64,1024]{3,2,0,1:T(8,128)(2,1)S(1)}, u32[]{:S(2)}, u32[]{:S(2)}) collective-permute-start(bf16[3,4,64,1024]{3,2,0,1:T(8,128)(2,1)S(1)} %pad_maximum_fusion), channel_id=1, source_target_pairs={{0,16},{1,17},{2,18},{3,19},{4,20},{5,21},{6,22},{7,23},{8,24},{9,... | collective-permute-start | bytes 4718600 | tf_op jit(solution)/shard_map/ppermute | solution.py:32
  35.8 8.4 %collective-permute-start.6 = (bf16[2,2,64,1024]{3,2,0,1:T(8,128)(2,1)S(1)}, bf16[2,2,64,1024]{3,2,0,1:T(8,128)(2,1)S(1)}, u32[]{:S(2)}, u32[]{:S(2)}) collective-permute-start(bf16[2,2,64,1024]{3,2,0,1:T(8,128)(2,1)S(1)} %slice.221), channel_id=1, source_target_pairs={{0,4},{1,5},{2,6},{3,7},{4,8},{5,9},{6,10},{7,11},{8,12},{9,13},{1... | collective-permute-start | bytes 1572872 | tf_op jit(solution)/shard_map/ppermute | solution.py:32
  37.2 12.4 %collective-permute-start.14 = (bf16[2,2,2,64,1024]{4,3,2,1,0:T(8,128)(2,1)S(1)}, bf16[2,2,2,64,1024]{4,3,2,1,0:T(8,128)(2,1)S(1)}, u32[]{:S(2)}, u32[]{:S(2)}) collective-permute-start(bf16[2,2,2,64,1024]{4,3,2,1,0:T(8,128)(2,1)S(1)} %pad_maximum_fusion.2), channel_id=1, source_target_pairs={{0,16},{1,17},{2,18},{3,19},{4,20},{5,21},{6,22},{7,23},{8,24},{9,... | collective-permute-start | bytes 3145736 | tf_op jit(solution)/shard_map/ppermute | solution.py:32
  37.4 9.1 %collective-permute-start.13 = (bf16[2,64,1024]{2,1,0:T(8,128)(2,1)S(1)}, bf16[2,64,1024]{2,1,0:T(8,128)(2,1)S(1)}, u32[]{:S(2)}, u32[]{:S(2)}) collective-permute-start(bf16[2,64,1024]{2,1,0:T(8,128)(2,1)S(1)} %slice_bitcast_fusion.1), channel_id=1, source_target_pairs={{0,32},{1,33},{2,34},{3,35},{4,36},{5,37},{6,38},{7,39},{8,40},{9,... | collective-permute-start | bytes 786440 | tf_op jit(solution)/shard_map/ppermute | solution.py:32
  40.4 9.2 %collective-permute-start.15 = (bf16[2,2,64,1024]{3,2,1,0:T(8,128)(2,1)S(1)}, bf16[2,2,64,1024]{3,2,1,0:T(8,128)(2,1)S(1)}, u32[]{:S(2)}, u32[]{:S(2)}) collective-permute-start(bf16[2,2,64,1024]{3,2,1,0:T(8,128)(2,1)S(1)} %collective-permute-done.12.t3), channel_id=1, source_target_pairs={{0,16},{1,17},{2,18},{3,19},{4,20},{5,21},{6,22},{7,23},{8,24},{9,... | collective-permute-start | bytes 1572872 | tf_op jit(solution)/shard_map/ppermute | solution.py:32
  44.3 5.3 %collective-permute-start.9 = (bf16[4,64,1024]{2,1,0:T(8,128)(2,1)S(1)}, bf16[4,64,1024]{2,1,0:T(8,128)(2,1)S(1)}, u32[]{:S(2)}, u32[]{:S(2)}) collective-permute-start(bf16[4,64,1024]{2,1,0:T(8,128)(2,1)S(1)} %pad_maximum_fusion.3), channel_id=1, source_target_pairs={{0,16},{1,17},{2,18},{3,19},{4,20},{5,21},{6,22},{7,23},{8,24},{9,... | collective-permute-start | bytes 1572872 | tf_op jit(solution)/shard_map/ppermute | solution.py:32
  46.4 3.2 %collective-permute-start.16 = (bf16[2,64,1024]{2,1,0:T(8,128)(2,1)S(1)}, bf16[2,64,1024]{2,1,0:T(8,128)(2,1)S(1)}, u32[]{:S(2)}, u32[]{:S(2)}) collective-permute-start(bf16[2,64,1024]{2,1,0:T(8,128)(2,1)S(1)} %collective-permute-done.13.far), channel_id=1, source_target_pairs={{0,16},{1,17},{2,18},{3,19},{4,20},{5,21},{6,22},{7,23},{8,24},{9,... | collective-permute-start | bytes 786440 | tf_op jit(solution)/shard_map/ppermute | solution.py:32
  60.9 6.3 %collective-permute-start.25 = (f32[8,1024]{1,0:T(8,128)S(1)}, f32[8,1024]{1,0:T(8,128)S(1)}, u32[]{:S(2)}, u32[]{:S(2)}) collective-permute-start(f32[8,1024]{1,0:T(8,128)S(1)} %get-tuple-element.37), channel_id=1, source_target_pairs={{0,96},{1,97},{2,98},{3,99},{4,100},{5,101},{6,102},{7,103},{8,104... | collective-permute-start | bytes 98312 | tf_op jit(solution)/shard_map/ppermute | solution.py:32
  61.4 7.9 %collective-permute-start.24 = (f32[8,1024]{1,0:T(8,128)S(1)}, f32[8,1024]{1,0:T(8,128)S(1)}, u32[]{:S(2)}, u32[]{:S(2)}) collective-permute-start(f32[8,1024]{1,0:T(8,128)S(1)} %get-tuple-element.37), channel_id=1, source_target_pairs={{0,64},{1,65},{2,66},{3,67},{4,68},{5,69},{6,70},{7,71},{8,72},{9,... | collective-permute-start | bytes 98312 | tf_op jit(solution)/shard_map/ppermute | solution.py:32
  66.1 3.3 %collective-permute-start.23 = (f32[8,1024]{1,0:T(8,128)S(1)}, f32[8,1024]{1,0:T(8,128)S(1)}, u32[]{:S(2)}, u32[]{:S(2)}) collective-permute-start(f32[8,1024]{1,0:T(8,128)S(1)} %get-tuple-element.37), channel_id=1, source_target_pairs={{0,32},{1,33},{2,34},{3,35},{4,36},{5,37},{6,38},{7,39},{8,40},{9,... | collective-permute-start | bytes 98312 | tf_op jit(solution)/shard_map/ppermute | solution.py:32
  66.1 7.8 %collective-permute-start.19 = (f32[8,1024]{1,0:T(8,128)S(1)}, f32[8,1024]{1,0:T(8,128)S(1)}, u32[]{:S(2)}, u32[]{:S(2)}) collective-permute-start(f32[8,1024]{1,0:T(8,128)S(1)} %get-tuple-element.36), channel_id=1, source_target_pairs={{0,3},{1,2},{2,1},{3,0},{4,7},{5,6},{6,5},{7,4},{8,11},{9,10},{10,... | collective-permute-start | bytes 98312 | tf_op jit(solution)/shard_map/ppermute | solution.py:32
  66.7 7.2 %collective-permute-start.18 = (f32[8,1024]{1,0:T(8,128)S(1)}, f32[8,1024]{1,0:T(8,128)S(1)}, u32[]{:S(2)}, u32[]{:S(2)}) collective-permute-start(f32[8,1024]{1,0:T(8,128)S(1)} %get-tuple-element.36), channel_id=1, source_target_pairs={{0,2},{1,3},{2,0},{3,1},{4,6},{5,7},{6,4},{7,5},{8,10},{9,11},{10,... | collective-permute-start | bytes 98312 | tf_op jit(solution)/shard_map/ppermute | solution.py:32
  67.2 6.7 %collective-permute-start.17 = (f32[8,1024]{1,0:T(8,128)S(1)}, f32[8,1024]{1,0:T(8,128)S(1)}, u32[]{:S(2)}, u32[]{:S(2)}) collective-permute-start(f32[8,1024]{1,0:T(8,128)S(1)} %get-tuple-element.36), channel_id=1, source_target_pairs={{0,1},{1,0},{2,3},{3,2},{4,5},{5,4},{6,7},{7,6},{8,9},{9,8},{10,11... | collective-permute-start | bytes 98312 | tf_op jit(solution)/shard_map/ppermute | solution.py:32
  69.5 8.1 %collective-permute-start.26 = (f32[5,1024]{1,0:T(8,128)S(1)}, f32[5,1024]{1,0:T(8,128)S(1)}, u32[]{:S(2)}, u32[]{:S(2)}) collective-permute-start(f32[5,1024]{1,0:T(8,128)S(1)} %concatenate.14), channel_id=1, source_target_pairs={{0,128},{1,129},{2,130},{3,131},{4,132},{5,133},{6,134},{7,135},{8... | collective-permute-start | bytes 61448 | tf_op jit(solution)/shard_map/ppermute | solution.py:32
  74.1 6.6 %collective-permute-start.22 = (f32[5,1024]{1,0:T(8,128)S(1)}, f32[5,1024]{1,0:T(8,128)S(1)}, u32[]{:S(2)}, u32[]{:S(2)}) collective-permute-start(f32[5,1024]{1,0:T(8,128)S(1)} %concatenate.13.ra), channel_id=1, source_target_pairs={{0,12},{1,13},{2,14},{3,15},{4,8},{5,9},{6,10},{7,11},{8,4},{9,5},... | collective-permute-start | bytes 61448 | tf_op jit(solution)/shard_map/ppermute | solution.py:32
  76.9 4.3 %collective-permute-start.21 = (f32[5,1024]{1,0:T(8,128)S(1)}, f32[5,1024]{1,0:T(8,128)S(1)}, u32[]{:S(2)}, u32[]{:S(2)}) collective-permute-start(f32[5,1024]{1,0:T(8,128)S(1)} %concatenate.13.ra), channel_id=1, source_target_pairs={{0,8},{1,9},{2,10},{3,11},{4,12},{5,13},{6,14},{7,15},{8,0},{9,1},... | collective-permute-start | bytes 61448 | tf_op jit(solution)/shard_map/ppermute | solution.py:32
  77.2 3.9 %collective-permute-start.20 = (f32[5,1024]{1,0:T(8,128)S(1)}, f32[5,1024]{1,0:T(8,128)S(1)}, u32[]{:S(2)}, u32[]{:S(2)}) collective-permute-start(f32[5,1024]{1,0:T(8,128)S(1)} %concatenate.13.ra), channel_id=1, source_target_pairs={{0,4},{1,5},{2,6},{3,7},{4,0},{5,1},{6,2},{7,3},{8,12},{9,13},{10,... | collective-permute-start | bytes 61448 | tf_op jit(solution)/shard_map/ppermute | solution.py:32
  77.7 3.9 %collective-permute-start.27 = (f32[5,1024]{1,0:T(8,128)S(1)}, f32[5,1024]{1,0:T(8,128)S(1)}, u32[]{:S(2)}, u32[]{:S(2)}) collective-permute-start(f32[5,1024]{1,0:T(8,128)S(1)} %concatenate.15.ca), channel_id=1, source_target_pairs={{0,16},{1,17},{2,18},{3,19},{4,20},{5,21},{6,22},{7,23},{8,24},{9,... | collective-permute-start | bytes 61448 | tf_op jit(solution)/shard_map/ppermute | solution.py:32
  93.9 7.1 %collective-permute-start.28 = (bf16[33,64,512]{2,1,0:T(8,128)(2,1)S(1)}, bf16[33,64,512]{2,1,0:T(8,128)(2,1)S(1)}, u32[]{:S(2)}, u32[]{:S(2)}) collective-permute-start(bf16[33,64,512]{2,1,0:T(8,128)(2,1)S(1)} %get-tuple-element.40), channel_id=1, source_target_pairs={{0,16},{1,17},{2,18},{3,19},{4,20},{5,21},{6,22},{7,23},{8,24},{9,... | collective-permute-start | bytes 6488072 | tf_op jit(solution)/shard_map/ppermute | solution.py:32
  101.4 8.7 %collective-permute-start.29 = (bf16[208,1024]{1,0:T(8,128)(2,1)S(1)}, bf16[208,1024]{1,0:T(8,128)(2,1)S(1)}, u32[]{:S(2)}, u32[]{:S(2)}) collective-permute-start(bf16[208,1024]{1,0:T(8,128)(2,1)S(1)} %get-tuple-element.45), channel_id=1, source_target_pairs={{0,64},{1,65},{2,66},{3,67},{4,68},{5,69},{6,70},{7,71},{8,72},{9,... | collective-permute-start | bytes 1277960 | tf_op jit(solution)/shard_map/ppermute | solution.py:32
  102.2 15.5 %collective-permute-start.32 = (bf16[528,512]{1,0:T(8,128)(2,1)S(1)}, bf16[528,512]{1,0:T(8,128)(2,1)S(1)}, u32[]{:S(2)}, u32[]{:S(2)}) collective-permute-start(bf16[528,512]{1,0:T(8,128)(2,1)S(1)} %get-tuple-element.50), channel_id=1, source_target_pairs={{0,1},{1,2},{2,3},{3,0},{4,5},{5,6},{6,7},{7,4},{8,9},{9,10},{10,1... | collective-permute-start | bytes 1622024 | tf_op jit(solution)/shard_map/ppermute | solution.py:32
  102.2 15.5 %collective-permute-start.33 = (bf16[528,512]{1,0:T(8,128)(2,1)S(1)}, bf16[528,512]{1,0:T(8,128)(2,1)S(1)}, u32[]{:S(2)}, u32[]{:S(2)}) collective-permute-start(bf16[528,512]{1,0:T(8,128)(2,1)S(1)} %get-tuple-element.51), channel_id=1, source_target_pairs={{0,3},{1,0},{2,1},{3,2},{4,7},{5,4},{6,5},{7,6},{8,11},{9,8},{10,9... | collective-permute-start | bytes 1622024 | tf_op jit(solution)/shard_map/ppermute | solution.py:32
  104.8 12.8 %collective-permute-start.34 = (bf16[528,512]{1,0:T(8,128)(2,1)S(1)}, bf16[528,512]{1,0:T(8,128)(2,1)S(1)}, u32[]{:S(2)}, u32[]{:S(2)}) collective-permute-start(bf16[528,512]{1,0:T(8,128)(2,1)S(1)} %get-tuple-element.52), channel_id=1, source_target_pairs={{0,2},{1,3},{2,0},{3,1},{4,6},{5,7},{6,4},{7,5},{8,10},{9,11},{10,... | collective-permute-start | bytes 1622024 | tf_op jit(solution)/shard_map/ppermute | solution.py:32
  110.2 16.5 %collective-permute-start.30 = (bf16[144,1024]{1,0:T(8,128)(2,1)S(1)}, bf16[144,1024]{1,0:T(8,128)(2,1)S(1)}, u32[]{:S(2)}, u32[]{:S(2)}) collective-permute-start(bf16[144,1024]{1,0:T(8,128)(2,1)S(1)} %get-tuple-element.47), channel_id=1, source_target_pairs={{0,32},{1,33},{2,34},{3,35},{4,36},{5,37},{6,38},{7,39},{8,40},{9,... | collective-permute-start | bytes 884744 | tf_op jit(solution)/shard_map/ppermute | solution.py:32
  115.6 12.2 %collective-permute-start.31 = (bf16[144,1024]{1,0:T(8,128)(2,1)S(1)}, bf16[144,1024]{1,0:T(8,128)(2,1)S(1)}, u32[]{:S(2)}, u32[]{:S(2)}) collective-permute-start(bf16[144,1024]{1,0:T(8,128)(2,1)S(1)} %get-tuple-element.48), channel_id=1, source_target_pairs={{0,64},{1,65},{2,66},{3,67},{4,68},{5,69},{6,70},{7,71},{8,72},{9,... | collective-permute-start | bytes 884744 | tf_op jit(solution)/shard_map/ppermute | solution.py:32
  118.0 4.4 %collective-permute-start.35 = (bf16[144,512]{1,0:T(8,128)(2,1)S(1)}, bf16[144,512]{1,0:T(8,128)(2,1)S(1)}, u32[]{:S(2)}, u32[]{:S(2)}) collective-permute-start(bf16[144,512]{1,0:T(8,128)(2,1)S(1)} %get-tuple-element.54), channel_id=1, source_target_pairs={{0,4},{1,5},{2,6},{3,7},{4,8},{5,9},{6,10},{7,11},{8,12},{9,13},{1... | collective-permute-start | bytes 442376 | tf_op jit(solution)/shard_map/ppermute | solution.py:32
  119.3 5.6 %collective-permute-start.36 = (bf16[144,512]{1,0:T(8,128)(2,1)S(1)}, bf16[144,512]{1,0:T(8,128)(2,1)S(1)}, u32[]{:S(2)}, u32[]{:S(2)}) collective-permute-start(bf16[144,512]{1,0:T(8,128)(2,1)S(1)} %get-tuple-element.55), channel_id=1, source_target_pairs={{0,8},{1,9},{2,10},{3,11},{4,12},{5,13},{6,14},{7,15},{8,0},{9,1},... | collective-permute-start | bytes 442376 | tf_op jit(solution)/shard_map/ppermute | solution.py:32
  120.2 6.5 %collective-permute-start.37 = (bf16[144,512]{1,0:T(8,128)(2,1)S(1)}, bf16[144,512]{1,0:T(8,128)(2,1)S(1)}, u32[]{:S(2)}, u32[]{:S(2)}) collective-permute-start(bf16[144,512]{1,0:T(8,128)(2,1)S(1)} %get-tuple-element.56), channel_id=1, source_target_pairs={{0,12},{1,13},{2,14},{3,15},{4,0},{5,1},{6,2},{7,3},{8,4},{9,5},{1... | collective-permute-start | bytes 442376 | tf_op jit(solution)/shard_map/ppermute | solution.py:32
  127.9 5.9 %collective-permute-start.38 = (bf16[80,1536]{1,0:T(8,128)(2,1)S(1)}, bf16[80,1536]{1,0:T(8,128)(2,1)S(1)}, u32[]{:S(2)}, u32[]{:S(2)}) collective-permute-start(bf16[80,1536]{1,0:T(8,128)(2,1)S(1)} %get-tuple-element.60), channel_id=1, source_target_pairs={{0,16},{1,17},{2,18},{3,19},{4,20},{5,21},{6,22},{7,23},{8,24},{9,... | collective-permute-start | bytes 737288 | tf_op jit(solution)/shard_map/ppermute | solution.py:32

commit v3 on v2

--- a/solution.py
+++ b/solution.py
@@ -153,7 +153,7 @@
         return out
 
     low = jnp.full((GROUP, LANES), -jnp.inf, F32)
-    col_tops = lax.fori_loop(0, size // GROUP, top_step, [[low] * tiles] * 2, unroll=2)
+    col_tops = lax.fori_loop(0, size // GROUP, top_step, [[low] * tiles] * 2, unroll=4)
     col_tops = [[jnp.max(v, axis=0, keepdims=True) for v in tops_k] for tops_k in col_tops]
     row_tops = []
     for k in range(2):
@@ -184,7 +184,7 @@
             return out
 
         none = jnp.zeros((GROUP, LANES), F32)
-        out = lax.fori_loop(0, size // GROUP, sum_step, [(none,) * 3] * len(span), unroll=2)
+        out = lax.fori_loop(0, size // GROUP, sum_step, [(none,) * 3] * len(span), unroll=8)
         for j, q in enumerate(span):
             a, b, w = [jnp.sum(v, axis=0, keepdims=True) for v in out[j]]
             zero = jnp.zeros_like(w)
@@ -300,7 +300,7 @@
             cs = [jnp.broadcast_to(col_s[:, s], (16, LANES)) for s in lanes]
 
             def step(i, inner):
-                part = pl.ds(pl.multiple_of(i * 16, 16), 16)
+                part = pl.ds(pl.multiple_of(r * chunk + i * 16, 16), 16)
                 rt, rs = wide[0, part, :], wide[1, part, :]
                 for j in range(span):
                     t, s = teach[part, lanes[j]], learn[part, lanes[j]]
@@ -308,7 +308,7 @@
                     coupling[part, lanes[j]] = (0.5 * v).astype(BF)
                 return inner
 
-            lax.fori_loop(r * (chunk // 16), (r + 1) * (chunk // 16), step, 0)
+            lax.fori_loop(0, chunk // 16, step, 0, unroll=8)
 
         @pl.when(r == 0)
         def _():
@@ -332,7 +332,7 @@
     enter[8].wait()
 
     def text_step(i, carry):
-        part = pl.ds(pl.multiple_of(i * chunk, chunk), chunk)
+        part = pl.ds(pl.multiple_of(i * 2 * chunk, 2 * chunk), 2 * chunk)
         product[part, :] = 100.0 * lax.dot_general(
             coupling[:, part],
             rows[...].reshape(size, d),
@@ -341,7 +341,7 @@
         )
         return carry
 
-    lax.fori_loop(0, 4, text_step, 0)
+    lax.fori_loop(0, 2, text_step, 0)
     out = 1 - 2 * c
 
     def text_block(k, core):
@@ -597,9 +597,11 @@
     core = lax.rem(lax.axis_index("row"), NC)
     keep = jnp.where(core == 0, teacher_image, student_image)
     give = jnp.where(core == 0, student_image, teacher_image)
-    got = swap(jnp.stack([give, teacher_text, student_text]), c_bits=1)
-    text_blocks = gather_cols(jnp.stack([jnp.stack([teacher_text, student_text]), got[1:]]))
-    image_blocks = gather_rows(jnp.stack([keep, got[0]]))
+    texts = [teacher_text, student_text]
+    texts = texts + [swap(v, c_bits=1) for v in texts]
+    text = jnp.stack(texts).reshape(2, 2, n, d)
+    text_blocks = gather_cols(text)
+    image_blocks = gather_rows(jnp.stack([keep, swap(give, c_bits=1)]))
     both, student, row_st, col_st = pass_1(
         list(image_blocks) + list(text_blocks), n, d
     )

time: 135 us -> 131 us (0.970)
  Pallas kernels: 25.4 us -> 22.4 us
  starting transfers between devices: 68.6 us -> 70.5 us
    ppermute x39 -> x41, starting transfers between devices: 68.6 us -> 70.5 us  [send(): return lax.ppermute(v, ('row', 'col'), pairs)]
    pallas_call x1, Pallas kernels: 12.3 us -> 10.5 us  [pass_2(): pl.pallas_call(pass_2_kernel, out_shape=(jax.ShapeDtypeStruct((33, n, d /...]
    another operation x4 -> x2, other arithmetic: 3.05 us -> 2.03 us  [the longest x1 1.04 us: per_device(): text = jnp.stack(texts).reshape(2, 2, n, d)]
    ppermute x39 -> x41, waiting for transfers between devices: 35.2 us -> 34.3 us  [send(): return lax.ppermute(v, ('row', 'col'), pairs)]
  transfers between devices with their start and end apart: 39 -> 41, of which waited for: 19 -> 20; matrix products, arithmetic and copies ran while one was open for 2% -> 2% of each run, Pallas kernels for 0% -> 0%
where the time goes in v3:
time: 131 us
  starting transfers between devices  70.5 us (54%)
  waiting for transfers between devices  34.3 us (26%)
  Pallas kernels  22.4 us (17%)
  other arithmetic  2.8 us (2%)
    ppermute x41, starting transfers between devices, send(): return lax.ppermute(v, ('row', 'col'), pairs)  70.5 us
    ppermute x41, waiting for transfers between devices, send(): return lax.ppermute(v, ('row', 'col'), pairs)  34.3 us
    pallas_call x1, Pallas kernels, pass_2(): pl.pallas_call(pass_2_kernel, out_shape=(jax.ShapeDtypeStruct((33, n, d /...  10.5 us
    pallas_call x1, Pallas kernels, pass_1(): pl.pallas_call(pass_1_kernel, out_shape=(both, blocks, small, small), in_...  10.1 us
  transfers between devices with their start and end apart: 41, of which 20 were waited for; matrix products, arithmetic and copies ran while one was open for 2% of the time, Pallas kernels for 0%

profile of v3, /device:TPU:39, one launch (start us, length us, event | category | flops | bytes accessed | tf_op | source)
XLA Modules:
  0.0 131.3 jit_solution(7837391536548382181)
XLA Ops:
  0.6 1.0 select_bitcast_fusion
  1.6 0.8 collective-permute-start
  3.4 3.0 %collective-permute-start.2 = (bf16[2,64,1024]{2,1,0:T(8,128)(2,1)S(1)}, bf16[2,64,1024]{2,1,0:T(8,128)(2,1)S(1)}, u32[]{:S(2)}, u32[]{:S(2)}) collective-permute-start(bf16[2,64,1024]{2,1,0:T(8,128)(2,1)S(1)} %get-tuple-element.74), channel_id=1, source_target_pairs={{0,2},{1,3},{2,0},{3,1},{4,6},{5,7},{6,4},{7,5},{8,10},{9,11},{10,... | collective-permute-start | bytes 786440 | tf_op jit(solution)/shard_map/ppermute | solution.py:32
  6.4 0.8 collective-permute-start.1
  7.2 0.7 collective-permute-start.3
  7.9 1.0 pad_maximum_fusion.4
  9.0 1.5 %collective-permute-done.2 = bf16[2,64,1024]{2,1,0:T(8,128)(2,1)S(1)} collective-permute-done((bf16[2,64,1024]{2,1,0:T(8,128)(2,1)S(1)}, bf16[2,64,1024]{2,1,0:T(8,128)(2,1)S(1)}, u32[]{:S(2)}, u32[]{:S(2)}) %collective-permute-start.2) | collective-permute-done | bytes 262176 | tf_op jit(solution)/shard_map/ppermute | solution.py:32
  10.5 3.2 %collective-permute-done.1 = bf16[2,64,1024]{2,1,0:T(8,128)(2,1)S(1)} collective-permute-done((bf16[2,64,1024]{2,1,0:T(8,128)(2,1)S(1)}, bf16[2,64,1024]{2,1,0:T(8,128)(2,1)S(1)}, u32[]{:S(2)}, u32[]{:S(2)}) %collective-permute-start.1) | collective-permute-done | bytes 262176 | tf_op jit(solution)/shard_map/ppermute | solution.py:32
  14.5 2.3 %collective-permute-start.4 = (bf16[2,4,64,1024]{3,2,1,0:T(8,128)(2,1)S(1)}, bf16[2,4,64,1024]{3,2,1,0:T(8,128)(2,1)S(1)}, u32[]{:S(2)}, u32[]{:S(2)}) collective-permute-start(bf16[2,4,64,1024]{3,2,1,0:T(8,128)(2,1)S(1)} %pad_maximum_fusion.1.line), channel_id=1, source_target_pairs={{0,4},{1,5},{2,6},{3,7},{4,8},{5,9},{6,10},{7,11},{8,12},{9,13},{1... | collective-permute-start | bytes 3145736 | tf_op jit(solution)/shard_map/ppermute | solution.py:32
  16.8 0.7 collective-permute-done.12.t1
  17.5 3.0 %collective-permute-start.13 = (bf16[2,2,64,1024]{3,2,1,0:T(8,128)(2,1)S(1)}, bf16[2,2,64,1024]{3,2,1,0:T(8,128)(2,1)S(1)}, u32[]{:S(2)}, u32[]{:S(2)}) collective-permute-start(bf16[2,2,64,1024]{3,2,1,0:T(8,128)(2,1)S(1)} %collective-permute-done.12.t1), channel_id=1, source_target_pairs={{0,32},{1,33},{2,34},{3,35},{4,36},{5,37},{6,38},{7,39},{8,40},{9,... | collective-permute-start | bytes 1572872 | tf_op jit(solution)/shard_map/ppermute | solution.py:32
  20.5 6.1 %collective-permute-done.13.t2 = bf16[2,2,64,1024]{3,2,1,0:T(8,128)(2,1)S(1)} collective-permute-done((bf16[2,2,64,1024]{3,2,1,0:T(8,128)(2,1)S(1)}, bf16[2,2,64,1024]{3,2,1,0:T(8,128)(2,1)S(1)}, u32[]{:S(2)}, u32[]{:S(2)}) %collective-permute-start.13) | collective-permute-done | bytes 524320 | tf_op jit(solution)/shard_map/ppermute | solution.py:32
  26.7 3.1 %collective-permute-start.14 = (bf16[2,2,64,1024]{3,2,1,0:T(8,128)(2,1)S(1)}, bf16[2,2,64,1024]{3,2,1,0:T(8,128)(2,1)S(1)}, u32[]{:S(2)}, u32[]{:S(2)}) collective-permute-start(bf16[2,2,64,1024]{3,2,1,0:T(8,128)(2,1)S(1)} %collective-permute-done.13.t2), channel_id=1, source_target_pairs={{0,32},{1,33},{2,34},{3,35},{4,36},{5,37},{6,38},{7,39},{8,40},{9,... | collective-permute-start | bytes 1572872 | tf_op jit(solution)/shard_map/ppermute | solution.py:32
  29.9 0.6 collective-permute-start.7
  30.8 3.5 %collective-permute-start.8 = (bf16[3,4,64,1024]{3,2,1,0:T(8,128)(2,1)S(1)}, bf16[3,4,64,1024]{3,2,1,0:T(8,128)(2,1)S(1)}, u32[]{:S(2)}, u32[]{:S(2)}) collective-permute-start(bf16[3,4,64,1024]{3,2,1,0:T(8,128)(2,1)S(1)} %pad_maximum_fusion), channel_id=1, source_target_pairs={{0,16},{1,17},{2,18},{3,19},{4,20},{5,21},{6,22},{7,23},{8,24},{9,... | collective-permute-start | bytes 4718600 | tf_op jit(solution)/shard_map/ppermute | solution.py:32
  34.3 1.3 %collective-permute-start.6 = (bf16[2,2,64,1024]{3,2,1,0:T(8,128)(2,1)S(1)}, bf16[2,2,64,1024]{3,2,1,0:T(8,128)(2,1)S(1)}, u32[]{:S(2)}, u32[]{:S(2)}) collective-permute-start(bf16[2,2,64,1024]{3,2,1,0:T(8,128)(2,1)S(1)} %slice.212), channel_id=1, source_target_pairs={{0,4},{1,5},{2,6},{3,7},{4,8},{5,9},{6,10},{7,11},{8,12},{9,13},{1... | collective-permute-start | bytes 1572872 | tf_op jit(solution)/shard_map/ppermute | solution.py:32
  35.9 3.5 %collective-permute-start.15 = (bf16[2,64,1024]{2,1,0:T(8,128)(2,1)S(1)}, bf16[2,64,1024]{2,1,0:T(8,128)(2,1)S(1)}, u32[]{:S(2)}, u32[]{:S(2)}) collective-permute-start(bf16[2,64,1024]{2,1,0:T(8,128)(2,1)S(1)} %slice_bitcast_fusion), channel_id=1, source_target_pairs={{0,32},{1,33},{2,34},{3,35},{4,36},{5,37},{6,38},{7,39},{8,40},{9,... | collective-permute-start | bytes 786440 | tf_op jit(solution)/shard_map/ppermute | solution.py:32
  39.5 1.2 collective-permute-start.17
  40.7 2.0 %collective-permute-done.6.far_a = bf16[2,2,64,1024]{3,2,1,0:T(8,128)(2,1)S(1)} collective-permute-done((bf16[2,2,64,1024]{3,2,1,0:T(8,128)(2,1)S(1)}, bf16[2,2,64,1024]{3,2,1,0:T(8,128)(2,1)S(1)}, u32[]{:S(2)}, u32[]{:S(2)}) %collective-permute-start.6) | collective-permute-done | bytes 524320 | tf_op jit(solution)/shard_map/ppermute | solution.py:32
  42.8 2.2 %collective-permute-start.9 = (bf16[4,64,1024]{2,1,0:T(8,128)(2,1)S(1)}, bf16[4,64,1024]{2,1,0:T(8,128)(2,1)S(1)}, u32[]{:S(2)}, u32[]{:S(2)}) collective-permute-start(bf16[4,64,1024]{2,1,0:T(8,128)(2,1)S(1)} %pad_maximum_fusion.3), channel_id=1, source_target_pairs={{0,16},{1,17},{2,18},{3,19},{4,20},{5,21},{6,22},{7,23},{8,24},{9,... | collective-permute-start | bytes 1572872 | tf_op jit(solution)/shard_map/ppermute | solution.py:32
  45.0 3.0 %collective-permute-start.18 = (bf16[2,64,1024]{2,1,0:T(8,128)(2,1)S(1)}, bf16[2,64,1024]{2,1,0:T(8,128)(2,1)S(1)}, u32[]{:S(2)}, u32[]{:S(2)}) collective-permute-start(bf16[2,64,1024]{2,1,0:T(8,128)(2,1)S(1)} %collective-permute-done.15.far), channel_id=1, source_target_pairs={{0,16},{1,17},{2,18},{3,19},{4,20},{5,21},{6,22},{7,23},{8,24},{9,... | collective-permute-start | bytes 786440 | tf_op jit(solution)/shard_map/ppermute | solution.py:32
  48.0 1.2 collective-permute-done.18.far_sib
  49.2 10.1 %shard_map.67 = (f32[2,1024,1024]{2,1,0:T(8,128)}, bf16[2,16,64,1024]{3,2,1,0:T(8,128)(2,1)}, f32[8,1024]{1,0:T(8,128)S(1)}, f32[8,1024]{1,0:T(8,128)S(1)}) custom-call(bf16[2,4,64,1024]{3,2,1,0:T(8,128)(2,1)S(1)} %pad_maximum_fusion.1.line, bf16[2,4,64,1024]{3,2,1,0:T(8,128)(2,1)S(1)} %collective-permute-done.4.up, ...), custom_call_target="tpu_custom_call" | custom-call | flops 4294967296 | bytes 20971520 | tf_op jit(solution)/shard_map/pallas_call | solution.py:208
  59.8 4.6 %collective-permute-start.26 = (f32[8,1024]{1,0:T(8,128)S(1)}, f32[8,1024]{1,0:T(8,128)S(1)}, u32[]{:S(2)}, u32[]{:S(2)}) collective-permute-start(f32[8,1024]{1,0:T(8,128)S(1)} %get-tuple-element.37), channel_id=1, source_target_pairs={{0,64},{1,65},{2,66},{3,67},{4,68},{5,69},{6,70},{7,71},{8,72},{9,... | collective-permute-start | bytes 98312 | tf_op jit(solution)/shard_map/ppermute | solution.py:32
  64.4 0.6 collective-permute-start.21
  65.1 2.6 %collective-permute-start.19 = (f32[8,1024]{1,0:T(8,128)S(1)}, f32[8,1024]{1,0:T(8,128)S(1)}, u32[]{:S(2)}, u32[]{:S(2)}) collective-permute-start(f32[8,1024]{1,0:T(8,128)S(1)} %get-tuple-element.36), channel_id=1, source_target_pairs={{0,1},{1,0},{2,3},{3,2},{4,5},{5,4},{6,7},{7,6},{8,9},{9,8},{10,11... | collective-permute-start | bytes 98312 | tf_op jit(solution)/shard_map/ppermute | solution.py:32
  67.9 4.4 %collective-permute-start.28 = (f32[5,1024]{1,0:T(8,128)S(1)}, f32[5,1024]{1,0:T(8,128)S(1)}, u32[]{:S(2)}, u32[]{:S(2)}) collective-permute-start(f32[5,1024]{1,0:T(8,128)S(1)} %concatenate.14), channel_id=1, source_target_pairs={{0,128},{1,129},{2,130},{3,131},{4,132},{5,133},{6,134},{7,135},{8... | collective-permute-start | bytes 61448 | tf_op jit(solution)/shard_map/ppermute | solution.py:32
  72.4 2.8 %collective-permute-start.24 = (f32[5,1024]{1,0:T(8,128)S(1)}, f32[5,1024]{1,0:T(8,128)S(1)}, u32[]{:S(2)}, u32[]{:S(2)}) collective-permute-start(f32[5,1024]{1,0:T(8,128)S(1)} %concatenate.13.ra), channel_id=1, source_target_pairs={{0,12},{1,13},{2,14},{3,15},{4,8},{5,9},{6,10},{7,11},{8,4},{9,5},... | collective-permute-start | bytes 61448 | tf_op jit(solution)/shard_map/ppermute | solution.py:32
  76.0 3.0 %collective-permute-start.29 = (f32[5,1024]{1,0:T(8,128)S(1)}, f32[5,1024]{1,0:T(8,128)S(1)}, u32[]{:S(2)}, u32[]{:S(2)}) collective-permute-start(f32[5,1024]{1,0:T(8,128)S(1)} %concatenate.15.ca), channel_id=1, source_target_pairs={{0,16},{1,17},{2,18},{3,19},{4,20},{5,21},{6,22},{7,23},{8,24},{9,... | collective-permute-start | bytes 61448 | tf_op jit(solution)/shard_map/ppermute | solution.py:32
  79.9 10.5 %shard_map.68 = (bf16[33,64,512]{2,1,0:T(8,128)(2,1)S(1)}, bf16[16,64,512]{2,1,0:T(8,128)(2,1)S(1)}, f32[8,64,1024]{2,1,0:T(8,128)S(1)}, f32[2,8,128]{2,1,0:T(8,128)S(1)}) custom-call(f32[2,1024,1024]{2,1,0:T(8,128)} %get-tuple-element.34.both_in, bf16[2,16,64,1024]{3,2,1,0:T(8,128)(2,1)} %get-tuple-element.35.student_in, f32[5,1024]{1,0:T(8,128)S(1)} %concatenate.13.ra, ...), custom_call_target="tpu_custom_call" | custom-call | flops 4294967296 | bytes 20971520 | tf_op jit(solution)/shard_map/pallas_call | solution.py:369
  90.5 3.2 %collective-permute-start.30 = (bf16[33,64,512]{2,1,0:T(8,128)(2,1)S(1)}, bf16[33,64,512]{2,1,0:T(8,128)(2,1)S(1)}, u32[]{:S(2)}, u32[]{:S(2)}) collective-permute-start(bf16[33,64,512]{2,1,0:T(8,128)(2,1)S(1)} %get-tuple-element.40), channel_id=1, source_target_pairs={{0,16},{1,17},{2,18},{3,19},{4,20},{5,21},{6,22},{7,23},{8,24},{9,... | collective-permute-start | bytes 6488072 | tf_op jit(solution)/shard_map/ppermute | solution.py:32
  93.6 3.9 %collective-permute-done.30.got = bf16[33,64,512]{2,1,0:T(8,128)(2,1)S(1)} collective-permute-done((bf16[33,64,512]{2,1,0:T(8,128)(2,1)S(1)}, bf16[33,64,512]{2,1,0:T(8,128)(2,1)S(1)}, u32[]{:S(2)}, u32[]{:S(2)}) %collective-permute-start.30) | collective-permute-done | bytes 2162720 | tf_op jit(solution)/shard_map/ppermute | solution.py:32
  97.9 0.8 collective-permute-start.31
  98.7 2.7 %collective-permute-start.35 = (bf16[528,512]{1,0:T(8,128)(2,1)S(1)}, bf16[528,512]{1,0:T(8,128)(2,1)S(1)}, u32[]{:S(2)}, u32[]{:S(2)}) collective-permute-start(bf16[528,512]{1,0:T(8,128)(2,1)S(1)} %get-tuple-element.51), channel_id=1, source_target_pairs={{0,3},{1,0},{2,1},{3,2},{4,7},{5,4},{6,5},{7,6},{8,11},{9,8},{10,9... | collective-permute-start | bytes 1622024 | tf_op jit(solution)/shard_map/ppermute | solution.py:32
  101.4 0.5 collective-permute-start.36
  101.9 4.6 %collective-permute-done.31.k34 = bf16[208,1024]{1,0:T(8,128)(2,1)S(1)} collective-permute-done((bf16[208,1024]{1,0:T(8,128)(2,1)S(1)}, bf16[208,1024]{1,0:T(8,128)(2,1)S(1)}, u32[]{:S(2)}, u32[]{:S(2)}) %collective-permute-start.31) | collective-permute-done | bytes 426016 | tf_op jit(solution)/shard_map/ppermute | solution.py:32
  106.7 5.4 %collective-permute-start.32 = (bf16[144,1024]{1,0:T(8,128)(2,1)S(1)}, bf16[144,1024]{1,0:T(8,128)(2,1)S(1)}, u32[]{:S(2)}, u32[]{:S(2)}) collective-permute-start(bf16[144,1024]{1,0:T(8,128)(2,1)S(1)} %get-tuple-element.47), channel_id=1, source_target_pairs={{0,32},{1,33},{2,34},{3,35},{4,36},{5,37},{6,38},{7,39},{8,40},{9,... | collective-permute-start | bytes 884744 | tf_op jit(solution)/shard_map/ppermute | solution.py:32
  112.1 1.5 %collective-permute-start.33 = (bf16[144,1024]{1,0:T(8,128)(2,1)S(1)}, bf16[144,1024]{1,0:T(8,128)(2,1)S(1)}, u32[]{:S(2)}, u32[]{:S(2)}) collective-permute-start(bf16[144,1024]{1,0:T(8,128)(2,1)S(1)} %get-tuple-element.48), channel_id=1, source_target_pairs={{0,64},{1,65},{2,66},{3,67},{4,68},{5,69},{6,70},{7,71},{8,72},{9,... | collective-permute-start | bytes 884744 | tf_op jit(solution)/shard_map/ppermute | solution.py:32
  113.6 0.6 collective-permute-done.34.p1
  114.5 1.4 %collective-permute-start.37 = (bf16[144,512]{1,0:T(8,128)(2,1)S(1)}, bf16[144,512]{1,0:T(8,128)(2,1)S(1)}, u32[]{:S(2)}, u32[]{:S(2)}) collective-permute-start(bf16[144,512]{1,0:T(8,128)(2,1)S(1)} %get-tuple-element.54), channel_id=1, source_target_pairs={{0,4},{1,5},{2,6},{3,7},{4,8},{5,9},{6,10},{7,11},{8,12},{9,13},{1... | collective-permute-start | bytes 442376 | tf_op jit(solution)/shard_map/ppermute | solution.py:32
  115.9 0.8 collective-permute-start.38
  116.7 2.1 %collective-permute-done.37.w1 = bf16[144,512]{1,0:T(8,128)(2,1)S(1)} collective-permute-done((bf16[144,512]{1,0:T(8,128)(2,1)S(1)}, bf16[144,512]{1,0:T(8,128)(2,1)S(1)}, u32[]{:S(2)}, u32[]{:S(2)}) %collective-permute-start.37) | collective-permute-done | bytes 147488 | tf_op jit(solution)/shard_map/ppermute | solution.py:32
  118.9 2.6 %collective-permute-done.38.w2 = bf16[144,512]{1,0:T(8,128)(2,1)S(1)} collective-permute-done((bf16[144,512]{1,0:T(8,128)(2,1)S(1)}, bf16[144,512]{1,0:T(8,128)(2,1)S(1)}, u32[]{:S(2)}, u32[]{:S(2)}) %collective-permute-start.38) | collective-permute-done | bytes 147488 | tf_op jit(solution)/shard_map/ppermute | solution.py:32
  121.5 1.8 %collective-permute-done.39.w3 = bf16[144,512]{1,0:T(8,128)(2,1)S(1)} collective-permute-done((bf16[144,512]{1,0:T(8,128)(2,1)S(1)}, bf16[144,512]{1,0:T(8,128)(2,1)S(1)}, u32[]{:S(2)}, u32[]{:S(2)}) %collective-permute-start.39) | collective-permute-done | bytes 147488 | tf_op jit(solution)/shard_map/ppermute | solution.py:32
  123.2 1.1 collective-permute-done.33.b2
  124.5 4.7 %collective-permute-start.40 = (bf16[80,1536]{1,0:T(8,128)(2,1)S(1)}, bf16[80,1536]{1,0:T(8,128)(2,1)S(1)}, u32[]{:S(2)}, u32[]{:S(2)}) collective-permute-start(bf16[80,1536]{1,0:T(8,128)(2,1)S(1)} %get-tuple-element.60), channel_id=1, source_target_pairs={{0,16},{1,17},{2,18},{3,19},{4,20},{5,21},{6,22},{7,23},{8,24},{9,... | collective-permute-start | bytes 737288 | tf_op jit(solution)/shard_map/ppermute | solution.py:32
  129.2 1.1 collective-permute-done.40.share
  130.4 0.8 shard_map.73
  (64 shorter events, 6.2 us)
Async XLA Ops:
  1.6 1.7 %collective-permute-start = (bf16[64,1024]{1,0:T(8,128)(2,1)S(1)}, bf16[64,1024]{1,0:T(8,128)(2,1)S(1)}, u32[]{:S(2)}, u32[]{:S(2)}) collective-permute-start(bf16[64,1024]{1,0:T(8,128)(2,1)S(1)} %get-tuple-element.76), channel_id=1, source_target_pairs={{0,16},{1,17},{2,18},{3,19},{4,20},{5,21},{6,22},{7,23},{8,24},{9,... | collective-permute-start | bytes 393224 | tf_op jit(solution)/shard_map/ppermute | solution.py:32
  2.4 5.5 %collective-permute-start.10 = (bf16[64,1024]{1,0:T(8,128)(2,1)}, bf16[64,1024]{1,0:T(8,128)(2,1)S(1)}, u32[]{:S(2)}, u32[]{:S(2)}) collective-permute-start(bf16[64,1024]{1,0:T(8,128)(2,1)} %param.5), channel_id=1, source_target_pairs={{0,16},{1,17},{2,18},{3,19},{4,20},{5,21},{6,22},{7,23},{8,24},{9,... | collective-permute-start | bytes 393224 | tf_op jit(solution)/shard_map/ppermute | solution.py:32
  2.5 5.4 %collective-permute-start.11 = (bf16[64,1024]{1,0:T(8,128)(2,1)}, bf16[64,1024]{1,0:T(8,128)(2,1)S(1)}, u32[]{:S(2)}, u32[]{:S(2)}) collective-permute-start(bf16[64,1024]{1,0:T(8,128)(2,1)} %param.7), channel_id=1, source_target_pairs={{0,16},{1,17},{2,18},{3,19},{4,20},{5,21},{6,22},{7,23},{8,24},{9,... | collective-permute-start | bytes 393224 | tf_op jit(solution)/shard_map/ppermute | solution.py:32
  3.4 7.1 %collective-permute-start.2 = (bf16[2,64,1024]{2,1,0:T(8,128)(2,1)S(1)}, bf16[2,64,1024]{2,1,0:T(8,128)(2,1)S(1)}, u32[]{:S(2)}, u32[]{:S(2)}) collective-permute-start(bf16[2,64,1024]{2,1,0:T(8,128)(2,1)S(1)} %get-tuple-element.74), channel_id=1, source_target_pairs={{0,2},{1,3},{2,0},{3,1},{4,6},{5,7},{6,4},{7,5},{8,10},{9,11},{10,... | collective-permute-start | bytes 786440 | tf_op jit(solution)/shard_map/ppermute | solution.py:32
  6.4 7.3 %collective-permute-start.1 = (bf16[2,64,1024]{2,1,0:T(8,128)(2,1)S(1)}, bf16[2,64,1024]{2,1,0:T(8,128)(2,1)S(1)}, u32[]{:S(2)}, u32[]{:S(2)}) collective-permute-start(bf16[2,64,1024]{2,1,0:T(8,128)(2,1)S(1)} %get-tuple-element.74), channel_id=1, source_target_pairs={{0,3},{1,0},{2,1},{3,2},{4,7},{5,4},{6,5},{7,6},{8,11},{9,8},{10,9... | collective-permute-start | bytes 786440 | tf_op jit(solution)/shard_map/ppermute | solution.py:32
  7.2 6.7 %collective-permute-start.3 = (bf16[2,64,1024]{2,1,0:T(8,128)(2,1)S(1)}, bf16[2,64,1024]{2,1,0:T(8,128)(2,1)S(1)}, u32[]{:S(2)}, u32[]{:S(2)}) collective-permute-start(bf16[2,64,1024]{2,1,0:T(8,128)(2,1)S(1)} %get-tuple-element.74), channel_id=1, source_target_pairs={{0,1},{1,2},{2,3},{3,0},{4,5},{5,6},{6,7},{7,4},{8,9},{9,10},{10,1... | collective-permute-start | bytes 786440 | tf_op jit(solution)/shard_map/ppermute | solution.py:32
  8.9 8.6 %collective-permute-start.12 = (bf16[2,2,64,1024]{3,2,1,0:T(8,128)(2,1)S(1)}, bf16[2,2,64,1024]{3,2,1,0:T(8,128)(2,1)S(1)}, u32[]{:S(2)}, u32[]{:S(2)}) collective-permute-start(bf16[2,2,64,1024]{3,2,1,0:T(8,128)(2,1)S(1)} %bitcast.28), channel_id=1, source_target_pairs={{0,32},{1,33},{2,34},{3,35},{4,36},{5,37},{6,38},{7,39},{8,40},{9,... | collective-permute-start | bytes 1572872 | tf_op jit(solution)/shard_map/ppermute | solution.py:32
  14.1 15.8 %collective-permute-start.5 = (bf16[2,4,64,1024]{3,2,1,0:T(8,128)(2,1)S(1)}, bf16[2,4,64,1024]{3,2,1,0:T(8,128)(2,1)S(1)}, u32[]{:S(2)}, u32[]{:S(2)}) collective-permute-start(bf16[2,4,64,1024]{3,2,1,0:T(8,128)(2,1)S(1)} %pad_maximum_fusion.1.line), channel_id=1, source_target_pairs={{0,12},{1,13},{2,14},{3,15},{4,0},{5,1},{6,2},{7,3},{8,4},{9,5},{1... | collective-permute-start | bytes 3145736 | tf_op jit(solution)/shard_map/ppermute | solution.py:32
  14.5 16.1 %collective-permute-start.4 = (bf16[2,4,64,1024]{3,2,1,0:T(8,128)(2,1)S(1)}, bf16[2,4,64,1024]{3,2,1,0:T(8,128)(2,1)S(1)}, u32[]{:S(2)}, u32[]{:S(2)}) collective-permute-start(bf16[2,4,64,1024]{3,2,1,0:T(8,128)(2,1)S(1)} %pad_maximum_fusion.1.line), channel_id=1, source_target_pairs={{0,4},{1,5},{2,6},{3,7},{4,8},{5,9},{6,10},{7,11},{8,12},{9,13},{1... | collective-permute-start | bytes 3145736 | tf_op jit(solution)/shard_map/ppermute | solution.py:32
  17.5 9.2 %collective-permute-start.13 = (bf16[2,2,64,1024]{3,2,1,0:T(8,128)(2,1)S(1)}, bf16[2,2,64,1024]{3,2,1,0:T(8,128)(2,1)S(1)}, u32[]{:S(2)}, u32[]{:S(2)}) collective-permute-start(bf16[2,2,64,1024]{3,2,1,0:T(8,128)(2,1)S(1)} %collective-permute-done.12.t1), channel_id=1, source_target_pairs={{0,32},{1,33},{2,34},{3,35},{4,36},{5,37},{6,38},{7,39},{8,40},{9,... | collective-permute-start | bytes 1572872 | tf_op jit(solution)/shard_map/ppermute | solution.py:32
  26.7 9.2 %collective-permute-start.14 = (bf16[2,2,64,1024]{3,2,1,0:T(8,128)(2,1)S(1)}, bf16[2,2,64,1024]{3,2,1,0:T(8,128)(2,1)S(1)}, u32[]{:S(2)}, u32[]{:S(2)}) collective-permute-start(bf16[2,2,64,1024]{3,2,1,0:T(8,128)(2,1)S(1)} %collective-permute-done.13.t2), channel_id=1, source_target_pairs={{0,32},{1,33},{2,34},{3,35},{4,36},{5,37},{6,38},{7,39},{8,40},{9,... | collective-permute-start | bytes 1572872 | tf_op jit(solution)/shard_map/ppermute | solution.py:32
  29.9 9.6 %collective-permute-start.7 = (bf16[2,2,64,1024]{3,2,1,0:T(8,128)(2,1)S(1)}, bf16[2,2,64,1024]{3,2,1,0:T(8,128)(2,1)S(1)}, u32[]{:S(2)}, u32[]{:S(2)}) collective-permute-start(bf16[2,2,64,1024]{3,2,1,0:T(8,128)(2,1)S(1)} %slice.213), channel_id=1, source_target_pairs={{0,12},{1,13},{2,14},{3,15},{4,0},{5,1},{6,2},{7,3},{8,4},{9,5},{1... | collective-permute-start | bytes 1572872 | tf_op jit(solution)/shard_map/ppermute | solution.py:32
  30.8 18.4 %collective-permute-start.8 = (bf16[3,4,64,1024]{3,2,1,0:T(8,128)(2,1)S(1)}, bf16[3,4,64,1024]{3,2,1,0:T(8,128)(2,1)S(1)}, u32[]{:S(2)}, u32[]{:S(2)}) collective-permute-start(bf16[3,4,64,1024]{3,2,1,0:T(8,128)(2,1)S(1)} %pad_maximum_fusion), channel_id=1, source_target_pairs={{0,16},{1,17},{2,18},{3,19},{4,20},{5,21},{6,22},{7,23},{8,24},{9,... | collective-permute-start | bytes 4718600 | tf_op jit(solution)/shard_map/ppermute | solution.py:32
  34.3 8.4 %collective-permute-start.6 = (bf16[2,2,64,1024]{3,2,1,0:T(8,128)(2,1)S(1)}, bf16[2,2,64,1024]{3,2,1,0:T(8,128)(2,1)S(1)}, u32[]{:S(2)}, u32[]{:S(2)}) collective-permute-start(bf16[2,2,64,1024]{3,2,1,0:T(8,128)(2,1)S(1)} %slice.212), channel_id=1, source_target_pairs={{0,4},{1,5},{2,6},{3,7},{4,8},{5,9},{6,10},{7,11},{8,12},{9,13},{1... | collective-permute-start | bytes 1572872 | tf_op jit(solution)/shard_map/ppermute | solution.py:32
  35.7 13.4 %collective-permute-start.16 = (bf16[2,2,2,64,1024]{4,3,2,1,0:T(8,128)(2,1)S(1)}, bf16[2,2,2,64,1024]{4,3,2,1,0:T(8,128)(2,1)S(1)}, u32[]{:S(2)}, u32[]{:S(2)}) collective-permute-start(bf16[2,2,2,64,1024]{4,3,2,1,0:T(8,128)(2,1)S(1)} %pad_maximum_fusion.2), channel_id=1, source_target_pairs={{0,16},{1,17},{2,18},{3,19},{4,20},{5,21},{6,22},{7,23},{8,24},{9,... | collective-permute-start | bytes 3145736 | tf_op jit(solution)/shard_map/ppermute | solution.py:32
  35.9 9.0 %collective-permute-start.15 = (bf16[2,64,1024]{2,1,0:T(8,128)(2,1)S(1)}, bf16[2,64,1024]{2,1,0:T(8,128)(2,1)S(1)}, u32[]{:S(2)}, u32[]{:S(2)}) collective-permute-start(bf16[2,64,1024]{2,1,0:T(8,128)(2,1)S(1)} %slice_bitcast_fusion), channel_id=1, source_target_pairs={{0,32},{1,33},{2,34},{3,35},{4,36},{5,37},{6,38},{7,39},{8,40},{9,... | collective-permute-start | bytes 786440 | tf_op jit(solution)/shard_map/ppermute | solution.py:32
  39.5 9.7 %collective-permute-start.17 = (bf16[2,2,64,1024]{3,2,1,0:T(8,128)(2,1)S(1)}, bf16[2,2,64,1024]{3,2,1,0:T(8,128)(2,1)S(1)}, u32[]{:S(2)}, u32[]{:S(2)}) collective-permute-start(bf16[2,2,64,1024]{3,2,1,0:T(8,128)(2,1)S(1)} %collective-permute-done.14.t3), channel_id=1, source_target_pairs={{0,16},{1,17},{2,18},{3,19},{4,20},{5,21},{6,22},{7,23},{8,24},{9,... | collective-permute-start | bytes 1572872 | tf_op jit(solution)/shard_map/ppermute | solution.py:32
  42.8 6.4 %collective-permute-start.9 = (bf16[4,64,1024]{2,1,0:T(8,128)(2,1)S(1)}, bf16[4,64,1024]{2,1,0:T(8,128)(2,1)S(1)}, u32[]{:S(2)}, u32[]{:S(2)}) collective-permute-start(bf16[4,64,1024]{2,1,0:T(8,128)(2,1)S(1)} %pad_maximum_fusion.3), channel_id=1, source_target_pairs={{0,16},{1,17},{2,18},{3,19},{4,20},{5,21},{6,22},{7,23},{8,24},{9,... | collective-permute-start | bytes 1572872 | tf_op jit(solution)/shard_map/ppermute | solution.py:32
  45.0 4.2 %collective-permute-start.18 = (bf16[2,64,1024]{2,1,0:T(8,128)(2,1)S(1)}, bf16[2,64,1024]{2,1,0:T(8,128)(2,1)S(1)}, u32[]{:S(2)}, u32[]{:S(2)}) collective-permute-start(bf16[2,64,1024]{2,1,0:T(8,128)(2,1)S(1)} %collective-permute-done.15.far), channel_id=1, source_target_pairs={{0,16},{1,17},{2,18},{3,19},{4,20},{5,21},{6,22},{7,23},{8,24},{9,... | collective-permute-start | bytes 786440 | tf_op jit(solution)/shard_map/ppermute | solution.py:32
  59.3 5.8 %collective-permute-start.27 = (f32[8,1024]{1,0:T(8,128)S(1)}, f32[8,1024]{1,0:T(8,128)S(1)}, u32[]{:S(2)}, u32[]{:S(2)}) collective-permute-start(f32[8,1024]{1,0:T(8,128)S(1)} %get-tuple-element.37), channel_id=1, source_target_pairs={{0,96},{1,97},{2,98},{3,99},{4,100},{5,101},{6,102},{7,103},{8,104... | collective-permute-start | bytes 98312 | tf_op jit(solution)/shard_map/ppermute | solution.py:32
  59.8 7.9 %collective-permute-start.26 = (f32[8,1024]{1,0:T(8,128)S(1)}, f32[8,1024]{1,0:T(8,128)S(1)}, u32[]{:S(2)}, u32[]{:S(2)}) collective-permute-start(f32[8,1024]{1,0:T(8,128)S(1)} %get-tuple-element.37), channel_id=1, source_target_pairs={{0,64},{1,65},{2,66},{3,67},{4,68},{5,69},{6,70},{7,71},{8,72},{9,... | collective-permute-start | bytes 98312 | tf_op jit(solution)/shard_map/ppermute | solution.py:32
  64.4 3.3 %collective-permute-start.25 = (f32[8,1024]{1,0:T(8,128)S(1)}, f32[8,1024]{1,0:T(8,128)S(1)}, u32[]{:S(2)}, u32[]{:S(2)}) collective-permute-start(f32[8,1024]{1,0:T(8,128)S(1)} %get-tuple-element.37), channel_id=1, source_target_pairs={{0,32},{1,33},{2,34},{3,35},{4,36},{5,37},{6,38},{7,39},{8,40},{9,... | collective-permute-start | bytes 98312 | tf_op jit(solution)/shard_map/ppermute | solution.py:32
  64.4 7.8 %collective-permute-start.21 = (f32[8,1024]{1,0:T(8,128)S(1)}, f32[8,1024]{1,0:T(8,128)S(1)}, u32[]{:S(2)}, u32[]{:S(2)}) collective-permute-start(f32[8,1024]{1,0:T(8,128)S(1)} %get-tuple-element.36), channel_id=1, source_target_pairs={{0,3},{1,2},{2,1},{3,0},{4,7},{5,6},{6,5},{7,4},{8,11},{9,10},{10,... | collective-permute-start | bytes 98312 | tf_op jit(solution)/shard_map/ppermute | solution.py:32
  65.0 7.2 %collective-permute-start.20 = (f32[8,1024]{1,0:T(8,128)S(1)}, f32[8,1024]{1,0:T(8,128)S(1)}, u32[]{:S(2)}, u32[]{:S(2)}) collective-permute-start(f32[8,1024]{1,0:T(8,128)S(1)} %get-tuple-element.36), channel_id=1, source_target_pairs={{0,2},{1,3},{2,0},{3,1},{4,6},{5,7},{6,4},{7,5},{8,10},{9,11},{10,... | collective-permute-start | bytes 98312 | tf_op jit(solution)/shard_map/ppermute | solution.py:32
  65.1 7.2 %collective-permute-start.19 = (f32[8,1024]{1,0:T(8,128)S(1)}, f32[8,1024]{1,0:T(8,128)S(1)}, u32[]{:S(2)}, u32[]{:S(2)}) collective-permute-start(f32[8,1024]{1,0:T(8,128)S(1)} %get-tuple-element.36), channel_id=1, source_target_pairs={{0,1},{1,0},{2,3},{3,2},{4,5},{5,4},{6,7},{7,6},{8,9},{9,8},{10,11... | collective-permute-start | bytes 98312 | tf_op jit(solution)/shard_map/ppermute | solution.py:32
  67.9 8.1 %collective-permute-start.28 = (f32[5,1024]{1,0:T(8,128)S(1)}, f32[5,1024]{1,0:T(8,128)S(1)}, u32[]{:S(2)}, u32[]{:S(2)}) collective-permute-start(f32[5,1024]{1,0:T(8,128)S(1)} %concatenate.14), channel_id=1, source_target_pairs={{0,128},{1,129},{2,130},{3,131},{4,132},{5,133},{6,134},{7,135},{8... | collective-permute-start | bytes 61448 | tf_op jit(solution)/shard_map/ppermute | solution.py:32
  72.4 6.6 %collective-permute-start.24 = (f32[5,1024]{1,0:T(8,128)S(1)}, f32[5,1024]{1,0:T(8,128)S(1)}, u32[]{:S(2)}, u32[]{:S(2)}) collective-permute-start(f32[5,1024]{1,0:T(8,128)S(1)} %concatenate.13.ra), channel_id=1, source_target_pairs={{0,12},{1,13},{2,14},{3,15},{4,8},{5,9},{6,10},{7,11},{8,4},{9,5},... | collective-permute-start | bytes 61448 | tf_op jit(solution)/shard_map/ppermute | solution.py:32
  75.2 4.3 %collective-permute-start.23 = (f32[5,1024]{1,0:T(8,128)S(1)}, f32[5,1024]{1,0:T(8,128)S(1)}, u32[]{:S(2)}, u32[]{:S(2)}) collective-permute-start(f32[5,1024]{1,0:T(8,128)S(1)} %concatenate.13.ra), channel_id=1, source_target_pairs={{0,8},{1,9},{2,10},{3,11},{4,12},{5,13},{6,14},{7,15},{8,0},{9,1},... | collective-permute-start | bytes 61448 | tf_op jit(solution)/shard_map/ppermute | solution.py:32
  75.6 3.9 %collective-permute-start.22 = (f32[5,1024]{1,0:T(8,128)S(1)}, f32[5,1024]{1,0:T(8,128)S(1)}, u32[]{:S(2)}, u32[]{:S(2)}) collective-permute-start(f32[5,1024]{1,0:T(8,128)S(1)} %concatenate.13.ra), channel_id=1, source_target_pairs={{0,4},{1,5},{2,6},{3,7},{4,0},{5,1},{6,2},{7,3},{8,12},{9,13},{10,... | collective-permute-start | bytes 61448 | tf_op jit(solution)/shard_map/ppermute | solution.py:32
  76.0 3.9 %collective-permute-start.29 = (f32[5,1024]{1,0:T(8,128)S(1)}, f32[5,1024]{1,0:T(8,128)S(1)}, u32[]{:S(2)}, u32[]{:S(2)}) collective-permute-start(f32[5,1024]{1,0:T(8,128)S(1)} %concatenate.15.ca), channel_id=1, source_target_pairs={{0,16},{1,17},{2,18},{3,19},{4,20},{5,21},{6,22},{7,23},{8,24},{9,... | collective-permute-start | bytes 61448 | tf_op jit(solution)/shard_map/ppermute | solution.py:32
  90.5 7.0 %collective-permute-start.30 = (bf16[33,64,512]{2,1,0:T(8,128)(2,1)S(1)}, bf16[33,64,512]{2,1,0:T(8,128)(2,1)S(1)}, u32[]{:S(2)}, u32[]{:S(2)}) collective-permute-start(bf16[33,64,512]{2,1,0:T(8,128)(2,1)S(1)} %get-tuple-element.40), channel_id=1, source_target_pairs={{0,16},{1,17},{2,18},{3,19},{4,20},{5,21},{6,22},{7,23},{8,24},{9,... | collective-permute-start | bytes 6488072 | tf_op jit(solution)/shard_map/ppermute | solution.py:32
  97.9 8.7 %collective-permute-start.31 = (bf16[208,1024]{1,0:T(8,128)(2,1)S(1)}, bf16[208,1024]{1,0:T(8,128)(2,1)S(1)}, u32[]{:S(2)}, u32[]{:S(2)}) collective-permute-start(bf16[208,1024]{1,0:T(8,128)(2,1)S(1)} %get-tuple-element.45), channel_id=1, source_target_pairs={{0,64},{1,65},{2,66},{3,67},{4,68},{5,69},{6,70},{7,71},{8,72},{9,... | collective-permute-start | bytes 1277960 | tf_op jit(solution)/shard_map/ppermute | solution.py:32
  98.7 15.5 %collective-permute-start.34 = (bf16[528,512]{1,0:T(8,128)(2,1)S(1)}, bf16[528,512]{1,0:T(8,128)(2,1)S(1)}, u32[]{:S(2)}, u32[]{:S(2)}) collective-permute-start(bf16[528,512]{1,0:T(8,128)(2,1)S(1)} %get-tuple-element.50), channel_id=1, source_target_pairs={{0,1},{1,2},{2,3},{3,0},{4,5},{5,6},{6,7},{7,4},{8,9},{9,10},{10,1... | collective-permute-start | bytes 1622024 | tf_op jit(solution)/shard_map/ppermute | solution.py:32
  98.7 15.5 %collective-permute-start.35 = (bf16[528,512]{1,0:T(8,128)(2,1)S(1)}, bf16[528,512]{1,0:T(8,128)(2,1)S(1)}, u32[]{:S(2)}, u32[]{:S(2)}) collective-permute-start(bf16[528,512]{1,0:T(8,128)(2,1)S(1)} %get-tuple-element.51), channel_id=1, source_target_pairs={{0,3},{1,0},{2,1},{3,2},{4,7},{5,4},{6,5},{7,6},{8,11},{9,8},{10,9... | collective-permute-start | bytes 1622024 | tf_op jit(solution)/shard_map/ppermute | solution.py:32
  101.4 12.8 %collective-permute-start.36 = (bf16[528,512]{1,0:T(8,128)(2,1)S(1)}, bf16[528,512]{1,0:T(8,128)(2,1)S(1)}, u32[]{:S(2)}, u32[]{:S(2)}) collective-permute-start(bf16[528,512]{1,0:T(8,128)(2,1)S(1)} %get-tuple-element.52), channel_id=1, source_target_pairs={{0,2},{1,3},{2,0},{3,1},{4,6},{5,7},{6,4},{7,5},{8,10},{9,11},{10,... | collective-permute-start | bytes 1622024 | tf_op jit(solution)/shard_map/ppermute | solution.py:32
  106.7 16.5 %collective-permute-start.32 = (bf16[144,1024]{1,0:T(8,128)(2,1)S(1)}, bf16[144,1024]{1,0:T(8,128)(2,1)S(1)}, u32[]{:S(2)}, u32[]{:S(2)}) collective-permute-start(bf16[144,1024]{1,0:T(8,128)(2,1)S(1)} %get-tuple-element.47), channel_id=1, source_target_pairs={{0,32},{1,33},{2,34},{3,35},{4,36},{5,37},{6,38},{7,39},{8,40},{9,... | collective-permute-start | bytes 884744 | tf_op jit(solution)/shard_map/ppermute | solution.py:32
  112.1 12.2 %collective-permute-start.33 = (bf16[144,1024]{1,0:T(8,128)(2,1)S(1)}, bf16[144,1024]{1,0:T(8,128)(2,1)S(1)}, u32[]{:S(2)}, u32[]{:S(2)}) collective-permute-start(bf16[144,1024]{1,0:T(8,128)(2,1)S(1)} %get-tuple-element.48), channel_id=1, source_target_pairs={{0,64},{1,65},{2,66},{3,67},{4,68},{5,69},{6,70},{7,71},{8,72},{9,... | collective-permute-start | bytes 884744 | tf_op jit(solution)/shard_map/ppermute | solution.py:32
  114.5 4.4 %collective-permute-start.37 = (bf16[144,512]{1,0:T(8,128)(2,1)S(1)}, bf16[144,512]{1,0:T(8,128)(2,1)S(1)}, u32[]{:S(2)}, u32[]{:S(2)}) collective-permute-start(bf16[144,512]{1,0:T(8,128)(2,1)S(1)} %get-tuple-element.54), channel_id=1, source_target_pairs={{0,4},{1,5},{2,6},{3,7},{4,8},{5,9},{6,10},{7,11},{8,12},{9,13},{1... | collective-permute-start | bytes 442376 | tf_op jit(solution)/shard_map/ppermute | solution.py:32
  115.9 5.6 %collective-permute-start.38 = (bf16[144,512]{1,0:T(8,128)(2,1)S(1)}, bf16[144,512]{1,0:T(8,128)(2,1)S(1)}, u32[]{:S(2)}, u32[]{:S(2)}) collective-permute-start(bf16[144,512]{1,0:T(8,128)(2,1)S(1)} %get-tuple-element.55), channel_id=1, source_target_pairs={{0,8},{1,9},{2,10},{3,11},{4,12},{5,13},{6,14},{7,15},{8,0},{9,1},... | collective-permute-start | bytes 442376 | tf_op jit(solution)/shard_map/ppermute | solution.py:32
  116.7 6.5 %collective-permute-start.39 = (bf16[144,512]{1,0:T(8,128)(2,1)S(1)}, bf16[144,512]{1,0:T(8,128)(2,1)S(1)}, u32[]{:S(2)}, u32[]{:S(2)}) collective-permute-start(bf16[144,512]{1,0:T(8,128)(2,1)S(1)} %get-tuple-element.56), channel_id=1, source_target_pairs={{0,12},{1,13},{2,14},{3,15},{4,0},{5,1},{6,2},{7,3},{8,4},{9,5},{1... | collective-permute-start | bytes 442376 | tf_op jit(solution)/shard_map/ppermute | solution.py:32
  124.5 5.9 %collective-permute-start.40 = (bf16[80,1536]{1,0:T(8,128)(2,1)S(1)}, bf16[80,1536]{1,0:T(8,128)(2,1)S(1)}, u32[]{:S(2)}, u32[]{:S(2)}) collective-permute-start(bf16[80,1536]{1,0:T(8,128)(2,1)S(1)} %get-tuple-element.60), channel_id=1, source_target_pairs={{0,16},{1,17},{2,18},{3,19},{4,20},{5,21},{6,22},{7,23},{8,24},{9,... | collective-permute-start | bytes 737288 | tf_op jit(solution)/shard_map/ppermute | solution.py:32

commit v4 on v3

--- a/solution.py
+++ b/solution.py
@@ -252,7 +252,7 @@
 
 def pass_2_kernel(
     both_in, student_in, ra, rb, rc, rd, ca, cb,
-    give, keep_image, keep_text, loss_part,
+    give, give_text, keep_image, keep_text, loss_part,
     teach, learn, rows, cols, coupling, wide, product, sem,
 ):
     z, c, y, x = position()
@@ -280,9 +280,9 @@
     whole = jnp.broadcast_to(part_r, (16, half))
     for k in range(3):
         piece = whole.astype(BF)
-        give[32, 16 * k : 16 * k + 16] = piece
+        give_text[16, 16 * k : 16 * k + 16] = piece
         whole = whole - piece.astype(F32)
-    give[32, 48:] = jnp.zeros((n - 48, half), BF)
+    give_text[16, 48:] = jnp.zeros((n - 48, half), BF)
     for k, v in ((0, row_t), (1, row_s)):
         wide[k] = jnp.broadcast_to(v, (LANES, size)).T
 
@@ -350,8 +350,8 @@
 
     def put(i, v):
         v = v.astype(BF)
-        give[16 + i] = v[:, :half]
-        give[24 + i] = v[:, half:]
+        give_text[i] = v[:, :half]
+        give_text[8 + i] = v[:, half:]
 
     put(0, text_block(0, 1 - c))
     put(1, text_block(4, 1 - c))
@@ -369,13 +369,14 @@
     return pl.pallas_call(
         pass_2_kernel,
         out_shape=(
-            jax.ShapeDtypeStruct((33, n, d // 2), BF),
+            jax.ShapeDtypeStruct((16, n, d // 2), BF),
+            jax.ShapeDtypeStruct((17, n, d // 2), BF),
             jax.ShapeDtypeStruct((16, n, d // 2), BF),
             jax.ShapeDtypeStruct((8, n, d), F32),
             jax.ShapeDtypeStruct((2, 8, LANES), F32),
         ),
         in_specs=[pl.BlockSpec(memory_space=pltpu.HBM)] * 2 + [vmem] * (len(args) - 2),
-        out_specs=(vmem,) * 4,
+        out_specs=(vmem,) * 5,
         scratch_shapes=[
             pltpu.VMEM((size, size), F32),
             pltpu.VMEM((size, size), F32),
@@ -422,16 +423,13 @@
     return jnp.where(flag + jnp.zeros(a.shape, jnp.int32) == 0, a, b)
 
 
-def load_kernel(
-    keep_text, keep_image, got, loss_part,
-    text_own, k1, k2, k34, image_own, p1, m1, far, rows_loss,
-):
+def load_text_kernel(keep_text, got, loss_part, text_own, k1, k2, k34, rows_loss):
     z, _, _, _ = position()
     n, h = got.shape[1:]
     for i in range(8):
         for q in range(2):
             lanes = slice(q * h, (q + 1) * h)
-            v = keep_text[i, :, lanes] + got[16 + 8 * q + i].astype(F32)
+            v = keep_text[i, :, lanes] + got[8 * q + i].astype(F32)
             if i == 0:
                 text_own[:, lanes] = v
             elif i == 1:
@@ -440,6 +438,17 @@
                 k34[(i - 6) * n : (i - 5) * n, lanes] = v.astype(BF)
             else:
                 (k1, k2)[i // 2 - 1][i % 2, :, lanes] = v
+    sib = got[16].astype(F32)
+    chip = loss_part[0, :1] + ((sib[0:1, :LANES] + sib[16:17, :LANES]) + sib[32:33, :LANES])
+    lane = lax.broadcasted_iota(jnp.int32, (1, LANES), 1)
+    mine = jnp.where(lane == z, chip, 0.0)
+    rows_loss[...] = jnp.broadcast_to(mine, (8, LANES))
+    k34[3 * n :] = jnp.zeros((16, 2 * h), BF)
+    pack(k34, 3 * n, 0, mine)
+
+
+def load_image_kernel(keep_image, got, loss_part, image_own, p1, m1, far):
+    n, h = got.shape[1:]
     image_own[0] = keep_image[0:4]
     image_own[1] = got[0:4]
     cols_loss = loss_part[1, :1]
@@ -448,13 +457,6 @@
         out[4 * n : 8 * n] = got[f * 4 : f * 4 + 4].reshape(4 * n, h)
         out[8 * n :] = jnp.zeros((16, h), BF)
         pack(out, 8 * n, 0, cols_loss)
-    sib = got[32].astype(F32)
-    chip = loss_part[0, :1] + ((sib[0:1, :LANES] + sib[16:17, :LANES]) + sib[32:33, :LANES])
-    lane = lax.broadcasted_iota(jnp.int32, (1, LANES), 1)
-    mine = jnp.where(lane == z, chip, 0.0)
-    rows_loss[...] = jnp.broadcast_to(mine, (8, LANES))
-    k34[3 * n :] = jnp.zeros((16, 2 * h), BF)
-    pack(k34, 3 * n, 0, mine)
 
 
 def pass_on_kernel(k1, k2, k34, rows_loss, b1, b2):
@@ -534,18 +536,20 @@
     total[0] = (jnp.sum(rows) + jnp.max(cols)) * scale
 
 
-def reduce_all(give, keep_image, keep_text, loss_part):
+def reduce_all(give, give_text, keep_image, keep_text, loss_part):
     n, d = keep_text.shape[1:]
     h = d // 2
-    got = swap(give, c_bits=1)
     small = ((8, LANES), F32)
     pair, line_out = ((2, n, d), F32), ((8 * n + 16, h), BF)
-    text_own, k1, k2, k34, image_own, p1, m1, far, rows_loss = vmem_call(
-        load_kernel,
-        [((n, d), F32), pair, pair, ((3 * n + 16, d), BF), ((2, 4, n, h), BF)]
-        + [line_out] * 3
-        + [small],
-        (keep_text, keep_image, got, loss_part),
+    text_own, k1, k2, k34, rows_loss = vmem_call(
+        load_text_kernel,
+        [((n, d), F32), pair, pair, ((3 * n + 16, d), BF), small],
+        (keep_text, swap(give_text, c_bits=1), loss_part),
+    )
+    image_own, p1, m1, far = vmem_call(
+        load_image_kernel,
+        [((2, 4, n, h), BF)] + [line_out] * 3,
+        (keep_image, swap(give, c_bits=1), loss_part),
     )
     far = move_first(far, 2)
     k34 = move_z(k34, 2)
@@ -605,10 +609,12 @@
     both, student, row_st, col_st = pass_1(
         list(image_blocks) + list(text_blocks), n, d
     )
-    give, keep_image, keep_text, loss_part = pass_2(
+    give, give_text, keep_image, keep_text, loss_part = pass_2(
         [both, student] + merge_steps(row_st, col_st), n, d
     )
-    text_grad, image_grad, loss = reduce_all(give, keep_image, keep_text, loss_part)
+    text_grad, image_grad, loss = reduce_all(
+        give, give_text, keep_image, keep_text, loss_part
+    )
     return (image_grad, text_grad, loss.reshape(()))
 
 

time: 131 us -> 130 us (level)
  waiting for transfers between devices: 34.3 us -> 32.7 us
    ppermute x41 -> x42, waiting for transfers between devices: 34.3 us -> 32.7 us  [send(): return lax.ppermute(v, ('row', 'col'), pairs)]
    ppermute x41 -> x42, starting transfers between devices: 70.5 us -> 70.4 us  [send(): return lax.ppermute(v, ('row', 'col'), pairs)]
  transfers between devices with their start and end apart: 41 -> 42, of which waited for: 20 -> 21; matrix products, arithmetic and copies ran while one was open for 2% -> 2% of each run, Pallas kernels for 0% -> 1%
where the time goes in v4:
time: 130 us
  starting transfers between devices  70.4 us (54%)
  waiting for transfers between devices  32.7 us (25%)
  Pallas kernels  22.3 us (17%)
  other arithmetic  2.8 us (2%)
    ppermute x42, starting transfers between devices, send(): return lax.ppermute(v, ('row', 'col'), pairs)  70.4 us
    ppermute x42, waiting for transfers between devices, send(): return lax.ppermute(v, ('row', 'col'), pairs)  32.7 us
    pallas_call x1, Pallas kernels, pass_2(): pl.pallas_call(pass_2_kernel, out_shape=(jax.ShapeDtypeStruct((16, n, d /...  10.5 us
    pallas_call x1, Pallas kernels, pass_1(): pl.pallas_call(pass_1_kernel, out_shape=(both, blocks, small, small), in_...  10.1 us
  transfers between devices with their start and end apart: 42, of which 21 were waited for; matrix products, arithmetic and copies ran while one was open for 2% of the time, Pallas kernels for 1%

profile of v4, /device:TPU:39, one launch (start us, length us, event | category | flops | bytes accessed | tf_op | source)
XLA Modules:
  0.0 129.6 jit_solution(6192051901305394452)
XLA Ops:
  0.6 1.0 select_bitcast_fusion
  1.6 0.8 collective-permute-start
  3.4 3.0 %collective-permute-start.2 = (bf16[2,64,1024]{2,1,0:T(8,128)(2,1)S(1)}, bf16[2,64,1024]{2,1,0:T(8,128)(2,1)S(1)}, u32[]{:S(2)}, u32[]{:S(2)}) collective-permute-start(bf16[2,64,1024]{2,1,0:T(8,128)(2,1)S(1)} %get-tuple-element.76), channel_id=1, source_target_pairs={{0,2},{1,3},{2,0},{3,1},{4,6},{5,7},{6,4},{7,5},{8,10},{9,11},{10,... | collective-permute-start | bytes 786440 | tf_op jit(solution)/shard_map/ppermute | solution.py:32
  6.4 0.8 collective-permute-start.1
  7.2 0.7 collective-permute-start.3
  7.9 1.0 pad_maximum_fusion.4
  9.0 1.5 %collective-permute-done.2 = bf16[2,64,1024]{2,1,0:T(8,128)(2,1)S(1)} collective-permute-done((bf16[2,64,1024]{2,1,0:T(8,128)(2,1)S(1)}, bf16[2,64,1024]{2,1,0:T(8,128)(2,1)S(1)}, u32[]{:S(2)}, u32[]{:S(2)}) %collective-permute-start.2) | collective-permute-done | bytes 262176 | tf_op jit(solution)/shard_map/ppermute | solution.py:32
  10.5 3.2 %collective-permute-done.1 = bf16[2,64,1024]{2,1,0:T(8,128)(2,1)S(1)} collective-permute-done((bf16[2,64,1024]{2,1,0:T(8,128)(2,1)S(1)}, bf16[2,64,1024]{2,1,0:T(8,128)(2,1)S(1)}, u32[]{:S(2)}, u32[]{:S(2)}) %collective-permute-start.1) | collective-permute-done | bytes 262176 | tf_op jit(solution)/shard_map/ppermute | solution.py:32
  14.5 2.3 %collective-permute-start.4 = (bf16[2,4,64,1024]{3,2,1,0:T(8,128)(2,1)S(1)}, bf16[2,4,64,1024]{3,2,1,0:T(8,128)(2,1)S(1)}, u32[]{:S(2)}, u32[]{:S(2)}) collective-permute-start(bf16[2,4,64,1024]{3,2,1,0:T(8,128)(2,1)S(1)} %pad_maximum_fusion.1.line), channel_id=1, source_target_pairs={{0,4},{1,5},{2,6},{3,7},{4,8},{5,9},{6,10},{7,11},{8,12},{9,13},{1... | collective-permute-start | bytes 3145736 | tf_op jit(solution)/shard_map/ppermute | solution.py:32
  16.8 0.7 collective-permute-done.12.t1
  17.5 3.0 %collective-permute-start.13 = (bf16[2,2,64,1024]{3,2,1,0:T(8,128)(2,1)S(1)}, bf16[2,2,64,1024]{3,2,1,0:T(8,128)(2,1)S(1)}, u32[]{:S(2)}, u32[]{:S(2)}) collective-permute-start(bf16[2,2,64,1024]{3,2,1,0:T(8,128)(2,1)S(1)} %collective-permute-done.12.t1), channel_id=1, source_target_pairs={{0,32},{1,33},{2,34},{3,35},{4,36},{5,37},{6,38},{7,39},{8,40},{9,... | collective-permute-start | bytes 1572872 | tf_op jit(solution)/shard_map/ppermute | solution.py:32
  20.5 6.1 %collective-permute-done.13.t2 = bf16[2,2,64,1024]{3,2,1,0:T(8,128)(2,1)S(1)} collective-permute-done((bf16[2,2,64,1024]{3,2,1,0:T(8,128)(2,1)S(1)}, bf16[2,2,64,1024]{3,2,1,0:T(8,128)(2,1)S(1)}, u32[]{:S(2)}, u32[]{:S(2)}) %collective-permute-start.13) | collective-permute-done | bytes 524320 | tf_op jit(solution)/shard_map/ppermute | solution.py:32
  26.7 3.1 %collective-permute-start.14 = (bf16[2,2,64,1024]{3,2,1,0:T(8,128)(2,1)S(1)}, bf16[2,2,64,1024]{3,2,1,0:T(8,128)(2,1)S(1)}, u32[]{:S(2)}, u32[]{:S(2)}) collective-permute-start(bf16[2,2,64,1024]{3,2,1,0:T(8,128)(2,1)S(1)} %collective-permute-done.13.t2), channel_id=1, source_target_pairs={{0,32},{1,33},{2,34},{3,35},{4,36},{5,37},{6,38},{7,39},{8,40},{9,... | collective-permute-start | bytes 1572872 | tf_op jit(solution)/shard_map/ppermute | solution.py:32
  29.9 0.6 collective-permute-start.7
  30.8 3.5 %collective-permute-start.8 = (bf16[3,4,64,1024]{3,2,1,0:T(8,128)(2,1)S(1)}, bf16[3,4,64,1024]{3,2,1,0:T(8,128)(2,1)S(1)}, u32[]{:S(2)}, u32[]{:S(2)}) collective-permute-start(bf16[3,4,64,1024]{3,2,1,0:T(8,128)(2,1)S(1)} %pad_maximum_fusion), channel_id=1, source_target_pairs={{0,16},{1,17},{2,18},{3,19},{4,20},{5,21},{6,22},{7,23},{8,24},{9,... | collective-permute-start | bytes 4718600 | tf_op jit(solution)/shard_map/ppermute | solution.py:32
  34.3 1.3 %collective-permute-start.6 = (bf16[2,2,64,1024]{3,2,1,0:T(8,128)(2,1)S(1)}, bf16[2,2,64,1024]{3,2,1,0:T(8,128)(2,1)S(1)}, u32[]{:S(2)}, u32[]{:S(2)}) collective-permute-start(bf16[2,2,64,1024]{3,2,1,0:T(8,128)(2,1)S(1)} %slice.212), channel_id=1, source_target_pairs={{0,4},{1,5},{2,6},{3,7},{4,8},{5,9},{6,10},{7,11},{8,12},{9,13},{1... | collective-permute-start | bytes 1572872 | tf_op jit(solution)/shard_map/ppermute | solution.py:32
  35.9 3.5 %collective-permute-start.15 = (bf16[2,64,1024]{2,1,0:T(8,128)(2,1)S(1)}, bf16[2,64,1024]{2,1,0:T(8,128)(2,1)S(1)}, u32[]{:S(2)}, u32[]{:S(2)}) collective-permute-start(bf16[2,64,1024]{2,1,0:T(8,128)(2,1)S(1)} %slice_bitcast_fusion), channel_id=1, source_target_pairs={{0,32},{1,33},{2,34},{3,35},{4,36},{5,37},{6,38},{7,39},{8,40},{9,... | collective-permute-start | bytes 786440 | tf_op jit(solution)/shard_map/ppermute | solution.py:32
  39.5 1.2 collective-permute-start.17
  40.7 2.0 %collective-permute-done.6.far_a = bf16[2,2,64,1024]{3,2,1,0:T(8,128)(2,1)S(1)} collective-permute-done((bf16[2,2,64,1024]{3,2,1,0:T(8,128)(2,1)S(1)}, bf16[2,2,64,1024]{3,2,1,0:T(8,128)(2,1)S(1)}, u32[]{:S(2)}, u32[]{:S(2)}) %collective-permute-start.6) | collective-permute-done | bytes 524320 | tf_op jit(solution)/shard_map/ppermute | solution.py:32
  42.8 2.2 %collective-permute-start.9 = (bf16[4,64,1024]{2,1,0:T(8,128)(2,1)S(1)}, bf16[4,64,1024]{2,1,0:T(8,128)(2,1)S(1)}, u32[]{:S(2)}, u32[]{:S(2)}) collective-permute-start(bf16[4,64,1024]{2,1,0:T(8,128)(2,1)S(1)} %pad_maximum_fusion.3), channel_id=1, source_target_pairs={{0,16},{1,17},{2,18},{3,19},{4,20},{5,21},{6,22},{7,23},{8,24},{9,... | collective-permute-start | bytes 1572872 | tf_op jit(solution)/shard_map/ppermute | solution.py:32
  45.0 3.0 %collective-permute-start.18 = (bf16[2,64,1024]{2,1,0:T(8,128)(2,1)S(1)}, bf16[2,64,1024]{2,1,0:T(8,128)(2,1)S(1)}, u32[]{:S(2)}, u32[]{:S(2)}) collective-permute-start(bf16[2,64,1024]{2,1,0:T(8,128)(2,1)S(1)} %collective-permute-done.15.far), channel_id=1, source_target_pairs={{0,16},{1,17},{2,18},{3,19},{4,20},{5,21},{6,22},{7,23},{8,24},{9,... | collective-permute-start | bytes 786440 | tf_op jit(solution)/shard_map/ppermute | solution.py:32
  48.0 1.2 collective-permute-done.18.far_sib
  49.2 10.1 %shard_map.67 = (f32[2,1024,1024]{2,1,0:T(8,128)}, bf16[2,16,64,1024]{3,2,1,0:T(8,128)(2,1)}, f32[8,1024]{1,0:T(8,128)S(1)}, f32[8,1024]{1,0:T(8,128)S(1)}) custom-call(bf16[2,4,64,1024]{3,2,1,0:T(8,128)(2,1)S(1)} %pad_maximum_fusion.1.line, bf16[2,4,64,1024]{3,2,1,0:T(8,128)(2,1)S(1)} %collective-permute-done.4.up, ...), custom_call_target="tpu_custom_call" | custom-call | flops 4294967296 | bytes 20971520 | tf_op jit(solution)/shard_map/pallas_call | solution.py:208
  59.8 4.6 %collective-permute-start.26 = (f32[8,1024]{1,0:T(8,128)S(1)}, f32[8,1024]{1,0:T(8,128)S(1)}, u32[]{:S(2)}, u32[]{:S(2)}) collective-permute-start(f32[8,1024]{1,0:T(8,128)S(1)} %get-tuple-element.38), channel_id=1, source_target_pairs={{0,64},{1,65},{2,66},{3,67},{4,68},{5,69},{6,70},{7,71},{8,72},{9,... | collective-permute-start | bytes 98312 | tf_op jit(solution)/shard_map/ppermute | solution.py:32
  64.4 0.6 collective-permute-start.21
  65.1 2.6 %collective-permute-start.19 = (f32[8,1024]{1,0:T(8,128)S(1)}, f32[8,1024]{1,0:T(8,128)S(1)}, u32[]{:S(2)}, u32[]{:S(2)}) collective-permute-start(f32[8,1024]{1,0:T(8,128)S(1)} %get-tuple-element.37), channel_id=1, source_target_pairs={{0,1},{1,0},{2,3},{3,2},{4,5},{5,4},{6,7},{7,6},{8,9},{9,8},{10,11... | collective-permute-start | bytes 98312 | tf_op jit(solution)/shard_map/ppermute | solution.py:32
  67.9 4.4 %collective-permute-start.28 = (f32[5,1024]{1,0:T(8,128)S(1)}, f32[5,1024]{1,0:T(8,128)S(1)}, u32[]{:S(2)}, u32[]{:S(2)}) collective-permute-start(f32[5,1024]{1,0:T(8,128)S(1)} %concatenate.14), channel_id=1, source_target_pairs={{0,128},{1,129},{2,130},{3,131},{4,132},{5,133},{6,134},{7,135},{8... | collective-permute-start | bytes 61448 | tf_op jit(solution)/shard_map/ppermute | solution.py:32
  72.4 2.8 %collective-permute-start.24 = (f32[5,1024]{1,0:T(8,128)S(1)}, f32[5,1024]{1,0:T(8,128)S(1)}, u32[]{:S(2)}, u32[]{:S(2)}) collective-permute-start(f32[5,1024]{1,0:T(8,128)S(1)} %concatenate.13.ra), channel_id=1, source_target_pairs={{0,12},{1,13},{2,14},{3,15},{4,8},{5,9},{6,10},{7,11},{8,4},{9,5},... | collective-permute-start | bytes 61448 | tf_op jit(solution)/shard_map/ppermute | solution.py:32
  76.0 3.0 %collective-permute-start.29 = (f32[5,1024]{1,0:T(8,128)S(1)}, f32[5,1024]{1,0:T(8,128)S(1)}, u32[]{:S(2)}, u32[]{:S(2)}) collective-permute-start(f32[5,1024]{1,0:T(8,128)S(1)} %concatenate.15.ca), channel_id=1, source_target_pairs={{0,16},{1,17},{2,18},{3,19},{4,20},{5,21},{6,22},{7,23},{8,24},{9,... | collective-permute-start | bytes 61448 | tf_op jit(solution)/shard_map/ppermute | solution.py:32
  79.9 10.5 %shard_map.68 = (bf16[16,64,512]{2,1,0:T(8,128)(2,1)S(1)}, bf16[17,64,512]{2,1,0:T(8,128)(2,1)S(1)}, bf16[16,64,512]{2,1,0:T(8,128)(2,1)S(1)}, f32[8,64,1024]{2,1,0:T(8,128)S(1)}, f32[2,8,128]{2,1,0:T(8,128)S(1)}) custom-call(f32[2,1024,1024]{2,1,0:T(8,128)} %get-tuple-element.35.both_in, bf16[2,16,64,1024]{3,2,1,0:T(8,128)(2,1)} %get-tuple-element.36.student_in, ...), custom_call_target="tpu_custom_call" | custom-call | flops 4294967296 | bytes 20971520 | tf_op jit(solution)/shard_map/pallas_call | solution.py:369
  90.5 3.2 %collective-permute-start.30 = (bf16[17,64,512]{2,1,0:T(8,128)(2,1)S(1)}, bf16[17,64,512]{2,1,0:T(8,128)(2,1)S(1)}, u32[]{:S(2)}, u32[]{:S(2)}) collective-permute-start(bf16[17,64,512]{2,1,0:T(8,128)(2,1)S(1)} %get-tuple-element.40), channel_id=1, source_target_pairs={{0,16},{1,17},{2,18},{3,19},{4,20},{5,21},{6,22},{7,23},{8,24},{9,... | collective-permute-start | bytes 3342344 | tf_op jit(solution)/shard_map/ppermute | solution.py:32
  93.7 2.3 %collective-permute-done.30.got = bf16[17,64,512]{2,1,0:T(8,128)(2,1)S(1)} collective-permute-done((bf16[17,64,512]{2,1,0:T(8,128)(2,1)S(1)}, bf16[17,64,512]{2,1,0:T(8,128)(2,1)S(1)}, u32[]{:S(2)}, u32[]{:S(2)}) %collective-permute-start.30) | collective-permute-done | bytes 1114144 | tf_op jit(solution)/shard_map/ppermute | solution.py:32
  96.2 0.8 collective-permute-start.31
  97.7 2.7 %collective-permute-start.36 = (bf16[528,512]{1,0:T(8,128)(2,1)S(1)}, bf16[528,512]{1,0:T(8,128)(2,1)S(1)}, u32[]{:S(2)}, u32[]{:S(2)}) collective-permute-start(bf16[528,512]{1,0:T(8,128)(2,1)S(1)} %get-tuple-element.53), channel_id=1, source_target_pairs={{0,3},{1,0},{2,1},{3,2},{4,7},{5,4},{6,5},{7,6},{8,11},{9,8},{10,9... | collective-permute-start | bytes 1622024 | tf_op jit(solution)/shard_map/ppermute | solution.py:32
  100.4 0.5 collective-permute-start.37
  100.9 3.9 %collective-permute-done.31.k34 = bf16[208,1024]{1,0:T(8,128)(2,1)S(1)} collective-permute-done((bf16[208,1024]{1,0:T(8,128)(2,1)S(1)}, bf16[208,1024]{1,0:T(8,128)(2,1)S(1)}, u32[]{:S(2)}, u32[]{:S(2)}) %collective-permute-start.31) | collective-permute-done | bytes 426016 | tf_op jit(solution)/shard_map/ppermute | solution.py:32
  105.0 5.4 %collective-permute-start.32 = (bf16[144,1024]{1,0:T(8,128)(2,1)S(1)}, bf16[144,1024]{1,0:T(8,128)(2,1)S(1)}, u32[]{:S(2)}, u32[]{:S(2)}) collective-permute-start(bf16[144,1024]{1,0:T(8,128)(2,1)S(1)} %get-tuple-element.47), channel_id=1, source_target_pairs={{0,32},{1,33},{2,34},{3,35},{4,36},{5,37},{6,38},{7,39},{8,40},{9,... | collective-permute-start | bytes 884744 | tf_op jit(solution)/shard_map/ppermute | solution.py:32
  110.4 1.5 %collective-permute-start.33 = (bf16[144,1024]{1,0:T(8,128)(2,1)S(1)}, bf16[144,1024]{1,0:T(8,128)(2,1)S(1)}, u32[]{:S(2)}, u32[]{:S(2)}) collective-permute-start(bf16[144,1024]{1,0:T(8,128)(2,1)S(1)} %get-tuple-element.48), channel_id=1, source_target_pairs={{0,64},{1,65},{2,66},{3,67},{4,68},{5,69},{6,70},{7,71},{8,72},{9,... | collective-permute-start | bytes 884744 | tf_op jit(solution)/shard_map/ppermute | solution.py:32
  111.9 1.3 %collective-permute-done.35.p1 = bf16[528,512]{1,0:T(8,128)(2,1)S(1)} collective-permute-done((bf16[528,512]{1,0:T(8,128)(2,1)S(1)}, bf16[528,512]{1,0:T(8,128)(2,1)S(1)}, u32[]{:S(2)}, u32[]{:S(2)}) %collective-permute-start.35) | collective-permute-done | bytes 540704 | tf_op jit(solution)/shard_map/ppermute | solution.py:32
  113.5 0.8 collective-permute-start.38
  114.4 0.8 collective-permute-start.39
  115.2 2.7 %collective-permute-done.38.w1 = bf16[144,512]{1,0:T(8,128)(2,1)S(1)} collective-permute-done((bf16[144,512]{1,0:T(8,128)(2,1)S(1)}, bf16[144,512]{1,0:T(8,128)(2,1)S(1)}, u32[]{:S(2)}, u32[]{:S(2)}) %collective-permute-start.38) | collective-permute-done | bytes 147488 | tf_op jit(solution)/shard_map/ppermute | solution.py:32
  117.9 2.1 %collective-permute-done.39.w2 = bf16[144,512]{1,0:T(8,128)(2,1)S(1)} collective-permute-done((bf16[144,512]{1,0:T(8,128)(2,1)S(1)}, bf16[144,512]{1,0:T(8,128)(2,1)S(1)}, u32[]{:S(2)}, u32[]{:S(2)}) %collective-permute-start.39) | collective-permute-done | bytes 147488 | tf_op jit(solution)/shard_map/ppermute | solution.py:32
  120.0 1.8 %collective-permute-done.40.w3 = bf16[144,512]{1,0:T(8,128)(2,1)S(1)} collective-permute-done((bf16[144,512]{1,0:T(8,128)(2,1)S(1)}, bf16[144,512]{1,0:T(8,128)(2,1)S(1)}, u32[]{:S(2)}, u32[]{:S(2)}) %collective-permute-start.40) | collective-permute-done | bytes 147488 | tf_op jit(solution)/shard_map/ppermute | solution.py:32
  121.8 0.6 collective-permute-done.33.b2
  122.5 5.0 %collective-permute-start.41 = (bf16[80,1536]{1,0:T(8,128)(2,1)S(1)}, bf16[80,1536]{1,0:T(8,128)(2,1)S(1)}, u32[]{:S(2)}, u32[]{:S(2)}) collective-permute-start(bf16[80,1536]{1,0:T(8,128)(2,1)S(1)} %get-tuple-element.62), channel_id=1, source_target_pairs={{0,16},{1,17},{2,18},{3,19},{4,20},{5,21},{6,22},{7,23},{8,24},{9,... | collective-permute-start | bytes 737288 | tf_op jit(solution)/shard_map/ppermute | solution.py:32
  127.5 1.1 collective-permute-done.41.share
  128.7 0.8 shard_map.74
  (67 shorter events, 6.8 us)
Async XLA Ops:
  1.6 1.7 %collective-permute-start = (bf16[64,1024]{1,0:T(8,128)(2,1)S(1)}, bf16[64,1024]{1,0:T(8,128)(2,1)S(1)}, u32[]{:S(2)}, u32[]{:S(2)}) collective-permute-start(bf16[64,1024]{1,0:T(8,128)(2,1)S(1)} %get-tuple-element.78), channel_id=1, source_target_pairs={{0,16},{1,17},{2,18},{3,19},{4,20},{5,21},{6,22},{7,23},{8,24},{9,... | collective-permute-start | bytes 393224 | tf_op jit(solution)/shard_map/ppermute | solution.py:32
  2.4 5.5 %collective-permute-start.10 = (bf16[64,1024]{1,0:T(8,128)(2,1)}, bf16[64,1024]{1,0:T(8,128)(2,1)S(1)}, u32[]{:S(2)}, u32[]{:S(2)}) collective-permute-start(bf16[64,1024]{1,0:T(8,128)(2,1)} %param.5), channel_id=1, source_target_pairs={{0,16},{1,17},{2,18},{3,19},{4,20},{5,21},{6,22},{7,23},{8,24},{9,... | collective-permute-start | bytes 393224 | tf_op jit(solution)/shard_map/ppermute | solution.py:32
  2.5 5.4 %collective-permute-start.11 = (bf16[64,1024]{1,0:T(8,128)(2,1)}, bf16[64,1024]{1,0:T(8,128)(2,1)S(1)}, u32[]{:S(2)}, u32[]{:S(2)}) collective-permute-start(bf16[64,1024]{1,0:T(8,128)(2,1)} %param.7), channel_id=1, source_target_pairs={{0,16},{1,17},{2,18},{3,19},{4,20},{5,21},{6,22},{7,23},{8,24},{9,... | collective-permute-start | bytes 393224 | tf_op jit(solution)/shard_map/ppermute | solution.py:32
  3.4 7.1 %collective-permute-start.2 = (bf16[2,64,1024]{2,1,0:T(8,128)(2,1)S(1)}, bf16[2,64,1024]{2,1,0:T(8,128)(2,1)S(1)}, u32[]{:S(2)}, u32[]{:S(2)}) collective-permute-start(bf16[2,64,1024]{2,1,0:T(8,128)(2,1)S(1)} %get-tuple-element.76), channel_id=1, source_target_pairs={{0,2},{1,3},{2,0},{3,1},{4,6},{5,7},{6,4},{7,5},{8,10},{9,11},{10,... | collective-permute-start | bytes 786440 | tf_op jit(solution)/shard_map/ppermute | solution.py:32
  6.4 7.3 %collective-permute-start.1 = (bf16[2,64,1024]{2,1,0:T(8,128)(2,1)S(1)}, bf16[2,64,1024]{2,1,0:T(8,128)(2,1)S(1)}, u32[]{:S(2)}, u32[]{:S(2)}) collective-permute-start(bf16[2,64,1024]{2,1,0:T(8,128)(2,1)S(1)} %get-tuple-element.76), channel_id=1, source_target_pairs={{0,3},{1,0},{2,1},{3,2},{4,7},{5,4},{6,5},{7,6},{8,11},{9,8},{10,9... | collective-permute-start | bytes 786440 | tf_op jit(solution)/shard_map/ppermute | solution.py:32
  7.2 6.7 %collective-permute-start.3 = (bf16[2,64,1024]{2,1,0:T(8,128)(2,1)S(1)}, bf16[2,64,1024]{2,1,0:T(8,128)(2,1)S(1)}, u32[]{:S(2)}, u32[]{:S(2)}) collective-permute-start(bf16[2,64,1024]{2,1,0:T(8,128)(2,1)S(1)} %get-tuple-element.76), channel_id=1, source_target_pairs={{0,1},{1,2},{2,3},{3,0},{4,5},{5,6},{6,7},{7,4},{8,9},{9,10},{10,1... | collective-permute-start | bytes 786440 | tf_op jit(solution)/shard_map/ppermute | solution.py:32
  8.9 8.6 %collective-permute-start.12 = (bf16[2,2,64,1024]{3,2,1,0:T(8,128)(2,1)S(1)}, bf16[2,2,64,1024]{3,2,1,0:T(8,128)(2,1)S(1)}, u32[]{:S(2)}, u32[]{:S(2)}) collective-permute-start(bf16[2,2,64,1024]{3,2,1,0:T(8,128)(2,1)S(1)} %bitcast.28), channel_id=1, source_target_pairs={{0,32},{1,33},{2,34},{3,35},{4,36},{5,37},{6,38},{7,39},{8,40},{9,... | collective-permute-start | bytes 1572872 | tf_op jit(solution)/shard_map/ppermute | solution.py:32
  14.1 15.8 %collective-permute-start.5 = (bf16[2,4,64,1024]{3,2,1,0:T(8,128)(2,1)S(1)}, bf16[2,4,64,1024]{3,2,1,0:T(8,128)(2,1)S(1)}, u32[]{:S(2)}, u32[]{:S(2)}) collective-permute-start(bf16[2,4,64,1024]{3,2,1,0:T(8,128)(2,1)S(1)} %pad_maximum_fusion.1.line), channel_id=1, source_target_pairs={{0,12},{1,13},{2,14},{3,15},{4,0},{5,1},{6,2},{7,3},{8,4},{9,5},{1... | collective-permute-start | bytes 3145736 | tf_op jit(solution)/shard_map/ppermute | solution.py:32
  14.5 16.1 %collective-permute-start.4 = (bf16[2,4,64,1024]{3,2,1,0:T(8,128)(2,1)S(1)}, bf16[2,4,64,1024]{3,2,1,0:T(8,128)(2,1)S(1)}, u32[]{:S(2)}, u32[]{:S(2)}) collective-permute-start(bf16[2,4,64,1024]{3,2,1,0:T(8,128)(2,1)S(1)} %pad_maximum_fusion.1.line), channel_id=1, source_target_pairs={{0,4},{1,5},{2,6},{3,7},{4,8},{5,9},{6,10},{7,11},{8,12},{9,13},{1... | collective-permute-start | bytes 3145736 | tf_op jit(solution)/shard_map/ppermute | solution.py:32
  17.5 9.2 %collective-permute-start.13 = (bf16[2,2,64,1024]{3,2,1,0:T(8,128)(2,1)S(1)}, bf16[2,2,64,1024]{3,2,1,0:T(8,128)(2,1)S(1)}, u32[]{:S(2)}, u32[]{:S(2)}) collective-permute-start(bf16[2,2,64,1024]{3,2,1,0:T(8,128)(2,1)S(1)} %collective-permute-done.12.t1), channel_id=1, source_target_pairs={{0,32},{1,33},{2,34},{3,35},{4,36},{5,37},{6,38},{7,39},{8,40},{9,... | collective-permute-start | bytes 1572872 | tf_op jit(solution)/shard_map/ppermute | solution.py:32
  26.7 9.2 %collective-permute-start.14 = (bf16[2,2,64,1024]{3,2,1,0:T(8,128)(2,1)S(1)}, bf16[2,2,64,1024]{3,2,1,0:T(8,128)(2,1)S(1)}, u32[]{:S(2)}, u32[]{:S(2)}) collective-permute-start(bf16[2,2,64,1024]{3,2,1,0:T(8,128)(2,1)S(1)} %collective-permute-done.13.t2), channel_id=1, source_target_pairs={{0,32},{1,33},{2,34},{3,35},{4,36},{5,37},{6,38},{7,39},{8,40},{9,... | collective-permute-start | bytes 1572872 | tf_op jit(solution)/shard_map/ppermute | solution.py:32
  29.9 9.6 %collective-permute-start.7 = (bf16[2,2,64,1024]{3,2,1,0:T(8,128)(2,1)S(1)}, bf16[2,2,64,1024]{3,2,1,0:T(8,128)(2,1)S(1)}, u32[]{:S(2)}, u32[]{:S(2)}) collective-permute-start(bf16[2,2,64,1024]{3,2,1,0:T(8,128)(2,1)S(1)} %slice.213), channel_id=1, source_target_pairs={{0,12},{1,13},{2,14},{3,15},{4,0},{5,1},{6,2},{7,3},{8,4},{9,5},{1... | collective-permute-start | bytes 1572872 | tf_op jit(solution)/shard_map/ppermute | solution.py:32
  30.8 18.4 %collective-permute-start.8 = (bf16[3,4,64,1024]{3,2,1,0:T(8,128)(2,1)S(1)}, bf16[3,4,64,1024]{3,2,1,0:T(8,128)(2,1)S(1)}, u32[]{:S(2)}, u32[]{:S(2)}) collective-permute-start(bf16[3,4,64,1024]{3,2,1,0:T(8,128)(2,1)S(1)} %pad_maximum_fusion), channel_id=1, source_target_pairs={{0,16},{1,17},{2,18},{3,19},{4,20},{5,21},{6,22},{7,23},{8,24},{9,... | collective-permute-start | bytes 4718600 | tf_op jit(solution)/shard_map/ppermute | solution.py:32
  34.3 8.4 %collective-permute-start.6 = (bf16[2,2,64,1024]{3,2,1,0:T(8,128)(2,1)S(1)}, bf16[2,2,64,1024]{3,2,1,0:T(8,128)(2,1)S(1)}, u32[]{:S(2)}, u32[]{:S(2)}) collective-permute-start(bf16[2,2,64,1024]{3,2,1,0:T(8,128)(2,1)S(1)} %slice.212), channel_id=1, source_target_pairs={{0,4},{1,5},{2,6},{3,7},{4,8},{5,9},{6,10},{7,11},{8,12},{9,13},{1... | collective-permute-start | bytes 1572872 | tf_op jit(solution)/shard_map/ppermute | solution.py:32
  35.7 13.4 %collective-permute-start.16 = (bf16[2,2,2,64,1024]{4,3,2,1,0:T(8,128)(2,1)S(1)}, bf16[2,2,2,64,1024]{4,3,2,1,0:T(8,128)(2,1)S(1)}, u32[]{:S(2)}, u32[]{:S(2)}) collective-permute-start(bf16[2,2,2,64,1024]{4,3,2,1,0:T(8,128)(2,1)S(1)} %pad_maximum_fusion.2), channel_id=1, source_target_pairs={{0,16},{1,17},{2,18},{3,19},{4,20},{5,21},{6,22},{7,23},{8,24},{9,... | collective-permute-start | bytes 3145736 | tf_op jit(solution)/shard_map/ppermute | solution.py:32
  35.9 9.0 %collective-permute-start.15 = (bf16[2,64,1024]{2,1,0:T(8,128)(2,1)S(1)}, bf16[2,64,1024]{2,1,0:T(8,128)(2,1)S(1)}, u32[]{:S(2)}, u32[]{:S(2)}) collective-permute-start(bf16[2,64,1024]{2,1,0:T(8,128)(2,1)S(1)} %slice_bitcast_fusion), channel_id=1, source_target_pairs={{0,32},{1,33},{2,34},{3,35},{4,36},{5,37},{6,38},{7,39},{8,40},{9,... | collective-permute-start | bytes 786440 | tf_op jit(solution)/shard_map/ppermute | solution.py:32
  39.5 9.7 %collective-permute-start.17 = (bf16[2,2,64,1024]{3,2,1,0:T(8,128)(2,1)S(1)}, bf16[2,2,64,1024]{3,2,1,0:T(8,128)(2,1)S(1)}, u32[]{:S(2)}, u32[]{:S(2)}) collective-permute-start(bf16[2,2,64,1024]{3,2,1,0:T(8,128)(2,1)S(1)} %collective-permute-done.14.t3), channel_id=1, source_target_pairs={{0,16},{1,17},{2,18},{3,19},{4,20},{5,21},{6,22},{7,23},{8,24},{9,... | collective-permute-start | bytes 1572872 | tf_op jit(solution)/shard_map/ppermute | solution.py:32
  42.8 6.4 %collective-permute-start.9 = (bf16[4,64,1024]{2,1,0:T(8,128)(2,1)S(1)}, bf16[4,64,1024]{2,1,0:T(8,128)(2,1)S(1)}, u32[]{:S(2)}, u32[]{:S(2)}) collective-permute-start(bf16[4,64,1024]{2,1,0:T(8,128)(2,1)S(1)} %pad_maximum_fusion.3), channel_id=1, source_target_pairs={{0,16},{1,17},{2,18},{3,19},{4,20},{5,21},{6,22},{7,23},{8,24},{9,... | collective-permute-start | bytes 1572872 | tf_op jit(solution)/shard_map/ppermute | solution.py:32
  45.0 4.2 %collective-permute-start.18 = (bf16[2,64,1024]{2,1,0:T(8,128)(2,1)S(1)}, bf16[2,64,1024]{2,1,0:T(8,128)(2,1)S(1)}, u32[]{:S(2)}, u32[]{:S(2)}) collective-permute-start(bf16[2,64,1024]{2,1,0:T(8,128)(2,1)S(1)} %collective-permute-done.15.far), channel_id=1, source_target_pairs={{0,16},{1,17},{2,18},{3,19},{4,20},{5,21},{6,22},{7,23},{8,24},{9,... | collective-permute-start | bytes 786440 | tf_op jit(solution)/shard_map/ppermute | solution.py:32
  59.3 5.8 %collective-permute-start.27 = (f32[8,1024]{1,0:T(8,128)S(1)}, f32[8,1024]{1,0:T(8,128)S(1)}, u32[]{:S(2)}, u32[]{:S(2)}) collective-permute-start(f32[8,1024]{1,0:T(8,128)S(1)} %get-tuple-element.38), channel_id=1, source_target_pairs={{0,96},{1,97},{2,98},{3,99},{4,100},{5,101},{6,102},{7,103},{8,104... | collective-permute-start | bytes 98312 | tf_op jit(solution)/shard_map/ppermute | solution.py:32
  59.8 7.9 %collective-permute-start.26 = (f32[8,1024]{1,0:T(8,128)S(1)}, f32[8,1024]{1,0:T(8,128)S(1)}, u32[]{:S(2)}, u32[]{:S(2)}) collective-permute-start(f32[8,1024]{1,0:T(8,128)S(1)} %get-tuple-element.38), channel_id=1, source_target_pairs={{0,64},{1,65},{2,66},{3,67},{4,68},{5,69},{6,70},{7,71},{8,72},{9,... | collective-permute-start | bytes 98312 | tf_op jit(solution)/shard_map/ppermute | solution.py:32
  64.4 3.3 %collective-permute-start.25 = (f32[8,1024]{1,0:T(8,128)S(1)}, f32[8,1024]{1,0:T(8,128)S(1)}, u32[]{:S(2)}, u32[]{:S(2)}) collective-permute-start(f32[8,1024]{1,0:T(8,128)S(1)} %get-tuple-element.38), channel_id=1, source_target_pairs={{0,32},{1,33},{2,34},{3,35},{4,36},{5,37},{6,38},{7,39},{8,40},{9,... | collective-permute-start | bytes 98312 | tf_op jit(solution)/shard_map/ppermute | solution.py:32
  64.4 7.8 %collective-permute-start.21 = (f32[8,1024]{1,0:T(8,128)S(1)}, f32[8,1024]{1,0:T(8,128)S(1)}, u32[]{:S(2)}, u32[]{:S(2)}) collective-permute-start(f32[8,1024]{1,0:T(8,128)S(1)} %get-tuple-element.37), channel_id=1, source_target_pairs={{0,3},{1,2},{2,1},{3,0},{4,7},{5,6},{6,5},{7,4},{8,11},{9,10},{10,... | collective-permute-start | bytes 98312 | tf_op jit(solution)/shard_map/ppermute | solution.py:32
  65.0 7.2 %collective-permute-start.20 = (f32[8,1024]{1,0:T(8,128)S(1)}, f32[8,1024]{1,0:T(8,128)S(1)}, u32[]{:S(2)}, u32[]{:S(2)}) collective-permute-start(f32[8,1024]{1,0:T(8,128)S(1)} %get-tuple-element.37), channel_id=1, source_target_pairs={{0,2},{1,3},{2,0},{3,1},{4,6},{5,7},{6,4},{7,5},{8,10},{9,11},{10,... | collective-permute-start | bytes 98312 | tf_op jit(solution)/shard_map/ppermute | solution.py:32
  65.1 7.2 %collective-permute-start.19 = (f32[8,1024]{1,0:T(8,128)S(1)}, f32[8,1024]{1,0:T(8,128)S(1)}, u32[]{:S(2)}, u32[]{:S(2)}) collective-permute-start(f32[8,1024]{1,0:T(8,128)S(1)} %get-tuple-element.37), channel_id=1, source_target_pairs={{0,1},{1,0},{2,3},{3,2},{4,5},{5,4},{6,7},{7,6},{8,9},{9,8},{10,11... | collective-permute-start | bytes 98312 | tf_op jit(solution)/shard_map/ppermute | solution.py:32
  67.9 8.1 %collective-permute-start.28 = (f32[5,1024]{1,0:T(8,128)S(1)}, f32[5,1024]{1,0:T(8,128)S(1)}, u32[]{:S(2)}, u32[]{:S(2)}) collective-permute-start(f32[5,1024]{1,0:T(8,128)S(1)} %concatenate.14), channel_id=1, source_target_pairs={{0,128},{1,129},{2,130},{3,131},{4,132},{5,133},{6,134},{7,135},{8... | collective-permute-start | bytes 61448 | tf_op jit(solution)/shard_map/ppermute | solution.py:32
  72.4 6.6 %collective-permute-start.24 = (f32[5,1024]{1,0:T(8,128)S(1)}, f32[5,1024]{1,0:T(8,128)S(1)}, u32[]{:S(2)}, u32[]{:S(2)}) collective-permute-start(f32[5,1024]{1,0:T(8,128)S(1)} %concatenate.13.ra), channel_id=1, source_target_pairs={{0,12},{1,13},{2,14},{3,15},{4,8},{5,9},{6,10},{7,11},{8,4},{9,5},... | collective-permute-start | bytes 61448 | tf_op jit(solution)/shard_map/ppermute | solution.py:32
  75.2 4.3 %collective-permute-start.23 = (f32[5,1024]{1,0:T(8,128)S(1)}, f32[5,1024]{1,0:T(8,128)S(1)}, u32[]{:S(2)}, u32[]{:S(2)}) collective-permute-start(f32[5,1024]{1,0:T(8,128)S(1)} %concatenate.13.ra), channel_id=1, source_target_pairs={{0,8},{1,9},{2,10},{3,11},{4,12},{5,13},{6,14},{7,15},{8,0},{9,1},... | collective-permute-start | bytes 61448 | tf_op jit(solution)/shard_map/ppermute | solution.py:32
  75.6 3.9 %collective-permute-start.22 = (f32[5,1024]{1,0:T(8,128)S(1)}, f32[5,1024]{1,0:T(8,128)S(1)}, u32[]{:S(2)}, u32[]{:S(2)}) collective-permute-start(f32[5,1024]{1,0:T(8,128)S(1)} %concatenate.13.ra), channel_id=1, source_target_pairs={{0,4},{1,5},{2,6},{3,7},{4,0},{5,1},{6,2},{7,3},{8,12},{9,13},{10,... | collective-permute-start | bytes 61448 | tf_op jit(solution)/shard_map/ppermute | solution.py:32
  76.0 3.9 %collective-permute-start.29 = (f32[5,1024]{1,0:T(8,128)S(1)}, f32[5,1024]{1,0:T(8,128)S(1)}, u32[]{:S(2)}, u32[]{:S(2)}) collective-permute-start(f32[5,1024]{1,0:T(8,128)S(1)} %concatenate.15.ca), channel_id=1, source_target_pairs={{0,16},{1,17},{2,18},{3,19},{4,20},{5,21},{6,22},{7,23},{8,24},{9,... | collective-permute-start | bytes 61448 | tf_op jit(solution)/shard_map/ppermute | solution.py:32
  90.5 5.5 %collective-permute-start.30 = (bf16[17,64,512]{2,1,0:T(8,128)(2,1)S(1)}, bf16[17,64,512]{2,1,0:T(8,128)(2,1)S(1)}, u32[]{:S(2)}, u32[]{:S(2)}) collective-permute-start(bf16[17,64,512]{2,1,0:T(8,128)(2,1)S(1)} %get-tuple-element.40), channel_id=1, source_target_pairs={{0,16},{1,17},{2,18},{3,19},{4,20},{5,21},{6,22},{7,23},{8,24},{9,... | collective-permute-start | bytes 3342344 | tf_op jit(solution)/shard_map/ppermute | solution.py:32
  93.6 3.9 %collective-permute-start.34 = (bf16[16,64,512]{2,1,0:T(8,128)(2,1)S(1)}, bf16[16,64,512]{2,1,0:T(8,128)(2,1)S(1)}, u32[]{:S(2)}, u32[]{:S(2)}) collective-permute-start(bf16[16,64,512]{2,1,0:T(8,128)(2,1)S(1)} %get-tuple-element.50), channel_id=1, source_target_pairs={{0,16},{1,17},{2,18},{3,19},{4,20},{5,21},{6,22},{7,23},{8,24},{9,... | collective-permute-start | bytes 3145736 | tf_op jit(solution)/shard_map/ppermute | solution.py:32
  96.2 8.7 %collective-permute-start.31 = (bf16[208,1024]{1,0:T(8,128)(2,1)S(1)}, bf16[208,1024]{1,0:T(8,128)(2,1)S(1)}, u32[]{:S(2)}, u32[]{:S(2)}) collective-permute-start(bf16[208,1024]{1,0:T(8,128)(2,1)S(1)} %get-tuple-element.45), channel_id=1, source_target_pairs={{0,64},{1,65},{2,66},{3,67},{4,68},{5,69},{6,70},{7,71},{8,72},{9,... | collective-permute-start | bytes 1277960 | tf_op jit(solution)/shard_map/ppermute | solution.py:32
  97.6 15.6 %collective-permute-start.35 = (bf16[528,512]{1,0:T(8,128)(2,1)S(1)}, bf16[528,512]{1,0:T(8,128)(2,1)S(1)}, u32[]{:S(2)}, u32[]{:S(2)}) collective-permute-start(bf16[528,512]{1,0:T(8,128)(2,1)S(1)} %get-tuple-element.52), channel_id=1, source_target_pairs={{0,1},{1,2},{2,3},{3,0},{4,5},{5,6},{6,7},{7,4},{8,9},{9,10},{10,1... | collective-permute-start | bytes 1622024 | tf_op jit(solution)/shard_map/ppermute | solution.py:32
  97.7 15.5 %collective-permute-start.36 = (bf16[528,512]{1,0:T(8,128)(2,1)S(1)}, bf16[528,512]{1,0:T(8,128)(2,1)S(1)}, u32[]{:S(2)}, u32[]{:S(2)}) collective-permute-start(bf16[528,512]{1,0:T(8,128)(2,1)S(1)} %get-tuple-element.53), channel_id=1, source_target_pairs={{0,3},{1,0},{2,1},{3,2},{4,7},{5,4},{6,5},{7,6},{8,11},{9,8},{10,9... | collective-permute-start | bytes 1622024 | tf_op jit(solution)/shard_map/ppermute | solution.py:32
  100.4 12.8 %collective-permute-start.37 = (bf16[528,512]{1,0:T(8,128)(2,1)S(1)}, bf16[528,512]{1,0:T(8,128)(2,1)S(1)}, u32[]{:S(2)}, u32[]{:S(2)}) collective-permute-start(bf16[528,512]{1,0:T(8,128)(2,1)S(1)} %get-tuple-element.54), channel_id=1, source_target_pairs={{0,2},{1,3},{2,0},{3,1},{4,6},{5,7},{6,4},{7,5},{8,10},{9,11},{10,... | collective-permute-start | bytes 1622024 | tf_op jit(solution)/shard_map/ppermute | solution.py:32
  105.0 16.8 %collective-permute-start.32 = (bf16[144,1024]{1,0:T(8,128)(2,1)S(1)}, bf16[144,1024]{1,0:T(8,128)(2,1)S(1)}, u32[]{:S(2)}, u32[]{:S(2)}) collective-permute-start(bf16[144,1024]{1,0:T(8,128)(2,1)S(1)} %get-tuple-element.47), channel_id=1, source_target_pairs={{0,32},{1,33},{2,34},{3,35},{4,36},{5,37},{6,38},{7,39},{8,40},{9,... | collective-permute-start | bytes 884744 | tf_op jit(solution)/shard_map/ppermute | solution.py:32
  110.4 11.9 %collective-permute-start.33 = (bf16[144,1024]{1,0:T(8,128)(2,1)S(1)}, bf16[144,1024]{1,0:T(8,128)(2,1)S(1)}, u32[]{:S(2)}, u32[]{:S(2)}) collective-permute-start(bf16[144,1024]{1,0:T(8,128)(2,1)S(1)} %get-tuple-element.48), channel_id=1, source_target_pairs={{0,64},{1,65},{2,66},{3,67},{4,68},{5,69},{6,70},{7,71},{8,72},{9,... | collective-permute-start | bytes 884744 | tf_op jit(solution)/shard_map/ppermute | solution.py:32
  113.5 4.4 %collective-permute-start.38 = (bf16[144,512]{1,0:T(8,128)(2,1)S(1)}, bf16[144,512]{1,0:T(8,128)(2,1)S(1)}, u32[]{:S(2)}, u32[]{:S(2)}) collective-permute-start(bf16[144,512]{1,0:T(8,128)(2,1)S(1)} %get-tuple-element.56), channel_id=1, source_target_pairs={{0,4},{1,5},{2,6},{3,7},{4,8},{5,9},{6,10},{7,11},{8,12},{9,13},{1... | collective-permute-start | bytes 442376 | tf_op jit(solution)/shard_map/ppermute | solution.py:32
  114.4 5.6 %collective-permute-start.39 = (bf16[144,512]{1,0:T(8,128)(2,1)S(1)}, bf16[144,512]{1,0:T(8,128)(2,1)S(1)}, u32[]{:S(2)}, u32[]{:S(2)}) collective-permute-start(bf16[144,512]{1,0:T(8,128)(2,1)S(1)} %get-tuple-element.57), channel_id=1, source_target_pairs={{0,8},{1,9},{2,10},{3,11},{4,12},{5,13},{6,14},{7,15},{8,0},{9,1},... | collective-permute-start | bytes 442376 | tf_op jit(solution)/shard_map/ppermute | solution.py:32
  115.2 6.5 %collective-permute-start.40 = (bf16[144,512]{1,0:T(8,128)(2,1)S(1)}, bf16[144,512]{1,0:T(8,128)(2,1)S(1)}, u32[]{:S(2)}, u32[]{:S(2)}) collective-permute-start(bf16[144,512]{1,0:T(8,128)(2,1)S(1)} %get-tuple-element.58), channel_id=1, source_target_pairs={{0,12},{1,13},{2,14},{3,15},{4,0},{5,1},{6,2},{7,3},{8,4},{9,5},{1... | collective-permute-start | bytes 442376 | tf_op jit(solution)/shard_map/ppermute | solution.py:32
  122.5 6.2 %collective-permute-start.41 = (bf16[80,1536]{1,0:T(8,128)(2,1)S(1)}, bf16[80,1536]{1,0:T(8,128)(2,1)S(1)}, u32[]{:S(2)}, u32[]{:S(2)}) collective-permute-start(bf16[80,1536]{1,0:T(8,128)(2,1)S(1)} %get-tuple-element.62), channel_id=1, source_target_pairs={{0,16},{1,17},{2,18},{3,19},{4,20},{5,21},{6,22},{7,23},{8,24},{9,... | collective-permute-start | bytes 737288 | tf_op jit(solution)/shard_map/ppermute | solution.py:32

commit v5 on v4

--- a/solution.py
+++ b/solution.py
@@ -478,7 +478,7 @@
     return (own + choose(odd, ahead, back)) + (far + choose(odd, back, ahead))
 
 
-def line_kernel(own, p1, m1, far, loss_part, out, w1, w2, w3, cols_loss):
+def line_kernel(own, far, p1, m1, loss_part, out, w1, w2, w3, cols_loss):
     _, c, y, x = position()
     n, h = own.shape[2:]
     for k, ref in enumerate((out, w1, w2, w3)):
@@ -496,7 +496,7 @@
 
 
 def last_kernel(
-    text_own, b1, b2, k34, rows_loss, line, w1, w2, w3, cols_loss,
+    text_own, b1, b2, k34, rows_loss, line, w2, w1, w3, cols_loss,
     text, image, share, loss,
 ):
     _, c, y, x = position()
@@ -563,7 +563,7 @@
     line, w1, w2, w3, cols_loss = vmem_call(
         line_kernel,
         [((2 * n, h), F32)] + [((2 * n + 16, h), BF)] * 3 + [small],
-        (image_own, p1, m1, far, loss_part),
+        (image_own, far, p1, m1, loss_part),
     )
     w1 = move_second(w1, 1)
     w2 = move_second(w2, 2)
@@ -571,7 +571,7 @@
     text, image, share, loss = vmem_call(
         last_kernel,
         [((n, d), F32), ((n, h), BF), ((n + 16, d + h), BF), ((2, 8, LANES), F32)],
-        (text_own, b1, b2, k34, rows_loss, line, w1, w2, w3, cols_loss),
+        (text_own, b1, b2, k34, rows_loss, line, w2, w1, w3, cols_loss),
     )
     vmem = pl.BlockSpec(memory_space=pltpu.VMEM)
     scale = 0.5 / (n * NX * NY * NZ * NC)

time: 130 us -> 130 us (level)
  starting transfers between devices: 70.4 us -> 72.6 us
  waiting for transfers between devices: 32.7 us -> 30.6 us
    ppermute x42, starting transfers between devices: 70.4 us -> 72.6 us  [send(): return lax.ppermute(v, ('row', 'col'), pairs)]
    ppermute x42, waiting for transfers between devices: 32.7 us -> 30.6 us  [send(): return lax.ppermute(v, ('row', 'col'), pairs)]
  transfers between devices with their start and end apart: 42 -> 42, of which waited for: 21 -> 20; matrix products, arithmetic and copies ran while one was open for 2% -> 2% of each run, Pallas kernels for 1% -> 1%
where the time goes in v5:
time: 130 us
  starting transfers between devices  72.6 us (56%)
  waiting for transfers between devices  30.6 us (24%)
  Pallas kernels  22.3 us (17%)
  other arithmetic  2.8 us (2%)
    ppermute x42, starting transfers between devices, send(): return lax.ppermute(v, ('row', 'col'), pairs)  72.6 us
    ppermute x42, waiting for transfers between devices, send(): return lax.ppermute(v, ('row', 'col'), pairs)  30.6 us
    pallas_call x1, Pallas kernels, pass_2(): pl.pallas_call(pass_2_kernel, out_shape=(jax.ShapeDtypeStruct((16, n, d /...  10.5 us
    pallas_call x1, Pallas kernels, pass_1(): pl.pallas_call(pass_1_kernel, out_shape=(both, blocks, small, small), in_...  10.1 us
  transfers between devices with their start and end apart: 42, of which 20 were waited for; matrix products, arithmetic and copies ran while one was open for 2% of the time, Pallas kernels for 1%

profile of v5, /device:TPU:39, one launch (start us, length us, event | category | flops | bytes accessed | tf_op | source)
XLA Modules:
  0.0 129.6 jit_solution(1589631100669631396)
XLA Ops:
  0.6 1.0 select_bitcast_fusion
  1.6 0.8 collective-permute-start
  3.4 3.0 %collective-permute-start.2 = (bf16[2,64,1024]{2,1,0:T(8,128)(2,1)S(1)}, bf16[2,64,1024]{2,1,0:T(8,128)(2,1)S(1)}, u32[]{:S(2)}, u32[]{:S(2)}) collective-permute-start(bf16[2,64,1024]{2,1,0:T(8,128)(2,1)S(1)} %get-tuple-element.76), channel_id=1, source_target_pairs={{0,2},{1,3},{2,0},{3,1},{4,6},{5,7},{6,4},{7,5},{8,10},{9,11},{10,... | collective-permute-start | bytes 786440 | tf_op jit(solution)/shard_map/ppermute | solution.py:32
  6.4 0.8 collective-permute-start.1
  7.2 0.7 collective-permute-start.3
  7.9 1.0 pad_maximum_fusion.4
  9.0 1.5 %collective-permute-done.2 = bf16[2,64,1024]{2,1,0:T(8,128)(2,1)S(1)} collective-permute-done((bf16[2,64,1024]{2,1,0:T(8,128)(2,1)S(1)}, bf16[2,64,1024]{2,1,0:T(8,128)(2,1)S(1)}, u32[]{:S(2)}, u32[]{:S(2)}) %collective-permute-start.2) | collective-permute-done | bytes 262176 | tf_op jit(solution)/shard_map/ppermute | solution.py:32
  10.5 3.2 %collective-permute-done.1 = bf16[2,64,1024]{2,1,0:T(8,128)(2,1)S(1)} collective-permute-done((bf16[2,64,1024]{2,1,0:T(8,128)(2,1)S(1)}, bf16[2,64,1024]{2,1,0:T(8,128)(2,1)S(1)}, u32[]{:S(2)}, u32[]{:S(2)}) %collective-permute-start.1) | collective-permute-done | bytes 262176 | tf_op jit(solution)/shard_map/ppermute | solution.py:32
  14.5 2.3 %collective-permute-start.4 = (bf16[2,4,64,1024]{3,2,1,0:T(8,128)(2,1)S(1)}, bf16[2,4,64,1024]{3,2,1,0:T(8,128)(2,1)S(1)}, u32[]{:S(2)}, u32[]{:S(2)}) collective-permute-start(bf16[2,4,64,1024]{3,2,1,0:T(8,128)(2,1)S(1)} %pad_maximum_fusion.1.line), channel_id=1, source_target_pairs={{0,4},{1,5},{2,6},{3,7},{4,8},{5,9},{6,10},{7,11},{8,12},{9,13},{1... | collective-permute-start | bytes 3145736 | tf_op jit(solution)/shard_map/ppermute | solution.py:32
  16.8 0.7 collective-permute-done.12.t1
  17.5 3.0 %collective-permute-start.13 = (bf16[2,2,64,1024]{3,2,1,0:T(8,128)(2,1)S(1)}, bf16[2,2,64,1024]{3,2,1,0:T(8,128)(2,1)S(1)}, u32[]{:S(2)}, u32[]{:S(2)}) collective-permute-start(bf16[2,2,64,1024]{3,2,1,0:T(8,128)(2,1)S(1)} %collective-permute-done.12.t1), channel_id=1, source_target_pairs={{0,32},{1,33},{2,34},{3,35},{4,36},{5,37},{6,38},{7,39},{8,40},{9,... | collective-permute-start | bytes 1572872 | tf_op jit(solution)/shard_map/ppermute | solution.py:32
  20.5 6.1 %collective-permute-done.13.t2 = bf16[2,2,64,1024]{3,2,1,0:T(8,128)(2,1)S(1)} collective-permute-done((bf16[2,2,64,1024]{3,2,1,0:T(8,128)(2,1)S(1)}, bf16[2,2,64,1024]{3,2,1,0:T(8,128)(2,1)S(1)}, u32[]{:S(2)}, u32[]{:S(2)}) %collective-permute-start.13) | collective-permute-done | bytes 524320 | tf_op jit(solution)/shard_map/ppermute | solution.py:32
  26.7 3.1 %collective-permute-start.14 = (bf16[2,2,64,1024]{3,2,1,0:T(8,128)(2,1)S(1)}, bf16[2,2,64,1024]{3,2,1,0:T(8,128)(2,1)S(1)}, u32[]{:S(2)}, u32[]{:S(2)}) collective-permute-start(bf16[2,2,64,1024]{3,2,1,0:T(8,128)(2,1)S(1)} %collective-permute-done.13.t2), channel_id=1, source_target_pairs={{0,32},{1,33},{2,34},{3,35},{4,36},{5,37},{6,38},{7,39},{8,40},{9,... | collective-permute-start | bytes 1572872 | tf_op jit(solution)/shard_map/ppermute | solution.py:32
  29.9 0.6 collective-permute-start.7
  30.8 3.5 %collective-permute-start.8 = (bf16[3,4,64,1024]{3,2,1,0:T(8,128)(2,1)S(1)}, bf16[3,4,64,1024]{3,2,1,0:T(8,128)(2,1)S(1)}, u32[]{:S(2)}, u32[]{:S(2)}) collective-permute-start(bf16[3,4,64,1024]{3,2,1,0:T(8,128)(2,1)S(1)} %pad_maximum_fusion), channel_id=1, source_target_pairs={{0,16},{1,17},{2,18},{3,19},{4,20},{5,21},{6,22},{7,23},{8,24},{9,... | collective-permute-start | bytes 4718600 | tf_op jit(solution)/shard_map/ppermute | solution.py:32
  34.3 1.3 %collective-permute-start.6 = (bf16[2,2,64,1024]{3,2,1,0:T(8,128)(2,1)S(1)}, bf16[2,2,64,1024]{3,2,1,0:T(8,128)(2,1)S(1)}, u32[]{:S(2)}, u32[]{:S(2)}) collective-permute-start(bf16[2,2,64,1024]{3,2,1,0:T(8,128)(2,1)S(1)} %slice.212), channel_id=1, source_target_pairs={{0,4},{1,5},{2,6},{3,7},{4,8},{5,9},{6,10},{7,11},{8,12},{9,13},{1... | collective-permute-start | bytes 1572872 | tf_op jit(solution)/shard_map/ppermute | solution.py:32
  35.9 3.5 %collective-permute-start.15 = (bf16[2,64,1024]{2,1,0:T(8,128)(2,1)S(1)}, bf16[2,64,1024]{2,1,0:T(8,128)(2,1)S(1)}, u32[]{:S(2)}, u32[]{:S(2)}) collective-permute-start(bf16[2,64,1024]{2,1,0:T(8,128)(2,1)S(1)} %slice_bitcast_fusion), channel_id=1, source_target_pairs={{0,32},{1,33},{2,34},{3,35},{4,36},{5,37},{6,38},{7,39},{8,40},{9,... | collective-permute-start | bytes 786440 | tf_op jit(solution)/shard_map/ppermute | solution.py:32
  39.5 1.2 collective-permute-start.17
  40.7 2.0 %collective-permute-done.6.far_a = bf16[2,2,64,1024]{3,2,1,0:T(8,128)(2,1)S(1)} collective-permute-done((bf16[2,2,64,1024]{3,2,1,0:T(8,128)(2,1)S(1)}, bf16[2,2,64,1024]{3,2,1,0:T(8,128)(2,1)S(1)}, u32[]{:S(2)}, u32[]{:S(2)}) %collective-permute-start.6) | collective-permute-done | bytes 524320 | tf_op jit(solution)/shard_map/ppermute | solution.py:32
  42.8 2.2 %collective-permute-start.9 = (bf16[4,64,1024]{2,1,0:T(8,128)(2,1)S(1)}, bf16[4,64,1024]{2,1,0:T(8,128)(2,1)S(1)}, u32[]{:S(2)}, u32[]{:S(2)}) collective-permute-start(bf16[4,64,1024]{2,1,0:T(8,128)(2,1)S(1)} %pad_maximum_fusion.3), channel_id=1, source_target_pairs={{0,16},{1,17},{2,18},{3,19},{4,20},{5,21},{6,22},{7,23},{8,24},{9,... | collective-permute-start | bytes 1572872 | tf_op jit(solution)/shard_map/ppermute | solution.py:32
  45.0 3.0 %collective-permute-start.18 = (bf16[2,64,1024]{2,1,0:T(8,128)(2,1)S(1)}, bf16[2,64,1024]{2,1,0:T(8,128)(2,1)S(1)}, u32[]{:S(2)}, u32[]{:S(2)}) collective-permute-start(bf16[2,64,1024]{2,1,0:T(8,128)(2,1)S(1)} %collective-permute-done.15.far), channel_id=1, source_target_pairs={{0,16},{1,17},{2,18},{3,19},{4,20},{5,21},{6,22},{7,23},{8,24},{9,... | collective-permute-start | bytes 786440 | tf_op jit(solution)/shard_map/ppermute | solution.py:32
  48.0 1.2 collective-permute-done.18.far_sib
  49.2 10.1 %shard_map.67 = (f32[2,1024,1024]{2,1,0:T(8,128)}, bf16[2,16,64,1024]{3,2,1,0:T(8,128)(2,1)}, f32[8,1024]{1,0:T(8,128)S(1)}, f32[8,1024]{1,0:T(8,128)S(1)}) custom-call(bf16[2,4,64,1024]{3,2,1,0:T(8,128)(2,1)S(1)} %pad_maximum_fusion.1.line, bf16[2,4,64,1024]{3,2,1,0:T(8,128)(2,1)S(1)} %collective-permute-done.4.up, ...), custom_call_target="tpu_custom_call" | custom-call | flops 4294967296 | bytes 20971520 | tf_op jit(solution)/shard_map/pallas_call | solution.py:208
  59.3 0.5 collective-permute-start.27
  59.8 4.6 %collective-permute-start.26 = (f32[8,1024]{1,0:T(8,128)S(1)}, f32[8,1024]{1,0:T(8,128)S(1)}, u32[]{:S(2)}, u32[]{:S(2)}) collective-permute-start(f32[8,1024]{1,0:T(8,128)S(1)} %get-tuple-element.38), channel_id=1, source_target_pairs={{0,64},{1,65},{2,66},{3,67},{4,68},{5,69},{6,70},{7,71},{8,72},{9,... | collective-permute-start | bytes 98312 | tf_op jit(solution)/shard_map/ppermute | solution.py:32
  64.4 0.6 collective-permute-start.21
  65.1 2.6 %collective-permute-start.19 = (f32[8,1024]{1,0:T(8,128)S(1)}, f32[8,1024]{1,0:T(8,128)S(1)}, u32[]{:S(2)}, u32[]{:S(2)}) collective-permute-start(f32[8,1024]{1,0:T(8,128)S(1)} %get-tuple-element.37), channel_id=1, source_target_pairs={{0,1},{1,0},{2,3},{3,2},{4,5},{5,4},{6,7},{7,6},{8,9},{9,8},{10,11... | collective-permute-start | bytes 98312 | tf_op jit(solution)/shard_map/ppermute | solution.py:32
  67.9 4.4 %collective-permute-start.28 = (f32[5,1024]{1,0:T(8,128)S(1)}, f32[5,1024]{1,0:T(8,128)S(1)}, u32[]{:S(2)}, u32[]{:S(2)}) collective-permute-start(f32[5,1024]{1,0:T(8,128)S(1)} %concatenate.14), channel_id=1, source_target_pairs={{0,128},{1,129},{2,130},{3,131},{4,132},{5,133},{6,134},{7,135},{8... | collective-permute-start | bytes 61448 | tf_op jit(solution)/shard_map/ppermute | solution.py:32
  72.4 2.8 %collective-permute-start.24 = (f32[5,1024]{1,0:T(8,128)S(1)}, f32[5,1024]{1,0:T(8,128)S(1)}, u32[]{:S(2)}, u32[]{:S(2)}) collective-permute-start(f32[5,1024]{1,0:T(8,128)S(1)} %concatenate.13.ra), channel_id=1, source_target_pairs={{0,12},{1,13},{2,14},{3,15},{4,8},{5,9},{6,10},{7,11},{8,4},{9,5},... | collective-permute-start | bytes 61448 | tf_op jit(solution)/shard_map/ppermute | solution.py:32
  76.0 3.0 %collective-permute-start.29 = (f32[5,1024]{1,0:T(8,128)S(1)}, f32[5,1024]{1,0:T(8,128)S(1)}, u32[]{:S(2)}, u32[]{:S(2)}) collective-permute-start(f32[5,1024]{1,0:T(8,128)S(1)} %concatenate.15.ca), channel_id=1, source_target_pairs={{0,16},{1,17},{2,18},{3,19},{4,20},{5,21},{6,22},{7,23},{8,24},{9,... | collective-permute-start | bytes 61448 | tf_op jit(solution)/shard_map/ppermute | solution.py:32
  79.9 10.5 %shard_map.68 = (bf16[16,64,512]{2,1,0:T(8,128)(2,1)S(1)}, bf16[17,64,512]{2,1,0:T(8,128)(2,1)S(1)}, bf16[16,64,512]{2,1,0:T(8,128)(2,1)S(1)}, f32[8,64,1024]{2,1,0:T(8,128)S(1)}, f32[2,8,128]{2,1,0:T(8,128)S(1)}) custom-call(f32[2,1024,1024]{2,1,0:T(8,128)} %get-tuple-element.35.both_in, bf16[2,16,64,1024]{3,2,1,0:T(8,128)(2,1)} %get-tuple-element.36.student_in, ...), custom_call_target="tpu_custom_call" | custom-call | flops 4294967296 | bytes 20971520 | tf_op jit(solution)/shard_map/pallas_call | solution.py:369
  90.5 3.2 %collective-permute-start.30 = (bf16[17,64,512]{2,1,0:T(8,128)(2,1)S(1)}, bf16[17,64,512]{2,1,0:T(8,128)(2,1)S(1)}, u32[]{:S(2)}, u32[]{:S(2)}) collective-permute-start(bf16[17,64,512]{2,1,0:T(8,128)(2,1)S(1)} %get-tuple-element.40), channel_id=1, source_target_pairs={{0,16},{1,17},{2,18},{3,19},{4,20},{5,21},{6,22},{7,23},{8,24},{9,... | collective-permute-start | bytes 3342344 | tf_op jit(solution)/shard_map/ppermute | solution.py:32
  93.7 2.3 %collective-permute-done.30.got = bf16[17,64,512]{2,1,0:T(8,128)(2,1)S(1)} collective-permute-done((bf16[17,64,512]{2,1,0:T(8,128)(2,1)S(1)}, bf16[17,64,512]{2,1,0:T(8,128)(2,1)S(1)}, u32[]{:S(2)}, u32[]{:S(2)}) %collective-permute-start.30) | collective-permute-done | bytes 1114144 | tf_op jit(solution)/shard_map/ppermute | solution.py:32
  96.2 0.8 collective-permute-start.31
  97.0 0.5 collective-permute-done.34.got
  97.6 1.8 %collective-permute-start.35 = (bf16[528,512]{1,0:T(8,128)(2,1)S(1)}, bf16[528,512]{1,0:T(8,128)(2,1)S(1)}, u32[]{:S(2)}, u32[]{:S(2)}) collective-permute-start(bf16[528,512]{1,0:T(8,128)(2,1)S(1)} %get-tuple-element.52), channel_id=1, source_target_pairs={{0,2},{1,3},{2,0},{3,1},{4,6},{5,7},{6,4},{7,5},{8,10},{9,11},{10,... | collective-permute-start | bytes 1622024 | tf_op jit(solution)/shard_map/ppermute | solution.py:32
  99.5 2.7 %collective-permute-start.37 = (bf16[528,512]{1,0:T(8,128)(2,1)S(1)}, bf16[528,512]{1,0:T(8,128)(2,1)S(1)}, u32[]{:S(2)}, u32[]{:S(2)}) collective-permute-start(bf16[528,512]{1,0:T(8,128)(2,1)S(1)} %get-tuple-element.54), channel_id=1, source_target_pairs={{0,3},{1,0},{2,1},{3,2},{4,7},{5,4},{6,5},{7,6},{8,11},{9,8},{10,9... | collective-permute-start | bytes 1622024 | tf_op jit(solution)/shard_map/ppermute | solution.py:32
  102.2 2.7 %collective-permute-done.31.k34 = bf16[208,1024]{1,0:T(8,128)(2,1)S(1)} collective-permute-done((bf16[208,1024]{1,0:T(8,128)(2,1)S(1)}, bf16[208,1024]{1,0:T(8,128)(2,1)S(1)}, u32[]{:S(2)}, u32[]{:S(2)}) %collective-permute-start.31) | collective-permute-done | bytes 426016 | tf_op jit(solution)/shard_map/ppermute | solution.py:32
  105.0 5.4 %collective-permute-start.32 = (bf16[144,1024]{1,0:T(8,128)(2,1)S(1)}, bf16[144,1024]{1,0:T(8,128)(2,1)S(1)}, u32[]{:S(2)}, u32[]{:S(2)}) collective-permute-start(bf16[144,1024]{1,0:T(8,128)(2,1)S(1)} %get-tuple-element.47), channel_id=1, source_target_pairs={{0,32},{1,33},{2,34},{3,35},{4,36},{5,37},{6,38},{7,39},{8,40},{9,... | collective-permute-start | bytes 884744 | tf_op jit(solution)/shard_map/ppermute | solution.py:32
  110.4 1.8 %collective-permute-start.33 = (bf16[144,1024]{1,0:T(8,128)(2,1)S(1)}, bf16[144,1024]{1,0:T(8,128)(2,1)S(1)}, u32[]{:S(2)}, u32[]{:S(2)}) collective-permute-start(bf16[144,1024]{1,0:T(8,128)(2,1)S(1)} %get-tuple-element.48), channel_id=1, source_target_pairs={{0,64},{1,65},{2,66},{3,67},{4,68},{5,69},{6,70},{7,71},{8,72},{9,... | collective-permute-start | bytes 884744 | tf_op jit(solution)/shard_map/ppermute | solution.py:32
  112.2 1.4 %collective-permute-done.36.p1 = bf16[528,512]{1,0:T(8,128)(2,1)S(1)} collective-permute-done((bf16[528,512]{1,0:T(8,128)(2,1)S(1)}, bf16[528,512]{1,0:T(8,128)(2,1)S(1)}, u32[]{:S(2)}, u32[]{:S(2)}) %collective-permute-start.36) | collective-permute-done | bytes 540704 | tf_op jit(solution)/shard_map/ppermute | solution.py:32
  114.2 1.9 %collective-permute-start.39 = (bf16[144,512]{1,0:T(8,128)(2,1)S(1)}, bf16[144,512]{1,0:T(8,128)(2,1)S(1)}, u32[]{:S(2)}, u32[]{:S(2)}) collective-permute-start(bf16[144,512]{1,0:T(8,128)(2,1)S(1)} %get-tuple-element.57), channel_id=1, source_target_pairs={{0,4},{1,5},{2,6},{3,7},{4,8},{5,9},{6,10},{7,11},{8,12},{9,13},{1... | collective-permute-start | bytes 442376 | tf_op jit(solution)/shard_map/ppermute | solution.py:32
  116.1 3.3 %collective-permute-done.38.w2 = bf16[144,512]{1,0:T(8,128)(2,1)S(1)} collective-permute-done((bf16[144,512]{1,0:T(8,128)(2,1)S(1)}, bf16[144,512]{1,0:T(8,128)(2,1)S(1)}, u32[]{:S(2)}, u32[]{:S(2)}) %collective-permute-start.38) | collective-permute-done | bytes 147488 | tf_op jit(solution)/shard_map/ppermute | solution.py:32
  119.4 2.2 %collective-permute-done.40.w3 = bf16[144,512]{1,0:T(8,128)(2,1)S(1)} collective-permute-done((bf16[144,512]{1,0:T(8,128)(2,1)S(1)}, bf16[144,512]{1,0:T(8,128)(2,1)S(1)}, u32[]{:S(2)}, u32[]{:S(2)}) %collective-permute-start.40) | collective-permute-done | bytes 147488 | tf_op jit(solution)/shard_map/ppermute | solution.py:32
  121.6 0.7 collective-permute-done.33.b2
  122.5 5.0 %collective-permute-start.41 = (bf16[80,1536]{1,0:T(8,128)(2,1)S(1)}, bf16[80,1536]{1,0:T(8,128)(2,1)S(1)}, u32[]{:S(2)}, u32[]{:S(2)}) collective-permute-start(bf16[80,1536]{1,0:T(8,128)(2,1)S(1)} %get-tuple-element.62), channel_id=1, source_target_pairs={{0,16},{1,17},{2,18},{3,19},{4,20},{5,21},{6,22},{7,23},{8,24},{9,... | collective-permute-start | bytes 737288 | tf_op jit(solution)/shard_map/ppermute | solution.py:32
  127.5 1.1 collective-permute-done.41.share
  128.7 0.8 shard_map.74
  (67 shorter events, 6.1 us)
Async XLA Ops:
  1.6 1.7 %collective-permute-start = (bf16[64,1024]{1,0:T(8,128)(2,1)S(1)}, bf16[64,1024]{1,0:T(8,128)(2,1)S(1)}, u32[]{:S(2)}, u32[]{:S(2)}) collective-permute-start(bf16[64,1024]{1,0:T(8,128)(2,1)S(1)} %get-tuple-element.78), channel_id=1, source_target_pairs={{0,16},{1,17},{2,18},{3,19},{4,20},{5,21},{6,22},{7,23},{8,24},{9,... | collective-permute-start | bytes 393224 | tf_op jit(solution)/shard_map/ppermute | solution.py:32
  2.4 5.5 %collective-permute-start.10 = (bf16[64,1024]{1,0:T(8,128)(2,1)}, bf16[64,1024]{1,0:T(8,128)(2,1)S(1)}, u32[]{:S(2)}, u32[]{:S(2)}) collective-permute-start(bf16[64,1024]{1,0:T(8,128)(2,1)} %param.5), channel_id=1, source_target_pairs={{0,16},{1,17},{2,18},{3,19},{4,20},{5,21},{6,22},{7,23},{8,24},{9,... | collective-permute-start | bytes 393224 | tf_op jit(solution)/shard_map/ppermute | solution.py:32
  2.5 5.4 %collective-permute-start.11 = (bf16[64,1024]{1,0:T(8,128)(2,1)}, bf16[64,1024]{1,0:T(8,128)(2,1)S(1)}, u32[]{:S(2)}, u32[]{:S(2)}) collective-permute-start(bf16[64,1024]{1,0:T(8,128)(2,1)} %param.7), channel_id=1, source_target_pairs={{0,16},{1,17},{2,18},{3,19},{4,20},{5,21},{6,22},{7,23},{8,24},{9,... | collective-permute-start | bytes 393224 | tf_op jit(solution)/shard_map/ppermute | solution.py:32
  3.4 7.1 %collective-permute-start.2 = (bf16[2,64,1024]{2,1,0:T(8,128)(2,1)S(1)}, bf16[2,64,1024]{2,1,0:T(8,128)(2,1)S(1)}, u32[]{:S(2)}, u32[]{:S(2)}) collective-permute-start(bf16[2,64,1024]{2,1,0:T(8,128)(2,1)S(1)} %get-tuple-element.76), channel_id=1, source_target_pairs={{0,2},{1,3},{2,0},{3,1},{4,6},{5,7},{6,4},{7,5},{8,10},{9,11},{10,... | collective-permute-start | bytes 786440 | tf_op jit(solution)/shard_map/ppermute | solution.py:32
  6.4 7.3 %collective-permute-start.1 = (bf16[2,64,1024]{2,1,0:T(8,128)(2,1)S(1)}, bf16[2,64,1024]{2,1,0:T(8,128)(2,1)S(1)}, u32[]{:S(2)}, u32[]{:S(2)}) collective-permute-start(bf16[2,64,1024]{2,1,0:T(8,128)(2,1)S(1)} %get-tuple-element.76), channel_id=1, source_target_pairs={{0,3},{1,0},{2,1},{3,2},{4,7},{5,4},{6,5},{7,6},{8,11},{9,8},{10,9... | collective-permute-start | bytes 786440 | tf_op jit(solution)/shard_map/ppermute | solution.py:32
  7.2 6.7 %collective-permute-start.3 = (bf16[2,64,1024]{2,1,0:T(8,128)(2,1)S(1)}, bf16[2,64,1024]{2,1,0:T(8,128)(2,1)S(1)}, u32[]{:S(2)}, u32[]{:S(2)}) collective-permute-start(bf16[2,64,1024]{2,1,0:T(8,128)(2,1)S(1)} %get-tuple-element.76), channel_id=1, source_target_pairs={{0,1},{1,2},{2,3},{3,0},{4,5},{5,6},{6,7},{7,4},{8,9},{9,10},{10,1... | collective-permute-start | bytes 786440 | tf_op jit(solution)/shard_map/ppermute | solution.py:32
  8.9 8.6 %collective-permute-start.12 = (bf16[2,2,64,1024]{3,2,1,0:T(8,128)(2,1)S(1)}, bf16[2,2,64,1024]{3,2,1,0:T(8,128)(2,1)S(1)}, u32[]{:S(2)}, u32[]{:S(2)}) collective-permute-start(bf16[2,2,64,1024]{3,2,1,0:T(8,128)(2,1)S(1)} %bitcast.28), channel_id=1, source_target_pairs={{0,32},{1,33},{2,34},{3,35},{4,36},{5,37},{6,38},{7,39},{8,40},{9,... | collective-permute-start | bytes 1572872 | tf_op jit(solution)/shard_map/ppermute | solution.py:32
  14.1 15.8 %collective-permute-start.5 = (bf16[2,4,64,1024]{3,2,1,0:T(8,128)(2,1)S(1)}, bf16[2,4,64,1024]{3,2,1,0:T(8,128)(2,1)S(1)}, u32[]{:S(2)}, u32[]{:S(2)}) collective-permute-start(bf16[2,4,64,1024]{3,2,1,0:T(8,128)(2,1)S(1)} %pad_maximum_fusion.1.line), channel_id=1, source_target_pairs={{0,12},{1,13},{2,14},{3,15},{4,0},{5,1},{6,2},{7,3},{8,4},{9,5},{1... | collective-permute-start | bytes 3145736 | tf_op jit(solution)/shard_map/ppermute | solution.py:32
  14.5 16.1 %collective-permute-start.4 = (bf16[2,4,64,1024]{3,2,1,0:T(8,128)(2,1)S(1)}, bf16[2,4,64,1024]{3,2,1,0:T(8,128)(2,1)S(1)}, u32[]{:S(2)}, u32[]{:S(2)}) collective-permute-start(bf16[2,4,64,1024]{3,2,1,0:T(8,128)(2,1)S(1)} %pad_maximum_fusion.1.line), channel_id=1, source_target_pairs={{0,4},{1,5},{2,6},{3,7},{4,8},{5,9},{6,10},{7,11},{8,12},{9,13},{1... | collective-permute-start | bytes 3145736 | tf_op jit(solution)/shard_map/ppermute | solution.py:32
  17.5 9.2 %collective-permute-start.13 = (bf16[2,2,64,1024]{3,2,1,0:T(8,128)(2,1)S(1)}, bf16[2,2,64,1024]{3,2,1,0:T(8,128)(2,1)S(1)}, u32[]{:S(2)}, u32[]{:S(2)}) collective-permute-start(bf16[2,2,64,1024]{3,2,1,0:T(8,128)(2,1)S(1)} %collective-permute-done.12.t1), channel_id=1, source_target_pairs={{0,32},{1,33},{2,34},{3,35},{4,36},{5,37},{6,38},{7,39},{8,40},{9,... | collective-permute-start | bytes 1572872 | tf_op jit(solution)/shard_map/ppermute | solution.py:32
  26.7 9.2 %collective-permute-start.14 = (bf16[2,2,64,1024]{3,2,1,0:T(8,128)(2,1)S(1)}, bf16[2,2,64,1024]{3,2,1,0:T(8,128)(2,1)S(1)}, u32[]{:S(2)}, u32[]{:S(2)}) collective-permute-start(bf16[2,2,64,1024]{3,2,1,0:T(8,128)(2,1)S(1)} %collective-permute-done.13.t2), channel_id=1, source_target_pairs={{0,32},{1,33},{2,34},{3,35},{4,36},{5,37},{6,38},{7,39},{8,40},{9,... | collective-permute-start | bytes 1572872 | tf_op jit(solution)/shard_map/ppermute | solution.py:32
  29.9 9.6 %collective-permute-start.7 = (bf16[2,2,64,1024]{3,2,1,0:T(8,128)(2,1)S(1)}, bf16[2,2,64,1024]{3,2,1,0:T(8,128)(2,1)S(1)}, u32[]{:S(2)}, u32[]{:S(2)}) collective-permute-start(bf16[2,2,64,1024]{3,2,1,0:T(8,128)(2,1)S(1)} %slice.213), channel_id=1, source_target_pairs={{0,12},{1,13},{2,14},{3,15},{4,0},{5,1},{6,2},{7,3},{8,4},{9,5},{1... | collective-permute-start | bytes 1572872 | tf_op jit(solution)/shard_map/ppermute | solution.py:32
  30.8 18.4 %collective-permute-start.8 = (bf16[3,4,64,1024]{3,2,1,0:T(8,128)(2,1)S(1)}, bf16[3,4,64,1024]{3,2,1,0:T(8,128)(2,1)S(1)}, u32[]{:S(2)}, u32[]{:S(2)}) collective-permute-start(bf16[3,4,64,1024]{3,2,1,0:T(8,128)(2,1)S(1)} %pad_maximum_fusion), channel_id=1, source_target_pairs={{0,16},{1,17},{2,18},{3,19},{4,20},{5,21},{6,22},{7,23},{8,24},{9,... | collective-permute-start | bytes 4718600 | tf_op jit(solution)/shard_map/ppermute | solution.py:32
  34.3 8.4 %collective-permute-start.6 = (bf16[2,2,64,1024]{3,2,1,0:T(8,128)(2,1)S(1)}, bf16[2,2,64,1024]{3,2,1,0:T(8,128)(2,1)S(1)}, u32[]{:S(2)}, u32[]{:S(2)}) collective-permute-start(bf16[2,2,64,1024]{3,2,1,0:T(8,128)(2,1)S(1)} %slice.212), channel_id=1, source_target_pairs={{0,4},{1,5},{2,6},{3,7},{4,8},{5,9},{6,10},{7,11},{8,12},{9,13},{1... | collective-permute-start | bytes 1572872 | tf_op jit(solution)/shard_map/ppermute | solution.py:32
  35.7 13.4 %collective-permute-start.16 = (bf16[2,2,2,64,1024]{4,3,2,1,0:T(8,128)(2,1)S(1)}, bf16[2,2,2,64,1024]{4,3,2,1,0:T(8,128)(2,1)S(1)}, u32[]{:S(2)}, u32[]{:S(2)}) collective-permute-start(bf16[2,2,2,64,1024]{4,3,2,1,0:T(8,128)(2,1)S(1)} %pad_maximum_fusion.2), channel_id=1, source_target_pairs={{0,16},{1,17},{2,18},{3,19},{4,20},{5,21},{6,22},{7,23},{8,24},{9,... | collective-permute-start | bytes 3145736 | tf_op jit(solution)/shard_map/ppermute | solution.py:32
  35.9 9.0 %collective-permute-start.15 = (bf16[2,64,1024]{2,1,0:T(8,128)(2,1)S(1)}, bf16[2,64,1024]{2,1,0:T(8,128)(2,1)S(1)}, u32[]{:S(2)}, u32[]{:S(2)}) collective-permute-start(bf16[2,64,1024]{2,1,0:T(8,128)(2,1)S(1)} %slice_bitcast_fusion), channel_id=1, source_target_pairs={{0,32},{1,33},{2,34},{3,35},{4,36},{5,37},{6,38},{7,39},{8,40},{9,... | collective-permute-start | bytes 786440 | tf_op jit(solution)/shard_map/ppermute | solution.py:32
  39.5 9.7 %collective-permute-start.17 = (bf16[2,2,64,1024]{3,2,1,0:T(8,128)(2,1)S(1)}, bf16[2,2,64,1024]{3,2,1,0:T(8,128)(2,1)S(1)}, u32[]{:S(2)}, u32[]{:S(2)}) collective-permute-start(bf16[2,2,64,1024]{3,2,1,0:T(8,128)(2,1)S(1)} %collective-permute-done.14.t3), channel_id=1, source_target_pairs={{0,16},{1,17},{2,18},{3,19},{4,20},{5,21},{6,22},{7,23},{8,24},{9,... | collective-permute-start | bytes 1572872 | tf_op jit(solution)/shard_map/ppermute | solution.py:32
  42.8 6.4 %collective-permute-start.9 = (bf16[4,64,1024]{2,1,0:T(8,128)(2,1)S(1)}, bf16[4,64,1024]{2,1,0:T(8,128)(2,1)S(1)}, u32[]{:S(2)}, u32[]{:S(2)}) collective-permute-start(bf16[4,64,1024]{2,1,0:T(8,128)(2,1)S(1)} %pad_maximum_fusion.3), channel_id=1, source_target_pairs={{0,16},{1,17},{2,18},{3,19},{4,20},{5,21},{6,22},{7,23},{8,24},{9,... | collective-permute-start | bytes 1572872 | tf_op jit(solution)/shard_map/ppermute | solution.py:32
  45.0 4.2 %collective-permute-start.18 = (bf16[2,64,1024]{2,1,0:T(8,128)(2,1)S(1)}, bf16[2,64,1024]{2,1,0:T(8,128)(2,1)S(1)}, u32[]{:S(2)}, u32[]{:S(2)}) collective-permute-start(bf16[2,64,1024]{2,1,0:T(8,128)(2,1)S(1)} %collective-permute-done.15.far), channel_id=1, source_target_pairs={{0,16},{1,17},{2,18},{3,19},{4,20},{5,21},{6,22},{7,23},{8,24},{9,... | collective-permute-start | bytes 786440 | tf_op jit(solution)/shard_map/ppermute | solution.py:32
  59.3 5.8 %collective-permute-start.27 = (f32[8,1024]{1,0:T(8,128)S(1)}, f32[8,1024]{1,0:T(8,128)S(1)}, u32[]{:S(2)}, u32[]{:S(2)}) collective-permute-start(f32[8,1024]{1,0:T(8,128)S(1)} %get-tuple-element.38), channel_id=1, source_target_pairs={{0,96},{1,97},{2,98},{3,99},{4,100},{5,101},{6,102},{7,103},{8,104... | collective-permute-start | bytes 98312 | tf_op jit(solution)/shard_map/ppermute | solution.py:32
  59.8 7.9 %collective-permute-start.26 = (f32[8,1024]{1,0:T(8,128)S(1)}, f32[8,1024]{1,0:T(8,128)S(1)}, u32[]{:S(2)}, u32[]{:S(2)}) collective-permute-start(f32[8,1024]{1,0:T(8,128)S(1)} %get-tuple-element.38), channel_id=1, source_target_pairs={{0,64},{1,65},{2,66},{3,67},{4,68},{5,69},{6,70},{7,71},{8,72},{9,... | collective-permute-start | bytes 98312 | tf_op jit(solution)/shard_map/ppermute | solution.py:32
  64.4 3.3 %collective-permute-start.25 = (f32[8,1024]{1,0:T(8,128)S(1)}, f32[8,1024]{1,0:T(8,128)S(1)}, u32[]{:S(2)}, u32[]{:S(2)}) collective-permute-start(f32[8,1024]{1,0:T(8,128)S(1)} %get-tuple-element.38), channel_id=1, source_target_pairs={{0,32},{1,33},{2,34},{3,35},{4,36},{5,37},{6,38},{7,39},{8,40},{9,... | collective-permute-start | bytes 98312 | tf_op jit(solution)/shard_map/ppermute | solution.py:32
  64.4 7.8 %collective-permute-start.21 = (f32[8,1024]{1,0:T(8,128)S(1)}, f32[8,1024]{1,0:T(8,128)S(1)}, u32[]{:S(2)}, u32[]{:S(2)}) collective-permute-start(f32[8,1024]{1,0:T(8,128)S(1)} %get-tuple-element.37), channel_id=1, source_target_pairs={{0,3},{1,2},{2,1},{3,0},{4,7},{5,6},{6,5},{7,4},{8,11},{9,10},{10,... | collective-permute-start | bytes 98312 | tf_op jit(solution)/shard_map/ppermute | solution.py:32
  65.0 7.2 %collective-permute-start.20 = (f32[8,1024]{1,0:T(8,128)S(1)}, f32[8,1024]{1,0:T(8,128)S(1)}, u32[]{:S(2)}, u32[]{:S(2)}) collective-permute-start(f32[8,1024]{1,0:T(8,128)S(1)} %get-tuple-element.37), channel_id=1, source_target_pairs={{0,2},{1,3},{2,0},{3,1},{4,6},{5,7},{6,4},{7,5},{8,10},{9,11},{10,... | collective-permute-start | bytes 98312 | tf_op jit(solution)/shard_map/ppermute | solution.py:32
  65.1 7.2 %collective-permute-start.19 = (f32[8,1024]{1,0:T(8,128)S(1)}, f32[8,1024]{1,0:T(8,128)S(1)}, u32[]{:S(2)}, u32[]{:S(2)}) collective-permute-start(f32[8,1024]{1,0:T(8,128)S(1)} %get-tuple-element.37), channel_id=1, source_target_pairs={{0,1},{1,0},{2,3},{3,2},{4,5},{5,4},{6,7},{7,6},{8,9},{9,8},{10,11... | collective-permute-start | bytes 98312 | tf_op jit(solution)/shard_map/ppermute | solution.py:32
  67.9 8.1 %collective-permute-start.28 = (f32[5,1024]{1,0:T(8,128)S(1)}, f32[5,1024]{1,0:T(8,128)S(1)}, u32[]{:S(2)}, u32[]{:S(2)}) collective-permute-start(f32[5,1024]{1,0:T(8,128)S(1)} %concatenate.14), channel_id=1, source_target_pairs={{0,128},{1,129},{2,130},{3,131},{4,132},{5,133},{6,134},{7,135},{8... | collective-permute-start | bytes 61448 | tf_op jit(solution)/shard_map/ppermute | solution.py:32
  72.4 6.6 %collective-permute-start.24 = (f32[5,1024]{1,0:T(8,128)S(1)}, f32[5,1024]{1,0:T(8,128)S(1)}, u32[]{:S(2)}, u32[]{:S(2)}) collective-permute-start(f32[5,1024]{1,0:T(8,128)S(1)} %concatenate.13.ra), channel_id=1, source_target_pairs={{0,12},{1,13},{2,14},{3,15},{4,8},{5,9},{6,10},{7,11},{8,4},{9,5},... | collective-permute-start | bytes 61448 | tf_op jit(solution)/shard_map/ppermute | solution.py:32
  75.2 4.3 %collective-permute-start.23 = (f32[5,1024]{1,0:T(8,128)S(1)}, f32[5,1024]{1,0:T(8,128)S(1)}, u32[]{:S(2)}, u32[]{:S(2)}) collective-permute-start(f32[5,1024]{1,0:T(8,128)S(1)} %concatenate.13.ra), channel_id=1, source_target_pairs={{0,8},{1,9},{2,10},{3,11},{4,12},{5,13},{6,14},{7,15},{8,0},{9,1},... | collective-permute-start | bytes 61448 | tf_op jit(solution)/shard_map/ppermute | solution.py:32
  75.6 3.9 %collective-permute-start.22 = (f32[5,1024]{1,0:T(8,128)S(1)}, f32[5,1024]{1,0:T(8,128)S(1)}, u32[]{:S(2)}, u32[]{:S(2)}) collective-permute-start(f32[5,1024]{1,0:T(8,128)S(1)} %concatenate.13.ra), channel_id=1, source_target_pairs={{0,4},{1,5},{2,6},{3,7},{4,0},{5,1},{6,2},{7,3},{8,12},{9,13},{10,... | collective-permute-start | bytes 61448 | tf_op jit(solution)/shard_map/ppermute | solution.py:32
  76.0 3.9 %collective-permute-start.29 = (f32[5,1024]{1,0:T(8,128)S(1)}, f32[5,1024]{1,0:T(8,128)S(1)}, u32[]{:S(2)}, u32[]{:S(2)}) collective-permute-start(f32[5,1024]{1,0:T(8,128)S(1)} %concatenate.15.ca), channel_id=1, source_target_pairs={{0,16},{1,17},{2,18},{3,19},{4,20},{5,21},{6,22},{7,23},{8,24},{9,... | collective-permute-start | bytes 61448 | tf_op jit(solution)/shard_map/ppermute | solution.py:32
  90.5 5.5 %collective-permute-start.30 = (bf16[17,64,512]{2,1,0:T(8,128)(2,1)S(1)}, bf16[17,64,512]{2,1,0:T(8,128)(2,1)S(1)}, u32[]{:S(2)}, u32[]{:S(2)}) collective-permute-start(bf16[17,64,512]{2,1,0:T(8,128)(2,1)S(1)} %get-tuple-element.40), channel_id=1, source_target_pairs={{0,16},{1,17},{2,18},{3,19},{4,20},{5,21},{6,22},{7,23},{8,24},{9,... | collective-permute-start | bytes 3342344 | tf_op jit(solution)/shard_map/ppermute | solution.py:32
  93.6 3.9 %collective-permute-start.34 = (bf16[16,64,512]{2,1,0:T(8,128)(2,1)S(1)}, bf16[16,64,512]{2,1,0:T(8,128)(2,1)S(1)}, u32[]{:S(2)}, u32[]{:S(2)}) collective-permute-start(bf16[16,64,512]{2,1,0:T(8,128)(2,1)S(1)} %get-tuple-element.50), channel_id=1, source_target_pairs={{0,16},{1,17},{2,18},{3,19},{4,20},{5,21},{6,22},{7,23},{8,24},{9,... | collective-permute-start | bytes 3145736 | tf_op jit(solution)/shard_map/ppermute | solution.py:32
  96.2 8.7 %collective-permute-start.31 = (bf16[208,1024]{1,0:T(8,128)(2,1)S(1)}, bf16[208,1024]{1,0:T(8,128)(2,1)S(1)}, u32[]{:S(2)}, u32[]{:S(2)}) collective-permute-start(bf16[208,1024]{1,0:T(8,128)(2,1)S(1)} %get-tuple-element.45), channel_id=1, source_target_pairs={{0,64},{1,65},{2,66},{3,67},{4,68},{5,69},{6,70},{7,71},{8,72},{9,... | collective-permute-start | bytes 1277960 | tf_op jit(solution)/shard_map/ppermute | solution.py:32
  97.6 14.5 %collective-permute-start.35 = (bf16[528,512]{1,0:T(8,128)(2,1)S(1)}, bf16[528,512]{1,0:T(8,128)(2,1)S(1)}, u32[]{:S(2)}, u32[]{:S(2)}) collective-permute-start(bf16[528,512]{1,0:T(8,128)(2,1)S(1)} %get-tuple-element.52), channel_id=1, source_target_pairs={{0,2},{1,3},{2,0},{3,1},{4,6},{5,7},{6,4},{7,5},{8,10},{9,11},{10,... | collective-permute-start | bytes 1622024 | tf_op jit(solution)/shard_map/ppermute | solution.py:32
  99.5 14.1 %collective-permute-start.36 = (bf16[528,512]{1,0:T(8,128)(2,1)S(1)}, bf16[528,512]{1,0:T(8,128)(2,1)S(1)}, u32[]{:S(2)}, u32[]{:S(2)}) collective-permute-start(bf16[528,512]{1,0:T(8,128)(2,1)S(1)} %get-tuple-element.53), channel_id=1, source_target_pairs={{0,1},{1,2},{2,3},{3,0},{4,5},{5,6},{6,7},{7,4},{8,9},{9,10},{10,1... | collective-permute-start | bytes 1622024 | tf_op jit(solution)/shard_map/ppermute | solution.py:32
  99.5 14.1 %collective-permute-start.37 = (bf16[528,512]{1,0:T(8,128)(2,1)S(1)}, bf16[528,512]{1,0:T(8,128)(2,1)S(1)}, u32[]{:S(2)}, u32[]{:S(2)}) collective-permute-start(bf16[528,512]{1,0:T(8,128)(2,1)S(1)} %get-tuple-element.54), channel_id=1, source_target_pairs={{0,3},{1,0},{2,1},{3,2},{4,7},{5,4},{6,5},{7,6},{8,11},{9,8},{10,9... | collective-permute-start | bytes 1622024 | tf_op jit(solution)/shard_map/ppermute | solution.py:32
  105.0 16.6 %collective-permute-start.32 = (bf16[144,1024]{1,0:T(8,128)(2,1)S(1)}, bf16[144,1024]{1,0:T(8,128)(2,1)S(1)}, u32[]{:S(2)}, u32[]{:S(2)}) collective-permute-start(bf16[144,1024]{1,0:T(8,128)(2,1)S(1)} %get-tuple-element.47), channel_id=1, source_target_pairs={{0,32},{1,33},{2,34},{3,35},{4,36},{5,37},{6,38},{7,39},{8,40},{9,... | collective-permute-start | bytes 884744 | tf_op jit(solution)/shard_map/ppermute | solution.py:32
  110.4 11.9 %collective-permute-start.33 = (bf16[144,1024]{1,0:T(8,128)(2,1)S(1)}, bf16[144,1024]{1,0:T(8,128)(2,1)S(1)}, u32[]{:S(2)}, u32[]{:S(2)}) collective-permute-start(bf16[144,1024]{1,0:T(8,128)(2,1)S(1)} %get-tuple-element.48), channel_id=1, source_target_pairs={{0,64},{1,65},{2,66},{3,67},{4,68},{5,69},{6,70},{7,71},{8,72},{9,... | collective-permute-start | bytes 884744 | tf_op jit(solution)/shard_map/ppermute | solution.py:32
  113.8 5.6 %collective-permute-start.38 = (bf16[144,512]{1,0:T(8,128)(2,1)S(1)}, bf16[144,512]{1,0:T(8,128)(2,1)S(1)}, u32[]{:S(2)}, u32[]{:S(2)}) collective-permute-start(bf16[144,512]{1,0:T(8,128)(2,1)S(1)} %get-tuple-element.56), channel_id=1, source_target_pairs={{0,8},{1,9},{2,10},{3,11},{4,12},{5,13},{6,14},{7,15},{8,0},{9,1},... | collective-permute-start | bytes 442376 | tf_op jit(solution)/shard_map/ppermute | solution.py:32
  114.2 5.2 %collective-permute-start.39 = (bf16[144,512]{1,0:T(8,128)(2,1)S(1)}, bf16[144,512]{1,0:T(8,128)(2,1)S(1)}, u32[]{:S(2)}, u32[]{:S(2)}) collective-permute-start(bf16[144,512]{1,0:T(8,128)(2,1)S(1)} %get-tuple-element.57), channel_id=1, source_target_pairs={{0,4},{1,5},{2,6},{3,7},{4,8},{5,9},{6,10},{7,11},{8,12},{9,13},{1... | collective-permute-start | bytes 442376 | tf_op jit(solution)/shard_map/ppermute | solution.py:32
  116.1 5.5 %collective-permute-start.40 = (bf16[144,512]{1,0:T(8,128)(2,1)S(1)}, bf16[144,512]{1,0:T(8,128)(2,1)S(1)}, u32[]{:S(2)}, u32[]{:S(2)}) collective-permute-start(bf16[144,512]{1,0:T(8,128)(2,1)S(1)} %get-tuple-element.58), channel_id=1, source_target_pairs={{0,12},{1,13},{2,14},{3,15},{4,0},{5,1},{6,2},{7,3},{8,4},{9,5},{1... | collective-permute-start | bytes 442376 | tf_op jit(solution)/shard_map/ppermute | solution.py:32
  122.5 6.2 %collective-permute-start.41 = (bf16[80,1536]{1,0:T(8,128)(2,1)S(1)}, bf16[80,1536]{1,0:T(8,128)(2,1)S(1)}, u32[]{:S(2)}, u32[]{:S(2)}) collective-permute-start(bf16[80,1536]{1,0:T(8,128)(2,1)S(1)} %get-tuple-element.62), channel_id=1, source_target_pairs={{0,16},{1,17},{2,18},{3,19},{4,20},{5,21},{6,22},{7,23},{8,24},{9,... | collective-permute-start | bytes 737288 | tf_op jit(solution)/shard_map/ppermute | solution.py:32
